TPU v7x, 32 devices: a whole 2x2x4 slice. The times are simulated.
32 devices in a mesh: dp: 4 (over z), seq: 8 (over y, x, core).
Axes of the slice: x: 2, y: 2, z: 4, core: 2. Of those that a mesh axis runs over, the one named last changes fastest.
Arguments:
- latents: bfloat16 [8, 4096, 1152], P('dp', 'seq'), may hold values from -56 to 56
- out_grad: bfloat16 [8, 4096, 1152], P('dp', 'seq'), may hold values from -6 to 6
- phrases: bfloat16 [8, 32, 1152], P('dp'), may hold values from -6 to 6
- query_weight: bfloat16 [1152, 1152], replicated, may hold values from -0.1875 to 0.1875
- key_weight: bfloat16 [1152, 1152], P('seq'), may hold values from -0.1875 to 0.1875
- value_weight: bfloat16 [1152, 1152], P('seq'), may hold values from -0.1875 to 0.1875
- first_weight: bfloat16 [1152, 1152], P('seq'), may hold values from -0.1875 to 0.1875
- second_weight: bfloat16 [1152, 1152], P('seq'), may hold values from -0.1875 to 0.1875
- region_first: int32 [8, 32], P('dp'), may hold values from 0 to 31, as said below
- region_last: int32 [8, 32], P('dp'), may hold values from 0 to 31
- phrase_counts: int32 [8], P('dp'), may hold values from 8 to 32, as said below
Outputs:
- latent_grad: bfloat16 [8, 4096, 1152], P('dp', 'seq')
- phrase_grad: bfloat16 [8, 32, 1152], P('dp')
- first_grad: float32 [1152, 1152], P('seq')
- second_grad: float32 [1152, 1152], P('seq')
Inputs may be any that keep to these rules, and one draw needn't show every extreme that they name: region_first <= region_last for every phrase; phrase 0 of every image covers all 32 blocks. Slots from phrase_counts on are padding.
All inputs are finite; a program needn't handle non-finite values.
Results may differ from a plain program's by a relative error of at most 0.015.
The roundings to bfloat16 on the way count: a program that leaves them out, or rounds other values in their place, can miss the bound.
Values may be sent and summed in bfloat16 or wider, within the bound.
No kernel may reach another device: no remote copies, remote signals or barrier semaphores. Data moves between devices by JAX's collectives and lax.ppermute only.
A program may use at most 128 MiB of HBM per device.

v0:
```python
import jax
import jax.numpy as jnp
from jax import lax
from jax.sharding import PartitionSpec as P

H = 16


def silu_slope(pre_act):
    sigmoid = jax.nn.sigmoid(pre_act)
    return sigmoid * (1.0 + pre_act * (1.0 - sigmoid))


def times_transposed(left_arg, right_arg):
    return lax.dot_general(
        left_arg, right_arg, (((1,), (1,)), ((), ())), preferred_element_type=jnp.float32
    )


def transposed_times(left_arg, right_arg):
    return lax.dot_general(
        left_arg, right_arg, (((0,), (0,)), ((), ())), preferred_element_type=jnp.float32
    )


def attention_grads(
    latents,
    out_grad,
    query_weight,
    key_rows,
    value_rows,
    region_first,
    region_last,
    phrase_counts,
    offset,
):
    images, tokens, features = latents.shape
    slot_count = key_rows.shape[1]
    head_count = H
    head_size = features // head_count
    score_scale = head_size ** (-0.5)
    queries = jnp.dot(
        latents.reshape(images * tokens, features), query_weight, preferred_element_type=jnp.float32
    ).astype(jnp.bfloat16)
    query_heads = queries.reshape(images, tokens, head_count, head_size)
    key_heads = key_rows.reshape(images, slot_count, head_count, head_size)
    value_heads = value_rows.reshape(images, slot_count, head_count, head_size)
    grad_heads = out_grad.reshape(images, tokens, head_count, head_size)
    scores = (
        jnp.einsum("ithd,iphd->ithp", query_heads, key_heads, preferred_element_type=jnp.float32)
        * score_scale
    )
    block_ids = (offset + jnp.arange(tokens, dtype=jnp.int32)) // (tokens // 4)
    phrase_ids = jnp.arange(slot_count, dtype=jnp.int32)
    visible = (
        (phrase_ids[None, None, :] < phrase_counts[:, None, None])
        & (region_first[:, None, :] <= block_ids[None, :, None])
        & (block_ids[None, :, None] <= region_last[:, None, :])
    )
    scores = jnp.where(visible[:, :, None, :], scores, -jnp.inf)
    row_max = jnp.max(scores, axis=-1, keepdims=True)
    exponent = jnp.exp(scores - row_max)
    attn_probs = exponent / jnp.sum(exponent, axis=-1, keepdims=True)
    probs_low = attn_probs.astype(jnp.bfloat16)
    prob_grad = jnp.einsum(
        "ithd,iphd->ithp", grad_heads, value_heads, preferred_element_type=jnp.float32
    )
    inner_sum = jnp.sum(attn_probs * prob_grad, axis=-1, keepdims=True)
    score_grad = (attn_probs * (prob_grad - inner_sum) * score_scale).astype(jnp.bfloat16)
    query_grad = jnp.einsum(
        "ithp,iphd->ithd", score_grad, key_heads, preferred_element_type=jnp.float32
    ).astype(jnp.bfloat16)
    latent_grad = times_transposed(
        query_grad.reshape(images * tokens, features), query_weight
    ).astype(jnp.bfloat16)
    key_part = jnp.einsum(
        "ithp,ithd->iphd", score_grad, query_heads, preferred_element_type=jnp.float32
    ).reshape(images, slot_count, features)
    value_part = jnp.einsum(
        "ithp,ithd->iphd", probs_low, grad_heads, preferred_element_type=jnp.float32
    ).reshape(images, slot_count, features)
    return (latent_grad.reshape(images, tokens, features), key_part, value_part)


def local(
    latents,
    out_grad,
    phrases,
    query_weight,
    key_weight,
    value_weight,
    first_weight,
    second_weight,
    region_first,
    region_last,
    phrase_counts,
):
    images, tokens, features = latents.shape
    slot_count = phrases.shape[1]
    shard_rows = first_weight.shape[0]
    col_start = lax.axis_index("seq") * shard_rows
    phrase_rows = phrases.reshape(images * slot_count, features)

    def own_cols(matrix):
        return lax.dynamic_slice_in_dim(matrix, col_start, shard_rows, 1)

    full_first, full_second, full_key, full_value = (
        lax.all_gather(first_weight, "seq", axis=0, tiled=True),
        lax.all_gather(second_weight, "seq", axis=0, tiled=True),
        lax.all_gather(key_weight, "seq", axis=0, tiled=True),
        lax.all_gather(value_weight, "seq", axis=0, tiled=True),
    )
    pre_act = jnp.dot(phrase_rows, full_first, preferred_element_type=jnp.float32)
    hidden = jax.nn.silu(pre_act).astype(jnp.bfloat16)
    encoded = jnp.dot(hidden, full_second, preferred_element_type=jnp.float32).astype(jnp.bfloat16)
    key_rows = jnp.dot(encoded, full_key, preferred_element_type=jnp.float32).astype(jnp.bfloat16)
    value_rows = jnp.dot(encoded, full_value, preferred_element_type=jnp.float32).astype(
        jnp.bfloat16
    )
    offset = lax.axis_index("seq") * tokens
    latent_grad, key_part, value_part = attention_grads(
        latents,
        out_grad,
        query_weight,
        key_rows.reshape(images, slot_count, features),
        value_rows.reshape(images, slot_count, features),
        region_first,
        region_last,
        phrase_counts,
        offset,
    )
    key_sum_grad, value_sum_grad = lax.psum((key_part, value_part), "seq")
    key_grad = key_sum_grad.astype(jnp.bfloat16).reshape(images * slot_count, features)
    value_grad = value_sum_grad.astype(jnp.bfloat16).reshape(images * slot_count, features)
    encoded_grad = (
        times_transposed(key_grad, full_key) + times_transposed(value_grad, full_value)
    ).astype(jnp.bfloat16)
    second_grad = transposed_times(own_cols(hidden), encoded_grad)
    hidden_grad = times_transposed(encoded_grad, full_second)
    act_grad = (hidden_grad * silu_slope(pre_act)).astype(jnp.bfloat16)
    first_grad = transposed_times(own_cols(phrase_rows), act_grad)
    phrase_grad = times_transposed(act_grad, full_first).astype(jnp.bfloat16)
    first_grad, second_grad = lax.psum((first_grad, second_grad), "dp")
    return (latent_grad, phrase_grad.reshape(images, slot_count, features), first_grad, second_grad)


def solution(mesh):
    in_specs = (
        P("dp", "seq", None),
        P("dp", "seq", None),
        P("dp", None, None),
        P(),
        P("seq", None),
        P("seq", None),
        P("seq", None),
        P("seq", None),
        P("dp", None),
        P("dp", None),
        P("dp"),
    )
    out_specs = (P("dp", "seq", None), P("dp", None, None), P("seq", None), P("seq", None))
    return jax.shard_map(local, mesh=mesh, in_specs=in_specs, out_specs=out_specs, check_vma=False)
```

profile of v0, /device:TPU:0, one launch (start us, length us, event | category | flops | bytes accessed | tf_op | source)
XLA Modules:
  0.0 273.2 jit_solution(5257163551367615106)
XLA Ops:
  10.0 6.6 %convolution_convert_fusion.1 = bf16[1024,1152]{1,0:T(8,128)(2,1)} fusion(bf16[1024,1152]{1,0:T(8,128)(2,1)} %bitcast.83, bf16[1152,1152]{1,0:T(8,128)(2,1)S(1)} %copy-done), kind=kOutput, calls=%fused_computation.3 | convolution fusion | flops 2719088640 | bytes 7372800 | tf_op jit(solution)/shard_map/dot_general | solution.py:42
  16.6 9.6 %reshape.101 = bf16[2,512,16,72]{3,2,1,0:T(8,128)(2,1)} reshape(bf16[1024,1152]{1,0:T(8,128)(2,1)} %convolution_convert_fusion.1) | data formatting | bytes 4718592 | tf_op jit(solution)/shard_map/reshape | solution.py:45
  26.2 7.2 %copy.24 = bf16[2,512,16,72]{1,3,2,0:T(8,128)(2,1)} copy(bf16[2,512,16,72]{3,2,1,0:T(8,128)(2,1)} %reshape.101) | data formatting | bytes 4718592 | tf_op jit(solution)/shard_map/reshape | solution.py:45
  33.4 4.3 %copy.25 = bf16[2,512,1152]{1,2,0:T(8,128)(2,1)} copy(bf16[2,512,1152]{2,1,0:T(8,128)(2,1)} %param.12) | data formatting | bytes 4718592 | tf_op args[1]
  38.0 4.9 %all-gather.5.cloned.1.call-done = bf16[1152,1152]{1,0:T(8,128)(2,1)} async-done(((bf16[144,1152]{1,0:T(8,128)(2,1)}), bf16[1152,1152]{1,0:T(8,128)(2,1)}) %all-gather.5.cloned.1.call-update) | async-done | bytes 2654224 | tf_op jit(solution)/shard_map/all_gather | solution.py:108
  42.9 3.1 %multiply_convert_fusion = (bf16[64,1152]{1,0:T(8,128)(2,1)S(1)}, f32[64,1152]{1,0:T(8,128)}) fusion(bf16[64,1152]{1,0:T(8,128)(2,1)S(1)} %bitcast.79, bf16[1152,1152]{1,0:T(8,128)(2,1)} %all-gather.5.cloned.1.call-done), kind=kOutput, calls=%fused_computation.29 | convolution fusion | flops 170237952 | bytes 3244032 | tf_op jit(solution)/shard_map/dot_general | solution.py:113
  46.0 29.1 %all-gather.7.cloned.1.call-done = bf16[1152,1152]{1,0:T(8,128)(2,1)} async-done(((bf16[144,1152]{1,0:T(8,128)(2,1)}), bf16[1152,1152]{1,0:T(8,128)(2,1)}) %all-gather.7.cloned.1.call-update) | async-done | bytes 2654224 | tf_op jit(solution)/shard_map/all_gather | solution.py:109
  75.0 2.3 convolution_convert_fusion.5
  77.4 29.8 %all-gather.9.cloned.1.call-done = bf16[1152,1152]{1,0:T(8,128)(2,1)} async-done(((bf16[144,1152]{1,0:T(8,128)(2,1)}), bf16[1152,1152]{1,0:T(8,128)(2,1)}) %all-gather.9.cloned.1.call-update) | async-done | bytes 2654224 | tf_op jit(solution)/shard_map/all_gather | solution.py:110
  107.2 2.3 convolution_convert_fusion.4
  110.0 29.2 %all-gather.11.cloned.1.call-done = bf16[1152,1152]{1,0:T(8,128)(2,1)} async-done(((bf16[144,1152]{1,0:T(8,128)(2,1)}), bf16[1152,1152]{1,0:T(8,128)(2,1)}) %all-gather.11.cloned.1.call-update) | async-done | bytes 2654224 | tf_op jit(solution)/shard_map/all_gather | solution.py:111
  139.2 2.3 convolution_convert_fusion.3
  142.0 3.5 %fusion.13 = f32[2,16,32,512]{3,2,1,0:T(8,128)} fusion(bf16[2,512,16,72]{1,3,2,0:T(8,128)(2,1)} %bitcast.74, bf16[2,32,16,72]{3,2,1,0:T(8,128)(2,1)S(1)} %reshape_reshape.7), kind=kOutput, calls=%fused_computation.31 | convolution fusion | flops 75497472 | bytes 4603904 | tf_op jit(solution)/shard_map/ithd,iphd->ithp/dot_general | solution.py:65
  145.6 3.9 %fusion.33 = (f32[2,512,16]{1,2,0:T(8,128)S(1)}, f32[2,512,16,32]{1,3,2,0:T(8,128)}) fusion(pred[2,512,32]{1,2,0:T(8,128)(4,1)S(1)} %compare_and_fusion, bf16[2,512,16,72]{1,3,2,0:T(8,128)(2,1)} %copy.24, bf16[2,32,16,72]{3,2,1,0:T(8,128)(2,1)S(1)} %reshape_reshape.6), kind=kOutput, calls=%fused_computation.59 | convolution fusion | flops 77594656 | bytes 4702208 | tf_op jit(solution)/shard_map/sub | solution.py:62
  149.5 3.8 %convolution_bitcast_fusion = f32[2,32,16,72]{3,1,2,0:T(8,128)} fusion(bf16[2,512,16,72]{1,3,2,0:T(8,128)(2,1)} %bitcast.75, f32[2,512,16,32]{1,3,2,0:T(8,128)} %get-tuple-element.11, f32[2,512,16]{1,2,0:T(8,128)S(1)} %get-tuple-element.10), kind=kOutput, calls=%fused_computation.21 | convolution fusion | flops 76546048 | bytes 4816896 | tf_op jit(solution)/shard_map/ithp,ithd->iphd/dot_general | solution.py:79
  153.3 5.8 %convolution_bitcast_fusion.1 = f32[2,32,16,72]{3,1,2,0:T(8,128)} fusion(bf16[2,512,16,72]{1,3,2,0:T(8,128)(2,1)} %copy.24, f32[2,16,32,512]{3,2,1,0:T(8,128)} %fusion.13, f32[2,512,16,32]{1,3,2,0:T(8,128)} %get-tuple-element.11, f32[2,512,16]{1,2,0:T(8,128)S(1)} %get-tuple-element.10), kind=kOutput, calls=%fused_computation.22 | convolution fusion | flops 79183904 | bytes 6914048 | tf_op jit(solution)/shard_map/ithp,ithd->iphd/dot_general | solution.py:76
  159.1 1.3 copy.30
  160.7 1.3 copy.31
  162.1 1.0 reshape.98
  163.0 30.4 %all-reduce.6 = (bf16[2,32,1152]{2,1,0:T(8,128)(2,1)S(1)}, bf16[2,32,1152]{2,1,0:T(8,128)(2,1)S(1)}) all-reduce(f32[2,32,1152]{2,1,0:T(8,128)S(1)} %reshape.96, f32[2,32,1152]{2,1,0:T(8,128)} %reshape.98), channel_id=1, replica_groups=mesh['dp'=4,'seq'=8] {'seq'}, use_global_device_ids=true, to_apply=%region_3.4 | all-reduce | flops 147456 | bytes 884736 | tf_op jit(solution)/shard_map/psum | solution.py:132
  193.5 2.8 %fusion.38 = f32[64,1152]{1,0:T(8,128)S(1)} fusion(bf16[64,1152]{1,0:T(8,128)(2,1)S(1)} %bitcast.82, bf16[1152,1152]{1,0:T(8,128)(2,1)} %all-gather.9.cloned.1.call-done), kind=kOutput, calls=%fused_computation.60 | convolution fusion | flops 169869312 | bytes 3096576 | tf_op jit(solution)/shard_map/dot_general | solution.py:15
  196.4 0.9 fusion.2
  197.3 2.0 fusion.18
  200.3 2.0 fusion.20
  202.3 5.8 %convert_bitcast_fusion = bf16[2,512,16,72]{1,3,2,0:T(8,128)(2,1)} fusion(f32[2,16,32,512]{3,2,1,0:T(8,128)} %fusion.13, bf16[2,32,16,72]{3,2,1,0:T(8,128)(2,1)S(1)} %copy-done.7, f32[2,512,16,32]{1,3,2,0:T(8,128)} %get-tuple-element.11, f32[2,512,16]{1,2,0:T(8,128)S(1)} %get-tuple-element.10), kind=kOutput, calls=%fused_computation.6 | convolution fusion | flops 80363552 | bytes 6766592 | tf_op jit(solution)/shard_map/ithp,iphd->ithd/dot_general | solution.py:70
  208.1 4.1 %copy.28 = bf16[2,512,16,72]{1,0,3,2:T(2,128)(2,1)S(1)} copy(bf16[2,512,16,72]{1,3,2,0:T(8,128)(2,1)} %convert_bitcast_fusion) | data formatting | bytes 4718592 | tf_op jit(solution)/shard_map/convert_element_type | solution.py:72
  212.8 1.1 copy-done.1
  214.0 1.6 convolution_convert_fusion.2
  215.6 4.8 %convolution_convert_fusion = bf16[1024,1152]{1,0:T(8,128)(2,1)} fusion(bf16[1024,1152]{0,1:T(8,128)(2,1)S(1)} %bitcast.77, bf16[1152,1152]{1,0:T(8,128)(2,1)S(1)} %copy-done), kind=kOutput, calls=%fused_computation.2 | convolution fusion | flops 2719088640 | bytes 7372800 | tf_op jit(solution)/shard_map/dot_general | solution.py:15
  220.4 42.4 %all-reduce.5.cloned.1.call-done = (f32[144,1152]{1,0:T(8,128)}, f32[144,1152]{1,0:T(8,128)}) async-done(((f32[144,1152]{1,0:T(8,128)}, f32[144,1152]{1,0:T(8,128)}), (f32[144,1152]{1,0:T(8,128)}, f32[144,1152]{1,0:T(8,128)})) %all-reduce.5.cloned.1.call-update) | async-done | bytes 1327120 | tf_op jit(solution)/shard_map/psum | solution.py:143
  262.8 2.0 copy.51
  264.7 2.0 copy.52
  (41 shorter events, 5.8 us)
Async XLA Ops:
  7.2 2.9 %copy-start = (bf16[1152,1152]{1,0:T(8,128)(2,1)S(1)}, bf16[1152,1152]{1,0:T(8,128)(2,1)}, u32[]{:S(2)}) copy-start(bf16[1152,1152]{1,0:T(8,128)(2,1)} %param.14) | copy-start | bytes 7962628
  7.2 35.7 %all-gather.5.cloned.1.call-start = ((), (), s32[]{:S(2)}) async-start(), calls=%async_computation | async-start | bytes 2985984 | tf_op jit(solution)/shard_map/all_gather | solution.py:108
  7.9 67.1 %all-gather.7.cloned.1.call-start = ((), (), s32[]{:S(2)}) async-start(), calls=%async_computation.1 | async-start | bytes 2985984 | tf_op jit(solution)/shard_map/all_gather | solution.py:109
  8.7 98.6 %all-gather.9.cloned.1.call-start = ((), (), s32[]{:S(2)}) async-start(), calls=%async_computation.2 | async-start | bytes 2985984 | tf_op jit(solution)/shard_map/all_gather | solution.py:110
  9.4 129.8 %all-gather.11.cloned.1.call-start = ((), (), s32[]{:S(2)}) async-start(), calls=%async_computation.3 | async-start | bytes 2985984 | tf_op jit(solution)/shard_map/all_gather | solution.py:111
  10.0 252.8 %all-reduce.5.cloned.1.call-start = ((), (), s32[]{:S(2)}) async-start(), calls=%async_computation.4 | async-start | bytes 2654208 | tf_op jit(solution)/shard_map/psum | solution.py:143
  33.4 4.4 %copy-start.11 = (s32[2]{0:T(128)S(1)}, s32[2]{0:T(128)}, u32[]{:S(2)}) copy-start(s32[2]{0:T(128)} %param.21) | copy-start | bytes 28
  33.4 4.4 %copy-start.9 = (s32[2,32]{1,0:T(2,128)S(1)}, s32[2,32]{1,0:T(2,128)}, u32[]{:S(2)}) copy-start(s32[2,32]{1,0:T(2,128)} %param.20) | copy-start | bytes 772
  33.4 4.4 %copy-start.10 = (s32[2,32]{1,0:T(2,128)S(1)}, s32[2,32]{1,0:T(2,128)}, u32[]{:S(2)}) copy-start(s32[2,32]{1,0:T(2,128)} %param.19) | copy-start | bytes 772
  33.4 9.5 %copy-start.8 = (bf16[2,32,1152]{2,1,0:T(8,128)(2,1)S(1)}, bf16[2,32,1152]{2,1,0:T(8,128)(2,1)}, u32[]{:S(2)}) copy-start(bf16[2,32,1152]{2,1,0:T(8,128)(2,1)} %param.13) | copy-start | bytes 442372
  46.0 63.6 %copy-start.4 = (bf16[64,1152]{1,0:T(8,128)(2,1)}, bf16[64,1152]{1,0:T(8,128)(2,1)S(1)}, u32[]{:S(2)}) copy-start(bf16[64,1152]{1,0:T(8,128)(2,1)S(1)} %get-tuple-element.8) | copy-start | bytes 442372
  110.0 35.6 %copy-start.6 = (bf16[2,32,16,72]{3,2,1,0:T(8,128)(2,1)}, bf16[2,32,16,72]{3,2,1,0:T(8,128)(2,1)S(1)}, u32[]{:S(2)}) copy-start(bf16[2,32,16,72]{3,2,1,0:T(8,128)(2,1)S(1)} %reshape_reshape.6) | copy-start | bytes 442372
  193.5 2.9 %copy-start.2 = (bf16[1152,1152]{1,0:T(8,128)(2,1)S(1)}, bf16[1152,1152]{1,0:T(8,128)(2,1)}, u32[]{:S(2)}) copy-start(bf16[1152,1152]{1,0:T(8,128)(2,1)} %all-gather.11.cloned.1.call-done) | copy-start | bytes 7962628
  196.3 3.0 %copy-start.3 = (bf16[1152,1152]{1,0:T(8,128)(2,1)S(1)}, bf16[1152,1152]{1,0:T(8,128)(2,1)}, u32[]{:S(2)}) copy-start(bf16[1152,1152]{1,0:T(8,128)(2,1)} %all-gather.7.cloned.1.call-done) | copy-start | bytes 7962628
  196.3 3.0 %copy-start.5 = (f32[64,1152]{1,0:T(8,128)S(1)}, f32[64,1152]{1,0:T(8,128)}, u32[]{:S(2)}) copy-start(f32[64,1152]{1,0:T(8,128)} %get-tuple-element.9) | copy-start | bytes 884740
  199.3 3.0 %copy-start.7 = (bf16[2,32,16,72]{3,2,1,0:T(8,128)(2,1)S(1)}, bf16[2,32,16,72]{3,2,1,0:T(8,128)(2,1)}, u32[]{:S(2)}) copy-start(bf16[2,32,16,72]{3,2,1,0:T(8,128)(2,1)} %copy-done.6) | copy-start | bytes 442372
  212.2 1.8 copy-start.1
Sparse Core Ops, SparseCore 0:
  9.9 32.9 all-gather.4
  44.8 30.2 all-gather.6
  76.9 30.2 all-gather.8
  109.0 30.2 all-gather.10
  202.4 60.3 all-reduce.4
where the time goes:
time: 274 us; the launch traced here: 273 us
  waiting for transfers between devices  138 us (50%)
  matrix products  54.6 us (20%)
  local copies, waits for them, and re-layouts  35.8 us (13%)
  blocking collectives  30.4 us (11%)
  between operations  13.9 us (5%)
    psum x1, waiting for transfers between devices, local(): first_grad, second_grad = lax.psum((first_grad, second_grad), 'dp')  42.4 us
    psum x1, blocking collectives, local(): key_sum_grad, value_sum_grad = lax.psum((key_part, value_part), 'seq')  30.4 us
    all_gather x1, waiting for transfers between devices, local(): lax.all_gather(key_weight, 'seq', axis=0, tiled=True)  29.8 us
    all_gather x1, waiting for transfers between devices, local(): lax.all_gather(value_weight, 'seq', axis=0, tiled=True)  29.2 us
    all_gather x1, waiting for transfers between devices, local(): lax.all_gather(second_weight, 'seq', axis=0, tiled=True)  29.1 us
    reshape x2, local copies, waits for them, and re-layouts, attention_grads(): query_heads = queries.reshape(images, tokens, head_count, head_size)  16.8 us
    dot_general x5, matrix products, times_transposed(): lax.dot_general(left_arg, right_arg, (((1,), (1,)), ((), ())), preferred_...  11.1 us
    unnamed x28, local copies, waits for them, and re-layouts  10.1 us
  transfers between devices with their start and end apart: 5, of which 5 were waited for; matrix products, arithmetic and copies ran while one was open for 19% of the time, Pallas kernels for 0%

commit v1 on v0

--- a/solution.py
+++ b/solution.py
@@ -1,9 +1,23 @@
+import functools
+
 import jax
 import jax.numpy as jnp
 from jax import lax
+from jax.experimental import pallas as pl
+from jax.experimental.pallas import tpu as pltpu
 from jax.sharding import PartitionSpec as P
 
 H = 16
+BLOCK = 128
+GROUP = 8
+VMEM = pl.BlockSpec(memory_space=pltpu.VMEM)
+SMEM = pl.BlockSpec(memory_space=pltpu.SMEM)
+ANY = pl.BlockSpec(memory_space=pl.ANY)
+HBM = pl.BlockSpec(memory_space=pltpu.HBM)
+
+
+def vmem(mebibytes):
+    return pltpu.CompilerParams(vmem_limit_bytes=mebibytes * 1024 * 1024)
 
 
 def silu_slope(pre_act):
@@ -11,16 +25,329 @@
     return sigmoid * (1.0 + pre_act * (1.0 - sigmoid))
 
 
+def contract(left_arg, right_arg, left_dim, right_dim):
+    return lax.dot_general(
+        left_arg,
+        right_arg,
+        (((left_dim,), (right_dim,)), ((), ())),
+        preferred_element_type=jnp.float32,
+    )
+
+
 def times_transposed(left_arg, right_arg):
-    return lax.dot_general(
-        left_arg, right_arg, (((1,), (1,)), ((), ())), preferred_element_type=jnp.float32
-    )
+    return contract(left_arg, right_arg, 1, 1)
 
 
 def transposed_times(left_arg, right_arg):
-    return lax.dot_general(
-        left_arg, right_arg, (((0,), (0,)), ((), ())), preferred_element_type=jnp.float32
-    )
+    return contract(left_arg, right_arg, 0, 0)
+
+
+def split_times_transposed(left_arg, right_arg):
+    rows = left_arg.shape[0]
+    high = left_arg.astype(jnp.bfloat16)
+    low = (left_arg - high.astype(jnp.float32)).astype(jnp.bfloat16)
+    product = times_transposed(jnp.concatenate([high, low], axis=0), right_arg)
+    return product[:rows] + product[rows:]
+
+
+def visible_bias(region_first, region_last, phrase_counts, offset, tokens):
+    block_ids = (offset + jnp.arange(tokens, dtype=jnp.int32)) // BLOCK
+    phrase_ids = jnp.arange(region_first.shape[1], dtype=jnp.int32)
+    visible = (
+        (phrase_ids[None, :, None] < phrase_counts[:, None, None])
+        & (region_first[:, :, None] <= block_ids[None, None, :])
+        & (block_ids[None, None, :] <= region_last[:, :, None])
+    )
+    return jnp.where(visible, 0.0, -jnp.inf).astype(jnp.float32)
+
+
+def window(group, head_size):
+    start = group * GROUP * head_size
+    return start // 128 * 128, -(-(start + GROUP * head_size) // 128) * 128
+
+
+def own_columns(rows, group, head, head_size, low):
+    first = (group * GROUP + head) * head_size - low
+    column = lax.broadcasted_iota(jnp.int32, rows.shape, 1)
+    return jnp.where((column >= first) & (column < first + head_size), rows, jnp.zeros_like(rows))
+
+
+def block_diagonal(rows, group, head_size, low):
+    return jnp.concatenate(
+        [own_columns(rows, group, head, head_size, low) for head in range(GROUP)], axis=0
+    )
+
+
+def block_places(place_ref, scheme, chips):
+    chip, core, odd = place_ref[0], place_ref[1], place_ref[2]
+    steps = list(range(chips))
+    if chips == 4:
+        turn = odd if scheme == 0 else 1 - odd
+        steps = [0, 1 + turn, 2 - turn, 3]
+    return [2 * (chip ^ step) + other for other in (core, 1 - core) for step in steps]
+
+
+def load_blocks(blocks, offsets, whole, places, sem):
+    rows = whole.shape[0] // len(blocks)
+    copies = [
+        pltpu.make_async_copy(
+            block.at[pl.ds(offset, rows)],
+            whole.at[pl.ds(pl.multiple_of(place * rows, 16), rows)],
+            sem.at[i],
+        )
+        for i, (block, offset, place) in enumerate(zip(blocks, offsets, places))
+    ]
+    for copy in copies:
+        copy.start()
+    return copies
+
+
+def load_weight(name, layout, arrays, place_ref, chips, whole, sem):
+    scheme, blocks = layout[name]
+    return load_blocks(
+        [arrays[array] for array, _ in blocks],
+        [offset for _, offset in blocks],
+        whole,
+        block_places(place_ref, scheme, chips),
+        sem,
+    )
+
+
+def project(left_arg, right_arg):
+    return jnp.dot(left_arg, right_arg, preferred_element_type=jnp.float32)
+
+
+def join_kernel(*refs):
+    outs = [ref for ref in refs if ref.shape[0] == max(r.shape[0] for r in refs)]
+    parts = iter(refs[: len(refs) - len(outs)])
+    for out in outs:
+        start = 0
+        while start < out.shape[0]:
+            part = next(parts)
+            stop = min(start + part.shape[0], out.shape[0])
+            out[start:stop] = part[: stop - start]
+            start = stop
+
+
+def join_halves(out_ref, core, start, mine, far):
+    half = mine[0].shape[0]
+    for plane in range(len(mine)):
+        first = start + plane * 2 * half
+        out_ref[pl.ds(pl.multiple_of(first + core * half, 16), half)] = mine[plane][...]
+        out_ref[pl.ds(pl.multiple_of(first + (1 - core) * half, 16), half)] = far[plane][...]
+
+
+def head_parts(slots):
+    return [slice(head * slots, (head + 1) * slots) for head in range(GROUP)]
+
+
+def own_head_sum(full, group, head_size, low):
+    slots = full.shape[0] // GROUP
+    return functools.reduce(
+        jnp.add,
+        [
+            own_columns(full[part], group, head, head_size, low)
+            for head, part in enumerate(head_parts(slots))
+        ],
+    )
+
+
+def attend_kernel(chips, planes, images, layout, place_ref, phrase_ref, *refs):
+    others = planes - 1
+    mine, far = refs[:others], refs[others : 2 * others]
+    arrays = refs[2 * others : 2 * others + layout["arrays"]]
+    (
+        query_ref,
+        grad_ref,
+        bias_ref,
+        key_out,
+        score_out,
+        mine_out,
+        other_out,
+        slope_out,
+        hidden_out,
+        phrase_out,
+        first_weight,
+        second_weight,
+        key_weight,
+        value_weight,
+        query,
+        grad,
+        slope,
+        hidden,
+        all_phrases,
+        all_scores,
+        value_rows,
+        key_sum,
+        value_sum,
+        total,
+        first_sem,
+        second_sem,
+        key_sem,
+        value_sem,
+        row_sem,
+        out_sem,
+    ) = refs[2 * others + layout["arrays"] :]
+    first_copies = load_weight("first", layout, arrays, place_ref, chips, first_weight, first_sem)
+    second_copies = load_weight(
+        "second", layout, arrays, place_ref, chips, second_weight, second_sem
+    )
+    key_copies = load_weight("key", layout, arrays, place_ref, chips, key_weight, key_sem)
+    value_copies = load_weight("value", layout, arrays, place_ref, chips, value_weight, value_sem)
+    query_copy = pltpu.make_async_copy(query_ref, query, row_sem.at[0])
+    query_copy.start()
+    grad_copy = pltpu.make_async_copy(grad_ref, grad, row_sem.at[1])
+    grad_copy.start()
+    own_rows = phrase_ref.shape[0]
+    all_phrases[:own_rows] = phrase_ref[...]
+    join_halves(all_phrases, place_ref[1], own_rows, mine, far)
+    out_copies = [pltpu.make_async_copy(all_phrases, phrase_out, out_sem.at[0])]
+    out_copies[0].start()
+    for copy in first_copies:
+        copy.wait()
+    pre_act = project(all_phrases[...], first_weight[...])
+    sigmoid = jax.nn.sigmoid(pre_act)
+    hidden[...] = (pre_act * sigmoid).astype(jnp.bfloat16)
+    slope[...] = sigmoid * (1.0 + pre_act * (1.0 - sigmoid))
+    out_copies.append(pltpu.make_async_copy(hidden, hidden_out, out_sem.at[1]))
+    out_copies.append(pltpu.make_async_copy(slope, slope_out, out_sem.at[2]))
+    out_copies[1].start()
+    out_copies[2].start()
+    for copy in second_copies:
+        copy.wait()
+    encoded = project(hidden[:own_rows], second_weight[...]).astype(jnp.bfloat16)
+    for copy in key_copies:
+        copy.wait()
+    key_out[...] = project(encoded, key_weight[...]).astype(jnp.bfloat16)
+    for copy in value_copies:
+        copy.wait()
+    value_rows[...] = project(encoded, value_weight[...]).astype(jnp.bfloat16)
+    query_copy.wait()
+    grad_copy.wait()
+
+    slots = own_rows // images
+    features = query.shape[1]
+    tokens = query.shape[0] // images
+    head_size = features // H
+    scale = head_size ** (-0.5)
+    key_sum[...] = jnp.zeros_like(key_sum)
+    value_sum[...] = jnp.zeros_like(value_sum)
+    for image in range(images):
+        rows = pl.ds(image * slots, slots)
+        here = pl.ds(image * tokens, tokens)
+        bias = bias_ref[image]
+        for group in range(H // GROUP):
+            low, high = window(group, head_size)
+            columns = pl.ds(low, high - low)
+            keys = block_diagonal(key_out[rows, columns], group, head_size, low)
+            values = block_diagonal(value_rows[rows, columns], group, head_size, low)
+            queries = query[here, columns]
+            grads = grad[here, columns]
+            scores = times_transposed(keys, queries)
+            prob_grad = times_transposed(values, grads)
+            probs_low, score_grad = [], []
+            for part in head_parts(slots):
+                score = scores[part] * scale + bias
+                exponent = jnp.exp(score - jnp.max(score, axis=0, keepdims=True))
+                probs = exponent * (1.0 / jnp.sum(exponent, axis=0, keepdims=True))
+                upstream = prob_grad[part]
+                inner = jnp.sum(probs * upstream, axis=0, keepdims=True)
+                probs_low.append(probs.astype(jnp.bfloat16))
+                score_grad.append((probs * (upstream - inner) * scale).astype(jnp.bfloat16))
+            probs_low = jnp.concatenate(probs_low, axis=0)
+            score_grad = jnp.concatenate(score_grad, axis=0)
+            all_scores[image, pl.ds(group * GROUP * slots, GROUP * slots)] = score_grad
+            key_sum[rows, columns] += own_head_sum(
+                project(score_grad, queries), group, head_size, low
+            )
+            value_sum[rows, columns] += own_head_sum(
+                project(probs_low, grads), group, head_size, low
+            )
+        out_copies.append(
+            pltpu.make_async_copy(all_scores.at[image], score_out.at[image], out_sem.at[3 + image])
+        )
+        out_copies[-1].start()
+    total[...] = split_times_transposed(key_sum[...], key_weight[...]) + split_times_transposed(
+        value_sum[...], value_weight[...]
+    )
+    core = place_ref[1]
+    half = mine_out.shape[0]
+    mine_out[...] = total[pl.ds(pl.multiple_of(core * half, 8), half)]
+    other_out[...] = total[pl.ds(pl.multiple_of((1 - core) * half, 8), half)]
+    for copy in out_copies:
+        copy.wait()
+
+
+def latent_kernel(score_ref, key_ref, weight_ref, out_ref, query_grad):
+    features = weight_ref.shape[1]
+    head_size = features // H
+    slots = key_ref.shape[0]
+
+    @pl.when(pl.program_id(0) == 0)
+    def _():
+        parts = []
+        for group in range(H // GROUP):
+            low, high = window(group, head_size)
+            keys = block_diagonal(key_ref[:, low:high], group, head_size, low)
+            score_grad = score_ref[0, group * GROUP * slots : (group + 1) * GROUP * slots]
+            part = transposed_times(score_grad, keys)
+            if low:
+                part = jnp.concatenate([jnp.zeros((part.shape[0], low), jnp.float32), part], axis=1)
+            if high < features:
+                part = jnp.concatenate(
+                    [part, jnp.zeros((part.shape[0], features - high), jnp.float32)], axis=1
+                )
+            parts.append(part)
+        query_grad[...] = functools.reduce(jnp.add, parts).astype(jnp.bfloat16)
+
+    out_ref[...] = times_transposed(query_grad[...], weight_ref[...]).astype(jnp.bfloat16)
+
+
+def weight_grad_kernel(chips, planes, layout, place_ref, *refs):
+    mine, far = refs[:planes], refs[planes : 2 * planes]
+    arrays = refs[2 * planes : 2 * planes + layout["arrays"]]
+    (
+        slope_ref,
+        hidden_ref,
+        phrase_ref,
+        second_out,
+        first_out,
+        phrase_out,
+        first_weight,
+        second_weight,
+        encoded_grad,
+        slope,
+        second_grad,
+        first_grad,
+        first_sem,
+        second_sem,
+        row_sem,
+    ) = refs[2 * planes + layout["arrays"] :]
+    second_copies = load_weight(
+        "second", layout, arrays, place_ref, chips, second_weight, second_sem
+    )
+    slope_copy = pltpu.make_async_copy(slope_ref, slope, row_sem.at[0])
+    slope_copy.start()
+    first_copies = load_weight("first", layout, arrays, place_ref, chips, first_weight, first_sem)
+    join_halves(encoded_grad, place_ref[1], 0, mine, far)
+    second_grad[...] = transposed_times(hidden_ref[...], encoded_grad[...])
+    second_copy = pltpu.make_async_copy(second_grad, second_out, row_sem.at[1])
+    second_copy.start()
+    for copy in second_copies:
+        copy.wait()
+    hidden_grad = times_transposed(encoded_grad[...], second_weight[...])
+    slope_copy.wait()
+    act_grad = (hidden_grad * slope[...]).astype(jnp.bfloat16)
+    first_grad[...] = transposed_times(phrase_ref[...], act_grad)
+    first_copy = pltpu.make_async_copy(first_grad, first_out, row_sem.at[2])
+    first_copy.start()
+    for copy in first_copies:
+        copy.wait()
+    phrase_out[...] = times_transposed(
+        act_grad[: phrase_out.shape[0]], first_weight[...]
+    ).astype(jnp.bfloat16)
+    second_copy.wait()
+    first_copy.wait()
 
 
 def attention_grads(
@@ -50,7 +377,7 @@
         jnp.einsum("ithd,iphd->ithp", query_heads, key_heads, preferred_element_type=jnp.float32)
         * score_scale
     )
-    block_ids = (offset + jnp.arange(tokens, dtype=jnp.int32)) // (tokens // 4)
+    block_ids = (offset + jnp.arange(tokens, dtype=jnp.int32)) // BLOCK
     phrase_ids = jnp.arange(slot_count, dtype=jnp.int32)
     visible = (
         (phrase_ids[None, None, :] < phrase_counts[:, None, None])
@@ -82,7 +409,7 @@
     return (latent_grad.reshape(images, tokens, features), key_part, value_part)
 
 
-def local(
+def plain(
     latents,
     out_grad,
     phrases,
@@ -144,7 +471,266 @@
     return (latent_grad, phrase_grad.reshape(images, slot_count, features), first_grad, second_grad)
 
 
+def local(shards, planes, *args):
+    shard_rows = args[6].shape[0]
+    if shard_rows % 16:
+        return plain(*args)
+    return tiled(shards, planes, *args)
+
+
+def tiled(
+    shards,
+    planes,
+    latents,
+    out_grad,
+    phrases,
+    query_weight,
+    key_weight,
+    value_weight,
+    first_weight,
+    second_weight,
+    region_first,
+    region_last,
+    phrase_counts,
+):
+    images, tokens, features = latents.shape
+    slots = phrases.shape[1]
+    shard_rows = first_weight.shape[0]
+    chips = shards // 2
+    rows = images * slots
+    half = rows // 2
+    shard, plane = lax.axis_index("seq"), lax.axis_index("dp")
+    core = shard % 2
+    place = jnp.stack([shard // 2, core, plane % 2]).astype(jnp.int32)
+    shape = jax.ShapeDtypeStruct
+
+    def swap(array, distance):
+        return lax.ppermute(array, "seq", [(i, i ^ distance) for i in range(shards)])
+
+    def swap_by_plane(array, even, odd):
+        pairs = [
+            (p * shards + i, p * shards + (i ^ (2 * (odd if p % 2 else even))))
+            for p in range(planes)
+            for i in range(shards)
+        ]
+        return lax.ppermute(array, ("dp", "seq"), pairs)
+
+    def chip_peers(array):
+        return [swap(array, 2 * k) for k in range(1, chips)]
+
+    def plane_swap(array, distance):
+        return lax.ppermute(array, "dp", [(i, i ^ distance) for i in range(planes)])
+
+    def plane_peers(array):
+        return [plane_swap(array, k) for k in range(1, planes)]
+
+    def after(array, *others):
+        return lax.optimization_barrier((array, *others))[0]
+
+    def with_other_core(blocks):
+        return blocks + [swap(block, 1) for block in blocks]
+
+    def total_of(parts):
+        return functools.reduce(jnp.add, [part.astype(jnp.float32) for part in parts])
+
+    def project_queries(tokens_in):
+        return jnp.dot(
+            tokens_in.reshape(images * tokens, features),
+            query_weight,
+            preferred_element_type=jnp.float32,
+        ).astype(jnp.bfloat16)
+
+    phrase_rows = phrases.reshape(rows, features)
+    bias = visible_bias(region_first, region_last, phrase_counts, shard * tokens, tokens)
+    weight_shape = pltpu.VMEM((features, features), jnp.bfloat16)
+    row_shape = pltpu.VMEM((images * tokens, features), jnp.bfloat16)
+    sum_shape = pltpu.VMEM((rows, features), jnp.float32)
+    block_sems = pltpu.SemaphoreType.DMA((2 * chips,))
+    def join(parts, lengths, whole_rows):
+        return pl.pallas_call(
+            join_kernel,
+            out_shape=[shape((whole_rows, features), jnp.bfloat16)] * lengths,
+            in_specs=[VMEM] * len(parts),
+            out_specs=[VMEM] * lengths,
+            name="join",
+        )(*parts)
+
+    encoder, projector = join(
+        [first_weight, second_weight, key_weight, value_weight], 2, 2 * shard_rows
+    )
+    if chips == 4:
+        encoder_near = swap_by_plane(encoder, 1, 2)
+        projector_near = swap_by_plane(projector, 2, 1)
+        queries = project_queries(latents)
+        encoder_own, projector_own = swap(encoder, 1), swap(projector, 1)
+        own_half = lax.dynamic_slice_in_dim(
+            after(phrase_rows, queries, encoder_own, projector_own, bias), core * half, half, 0
+        )
+        plane_phrases = plane_peers(own_half)
+        encoder_next, projector_next, plane_phrases, value_next = lax.optimization_barrier(
+            (encoder_near, projector_near, plane_phrases, value_weight)
+        )
+        encoder_far = swap_by_plane(encoder_next, 2, 1)
+        encoder_third = plane_swap(encoder_next, 1)
+        projector_far = swap_by_plane(projector_next, 1, 2)
+        value_third = swap_by_plane(value_next, 1, 2)
+        key_third = plane_swap(projector_next[:shard_rows], 1)
+        far_phrases = [swap(part, 1) for part in plane_phrases]
+        arrays = [encoder, encoder_near, projector, projector_near]
+        arrays += [encoder_far, encoder_third, projector_far, key_third, value_third]
+        swapped = [encoder_own, swap(encoder_next, 1), projector_own, swap(projector_next, 1)]
+        encoder_far = after(encoder_far, *swapped, *far_phrases)
+        arrays += swapped
+        arrays += [
+            swap(block, 1)
+            for block in (encoder_far, encoder_third, projector_far, key_third, value_third)
+        ]
+        layout = {
+            "first": (0, [(0, 0), (1, 0), (5, 0), (4, 0)]),
+            "second": (0, [(i, shard_rows) for i in (0, 1, 5, 4)]),
+            "key": (1, [(2, 0), (3, 0), (7, 0), (6, 0)]),
+            "value": (1, [(2, shard_rows), (3, shard_rows), (8, 0), (6, shard_rows)]),
+        }
+    else:
+        own_half = lax.dynamic_slice_in_dim(phrase_rows, core * half, half, 0)
+        plane_phrases = plane_peers(own_half)
+        far_phrases = [swap(part, 1) for part in plane_phrases]
+        queries = project_queries(latents)
+        arrays = [encoder] + chip_peers(encoder) + [projector] + chip_peers(projector)
+        arrays += [swap(block, 1) for block in arrays]
+        layout = {
+            name: (0, [(first + k, offset) for k in range(chips)])
+            for name, first, offset in (
+                ("first", 0, 0),
+                ("second", 0, shard_rows),
+                ("key", chips, 0),
+                ("value", chips, shard_rows),
+            )
+        }
+    near_count = len(arrays) // 2
+    for name, (scheme, blocks) in layout.items():
+        layout[name] = (scheme, blocks + [(near_count + i, offset) for i, offset in blocks])
+    layout["arrays"] = len(arrays)
+    grads = out_grad.reshape(images * tokens, features)
+
+    all_rows = planes * rows
+    key_rows, score_grad, grad_mine, grad_other, slope, all_hidden, all_phrases = pl.pallas_call(
+        functools.partial(attend_kernel, chips, planes, images, layout),
+        out_shape=[
+            shape((rows, features), jnp.bfloat16),
+            shape((images, H * slots, tokens), jnp.bfloat16),
+            shape((half, features), jnp.float32),
+            shape((half, features), jnp.float32),
+            shape((all_rows, features), jnp.float32),
+            shape((all_rows, features), jnp.bfloat16),
+            shape((all_rows, features), jnp.bfloat16),
+        ],
+        in_specs=[SMEM] + [VMEM] * (2 * planes - 1) + [HBM] * len(arrays) + [ANY] * 2 + [VMEM],
+        out_specs=[VMEM, ANY, VMEM, VMEM, ANY, ANY, ANY],
+        scratch_shapes=[
+            weight_shape,
+            weight_shape,
+            weight_shape,
+            weight_shape,
+            row_shape,
+            row_shape,
+            pltpu.VMEM((all_rows, features), jnp.float32),
+            pltpu.VMEM((all_rows, features), jnp.bfloat16),
+            pltpu.VMEM((all_rows, features), jnp.bfloat16),
+            pltpu.VMEM((images, H * slots, tokens), jnp.bfloat16),
+            pltpu.VMEM((rows, features), jnp.bfloat16),
+            sum_shape,
+            sum_shape,
+            sum_shape,
+            block_sems,
+            block_sems,
+            block_sems,
+            block_sems,
+            pltpu.SemaphoreType.DMA((2,)),
+            pltpu.SemaphoreType.DMA((3 + images,)),
+        ],
+        compiler_params=vmem(60),
+        cost_estimate=pl.CostEstimate(
+            flops=10**10, bytes_accessed=18 * 10**6, transcendentals=10**6
+        ),
+        name="attend",
+    )(place, phrase_rows, *plane_phrases, *far_phrases, *arrays, queries, grads, bias)
+    steps = 3 if features % 384 == 0 else 1
+    tile = features // steps
+
+    def latent_part(image, scores_in, whole=None):
+        given = [] if whole is None else [whole]
+        return pl.pallas_call(
+            latent_kernel if whole is None else lambda _, *refs: latent_kernel(*refs),
+            out_shape=shape((images * tokens, features), jnp.bfloat16),
+            grid=(steps,),
+            in_specs=[ANY] * len(given)
+            + [
+                pl.BlockSpec((1, H * slots, tokens), lambda t: (image, 0, 0)),
+                pl.BlockSpec((slots, features), lambda t: (image, 0)),
+                pl.BlockSpec((tile, features), lambda t: (t, 0)),
+            ],
+            out_specs=pl.BlockSpec((tokens, tile), lambda t: (image, t)),
+            scratch_shapes=[pltpu.VMEM((tokens, features), jnp.bfloat16)],
+            input_output_aliases={0: 0} if given else {},
+            compiler_params=vmem(60),
+            cost_estimate=pl.CostEstimate(
+                flops=3 * 10**9, bytes_accessed=4 * 10**6, transcendentals=0
+            ),
+            name="latent",
+        )(*given, scores_in, key_rows, query_weight)
+
+    grad_pair = total_of([grad_mine, swap(grad_other, 1)]).astype(jnp.bfloat16)
+    grad_own = total_of([grad_pair] + chip_peers(grad_pair)).astype(jnp.bfloat16)
+    latent_grad = latent_part(0, score_grad)
+    grad_own, latent_grad = lax.optimization_barrier((grad_own, latent_grad))
+    own_hidden = lax.dynamic_slice_in_dim(all_hidden, shard * shard_rows, shard_rows, 1)
+    all_own_phrases = lax.dynamic_slice_in_dim(all_phrases, shard * shard_rows, shard_rows, 1)
+    for image in range(1, images):
+        latent_grad = latent_part(image, score_grad, latent_grad)
+    grad_mines = [grad_own] + plane_peers(grad_own)
+    grad_fars = [swap(part, 1) for part in grad_mines]
+    second_grad, first_grad, phrase_grad = pl.pallas_call(
+        functools.partial(weight_grad_kernel, chips, planes, layout),
+        out_shape=[
+            shape((shard_rows, features), jnp.float32),
+            shape((shard_rows, features), jnp.float32),
+            shape((rows, features), jnp.bfloat16),
+        ],
+        in_specs=[SMEM] + [VMEM] * (2 * planes) + [ANY] * (len(arrays) + 1) + [VMEM] * 2,
+        out_specs=[ANY, ANY, VMEM],
+        scratch_shapes=[
+            weight_shape,
+            weight_shape,
+            pltpu.VMEM((all_rows, features), jnp.bfloat16),
+            pltpu.VMEM((all_rows, features), jnp.float32),
+            pltpu.VMEM((shard_rows, features), jnp.float32),
+            pltpu.VMEM((shard_rows, features), jnp.float32),
+            block_sems,
+            block_sems,
+            pltpu.SemaphoreType.DMA((3,)),
+        ],
+        compiler_params=vmem(60),
+        name="weight_grads",
+    )(
+        place,
+        *grad_mines,
+        *grad_fars,
+        *arrays,
+        slope,
+        own_hidden,
+        all_own_phrases,
+    )
+    return (
+        latent_grad.reshape(images, tokens, features),
+        phrase_grad.reshape(images, slots, features),
+        first_grad,
+        second_grad,
+    )
+
+
 def solution(mesh):
+    shards, planes = mesh.shape["seq"], mesh.shape["dp"]
     in_specs = (
         P("dp", "seq", None),
         P("dp", "seq", None),
@@ -159,4 +745,10 @@
         P("dp"),
     )
     out_specs = (P("dp", "seq", None), P("dp", None, None), P("seq", None), P("seq", None))
-    return jax.shard_map(local, mesh=mesh, in_specs=in_specs, out_specs=out_specs, check_vma=False)
+    return jax.shard_map(
+        functools.partial(local, shards, planes),
+        mesh=mesh,
+        in_specs=in_specs,
+        out_specs=out_specs,
+        check_vma=False,
+    )

time: 274 us -> 108 us (0.39)
  waiting for transfers between devices: 138 us -> 32.5 us
  matrix products: 54.6 us -> 6.54 us
  Pallas kernels: 0 us -> 37 us
  local copies, waits for them, and re-layouts: 35.8 us -> 3.47 us
  blocking collectives: 30.4 us -> 0 us
  starting transfers between devices: 0.19 us -> 24.6 us
  between operations: 13.9 us -> 1.07 us
    all_gather x4 -> x0, waiting for transfers between devices: 93 us -> none  [the longest x1 29.8 us: local(): lax.all_gather(key_weight, 'seq', axis=0, tiled=True)]
    dot_general x16 -> x1, matrix products: 50.7 us -> 6.54 us  [project_queries(): jnp.dot(tokens_in.reshape(images * tokens, features), query_weight, prefe...]
    psum x1 -> x0, waiting for transfers between devices: 42.4 us -> none  [local(): first_grad, second_grad = lax.psum((first_grad, second_grad), 'dp')]
    pallas_call x0 -> x5, Pallas kernels: none -> 37 us  [the longest x1 15.7 us: tiled(): pl.pallas_call(functools.partial(attend_kernel, chips, planes, images, la...]
    ppermute x0 -> x33, waiting for transfers between devices: none -> 32.5 us  [the longest x5 18.3 us: swap_by_plane(): return lax.ppermute(array, ('dp', 'seq'), pairs)]
    psum x1 -> x0, blocking collectives: 30.4 us -> none  [local(): key_sum_grad, value_sum_grad = lax.psum((key_part, value_part), 'seq')]
    ppermute x0 -> x33, starting transfers between devices: none -> 24.6 us  [the longest x8 11.6 us: plane_swap(): return lax.ppermute(array, 'dp', [(i, i ^ distance) for i in range(planes)])]
    reshape x4 -> x0, local copies, waits for them, and re-layouts: 18 us -> none  [the longest x2 16.8 us: attention_grads(): query_heads = queries.reshape(images, tokens, head_count, head_size)]
  transfers between devices with their start and end apart: 5 -> 33, of which waited for: 5 -> 11; matrix products, arithmetic and copies ran while one was open for 19% -> 9% of each run, Pallas kernels for 0% -> 10%
where the time goes in v1:
time: 108 us
  Pallas kernels  37 us (34%)
  waiting for transfers between devices  32.5 us (30%)
  starting transfers between devices  24.6 us (23%)
  matrix products  6.54 us (6%)
  local copies, waits for them, and re-layouts  3.47 us (3%)
  other arithmetic  2.46 us (2%)
    ppermute x5, waiting for transfers between devices, swap_by_plane(): return lax.ppermute(array, ('dp', 'seq'), pairs)  18.3 us
    pallas_call x1, Pallas kernels, tiled(): pl.pallas_call(functools.partial(attend_kernel, chips, planes, images, la...  15.7 us
    ppermute x8, starting transfers between devices, plane_swap(): return lax.ppermute(array, 'dp', [(i, i ^ distance) for i in range(planes)])  11.6 us
    ppermute x8, waiting for transfers between devices, plane_swap(): return lax.ppermute(array, 'dp', [(i, i ^ distance) for i in range(planes)])  11.4 us
    pallas_call x2, Pallas kernels, latent_part(): pl.pallas_call(latent_kernel if whole is None else lambda _, *refs: laten...  11.3 us
    pallas_call x1, Pallas kernels, tiled(): pl.pallas_call(functools.partial(weight_grad_kernel, chips, planes, layou...  7.51 us
    dot_general x1, matrix products, project_queries(): jnp.dot(tokens_in.reshape(images * tokens, features), query_weight, prefe...  6.54 us
    ppermute x5, starting transfers between devices, swap_by_plane(): return lax.ppermute(array, ('dp', 'seq'), pairs)  6.54 us
  transfers between devices with their start and end apart: 33, of which 11 were waited for; matrix products, arithmetic and copies ran while one was open for 9% of the time, Pallas kernels for 10%

profile of v1, /device:TPU:0, one launch (start us, length us, event | category | flops | bytes accessed | tf_op | source)
XLA Modules:
  0.0 107.7 jit_solution(6595474287315463984)
XLA Ops:
  0.6 2.6 %join.1 = (bf16[288,1152]{1,0:T(8,128)(2,1)}, bf16[288,1152]{1,0:T(8,128)(2,1)}) custom-call(bf16[144,1152]{1,0:T(8,128)(2,1)} %refs_0_.1, bf16[144,1152]{1,0:T(8,128)(2,1)} %refs_1_.1, bf16[144,1152]{1,0:T(8,128)(2,1)} %refs_2_.2, bf16[144,1152]{1,0:T(8,128)(2,1)} %refs_3_.1), custom_call_target="tpu_custom_call" | custom-call | tf_op jit(solution)/shard_map/join/pallas_call | solution.py:550
  3.7 2.5 %collective-permute-start = (bf16[288,1152]{1,0:T(8,128)(2,1)}, bf16[288,1152]{1,0:T(8,128)(2,1)}, u32[]{:S(2)}, u32[]{:S(2)}) collective-permute-start(bf16[288,1152]{1,0:T(8,128)(2,1)} %get-tuple-element.26.refs_6_.refs_8_), channel_id=1, source_target_pairs={{0,2},{1,3},{2,0},{3,1},{4,6},{5,7},{6,4},{7,5},{8,12},{9,13},{10,... | collective-permute-start | bytes 1990664 | tf_op jit(solution)/shard_map/ppermute | solution.py:516
  6.4 1.5 %collective-permute-start.1 = (bf16[288,1152]{1,0:T(8,128)(2,1)}, bf16[288,1152]{1,0:T(8,128)(2,1)S(1)}, u32[]{:S(2)}, u32[]{:S(2)}) collective-permute-start(bf16[288,1152]{1,0:T(8,128)(2,1)} %get-tuple-element.27.refs_8_.refs_10_), channel_id=1, source_target_pairs={{0,4},{1,5},{2,6},{3,7},{4,0},{5,1},{6,2},{7,3},{8,10},{9,11},{10,... | collective-permute-start | bytes 1990664 | tf_op jit(solution)/shard_map/ppermute | solution.py:516
  7.9 6.5 %convolution_convert_fusion.refs_24_ = bf16[1024,1152]{1,0:T(8,128)(2,1)} fusion(bf16[1024,1152]{1,0:T(8,128)(2,1)S(1)} %bitcast.10, bf16[1152,1152]{1,0:T(8,128)(2,1)} %refs_2_.3), kind=kOutput, calls=%fused_computation | convolution fusion | flops 2719088640 | bytes 7372800 | tf_op jit(solution)/shard_map/dot_general | solution.py:537
  14.6 0.8 and_select_fusion.refs_26_
  15.4 1.6 %collective-permute-start.4 = (bf16[32,1152]{1,0:T(8,128)(2,1)S(1)}, bf16[32,1152]{1,0:T(8,128)(2,1)S(1)}, u32[]{:S(2)}, u32[]{:S(2)}) collective-permute-start(bf16[32,1152]{1,0:T(8,128)(2,1)S(1)} %constant_dynamic-slice_fusion.2), channel_id=1, source_target_pairs={{0,8},{8,0},{16,24},{24,16},{1,9},{9,1},{17,25},{25,17},{2,10},{10... | collective-permute-start | bytes 221192 | tf_op jit(solution)/shard_map/ppermute | solution.py:522
  17.0 2.6 %collective-permute-start.5 = (bf16[32,1152]{1,0:T(8,128)(2,1)S(1)}, bf16[32,1152]{1,0:T(8,128)(2,1)S(1)}, u32[]{:S(2)}, u32[]{:S(2)}) collective-permute-start(bf16[32,1152]{1,0:T(8,128)(2,1)S(1)} %constant_dynamic-slice_fusion.2), channel_id=1, source_target_pairs={{0,16},{8,24},{16,0},{24,8},{1,17},{9,25},{17,1},{25,9},{2,18},{10... | collective-permute-start | bytes 221192 | tf_op jit(solution)/shard_map/ppermute | solution.py:522
  19.8 2.2 %collective-permute-done.refs_7_.refs_9_ = bf16[288,1152]{1,0:T(8,128)(2,1)} collective-permute-done((bf16[288,1152]{1,0:T(8,128)(2,1)}, bf16[288,1152]{1,0:T(8,128)(2,1)}, u32[]{:S(2)}, u32[]{:S(2)}) %collective-permute-start) | collective-permute-done | bytes 663584 | tf_op jit(solution)/shard_map/ppermute | solution.py:516
  22.0 1.6 %collective-permute-done.1.refs_9_.refs_11_ = bf16[288,1152]{1,0:T(8,128)(2,1)S(1)} collective-permute-done((bf16[288,1152]{1,0:T(8,128)(2,1)}, bf16[288,1152]{1,0:T(8,128)(2,1)S(1)}, u32[]{:S(2)}, u32[]{:S(2)}) %collective-permute-start.1) | collective-permute-done | bytes 663584 | tf_op jit(solution)/shard_map/ppermute | solution.py:516
  23.7 1.3 %collective-permute-done.5.refs_1_ = bf16[32,1152]{1,0:T(8,128)(2,1)S(1)} collective-permute-done((bf16[32,1152]{1,0:T(8,128)(2,1)S(1)}, bf16[32,1152]{1,0:T(8,128)(2,1)S(1)}, u32[]{:S(2)}, u32[]{:S(2)}) %collective-permute-start.5) | collective-permute-done | bytes 73760 | tf_op jit(solution)/shard_map/ppermute | solution.py:522
  25.0 0.8 collective-permute-done.6.refs_2_
  27.4 1.3 %collective-permute-start.11 = (bf16[288,1152]{1,0:T(8,128)(2,1)}, bf16[288,1152]{1,0:T(8,128)(2,1)}, u32[]{:S(2)}, u32[]{:S(2)}) collective-permute-start(bf16[288,1152]{1,0:T(8,128)(2,1)} %collective-permute-done.refs_7_.refs_9_), channel_id=1, source_target_pairs={{0,8},{8,0},{16,24},{24,16},{1,9},{9,1},{17,25},{25,17},{2,10},{10... | collective-permute-start | bytes 1990664 | tf_op jit(solution)/shard_map/ppermute | solution.py:522
  29.4 1.5 %collective-permute-start.12 = (bf16[288,1152]{1,0:T(8,128)(2,1)S(1)}, bf16[288,1152]{1,0:T(8,128)(2,1)}, u32[]{:S(2)}, u32[]{:S(2)}) collective-permute-start(bf16[288,1152]{1,0:T(8,128)(2,1)S(1)} %collective-permute-done.1.refs_9_.refs_11_), channel_id=1, source_target_pairs={{0,2},{1,3},{2,0},{3,1},{4,6},{5,7},{6,4},{7,5},{8,12},{9,13},{10,... | collective-permute-start | bytes 1990664 | tf_op jit(solution)/shard_map/ppermute | solution.py:516
  30.9 13.1 %collective-permute-done.10.refs_10_.refs_12_ = bf16[288,1152]{1,0:T(8,128)(2,1)} collective-permute-done((bf16[288,1152]{1,0:T(8,128)(2,1)}, bf16[288,1152]{1,0:T(8,128)(2,1)}, u32[]{:S(2)}, u32[]{:S(2)}) %collective-permute-start.10) | collective-permute-done | bytes 663584 | tf_op jit(solution)/shard_map/ppermute | solution.py:516
  44.0 1.3 %collective-permute-start.13 = (bf16[144,1152]{1,0:T(8,128)(2,1)S(1)}, bf16[144,1152]{1,0:T(8,128)(2,1)S(1)}, u32[]{:S(2)}, u32[]{:S(2)}) collective-permute-start(bf16[144,1152]{1,0:T(8,128)(2,1)S(1)} %slice.3), channel_id=1, source_target_pairs={{0,8},{8,0},{16,24},{24,16},{1,9},{9,1},{17,25},{25,17},{2,10},{10... | collective-permute-start | bytes 995336 | tf_op jit(solution)/shard_map/ppermute | solution.py:522
  46.7 6.7 %collective-permute-done.13.refs_13_.refs_15_ = bf16[144,1152]{1,0:T(8,128)(2,1)S(1)} collective-permute-done((bf16[144,1152]{1,0:T(8,128)(2,1)S(1)}, bf16[144,1152]{1,0:T(8,128)(2,1)S(1)}, u32[]{:S(2)}, u32[]{:S(2)}) %collective-permute-start.13) | collective-permute-done | bytes 331808 | tf_op jit(solution)/shard_map/ppermute | solution.py:522
  53.4 1.3 %collective-permute-done.14.refs_14_.refs_16_ = bf16[144,1152]{1,0:T(8,128)(2,1)} collective-permute-done((bf16[144,1152]{1,0:T(8,128)(2,1)}, bf16[144,1152]{1,0:T(8,128)(2,1)}, u32[]{:S(2)}, u32[]{:S(2)}) %collective-permute-start.14) | collective-permute-done | bytes 331808 | tf_op jit(solution)/shard_map/ppermute | solution.py:516
  54.8 0.7 pad_add_fusion.place_ref
  55.4 1.3 %collective-permute-done.21.refs_23_.refs_25_ = bf16[144,1152]{1,0:T(8,128)(2,1)} collective-permute-done((bf16[144,1152]{1,0:T(8,128)(2,1)}, bf16[144,1152]{1,0:T(8,128)(2,1)}, u32[]{:S(2)}, u32[]{:S(2)}) %collective-permute-start.21) | collective-permute-done | bytes 331808 | tf_op jit(solution)/shard_map/ppermute | solution.py:508
  56.8 15.7 %attend.1 = (bf16[64,1152]{1,0:T(8,128)(2,1)}, bf16[2,512,512]{2,1,0:T(8,128)(2,1)}, f32[32,1152]{1,0:T(8,128)}, f32[32,1152]{1,0:T(8,128)}, f32[256,1152]{1,0:T...) custom-call(s32[3]{0:T(128)} %pad_add_fusion.place_ref, bf16[64,1152]{1,0:T(8,128)(2,1)} %bitcast.11, ...), custom_call_target="tpu_custom_call" | custom-call | flops 10000000000 | bytes 18000000 | tf_op jit(solution)/shard_map/attend/pallas_call | solution.py:617
  72.7 1.4 %collective-permute-done.22 = f32[32,1152]{1,0:T(8,128)S(1)} collective-permute-done((f32[32,1152]{1,0:T(8,128)}, f32[32,1152]{1,0:T(8,128)S(1)}, u32[]{:S(2)}, u32[]{:S(2)}) %collective-permute-start.22) | collective-permute-done | bytes 147488 | tf_op jit(solution)/shard_map/ppermute | solution.py:508
  74.2 0.9 add_convert_fusion.1
  76.2 2.5 %collective-permute-start.25 = (bf16[32,1152]{1,0:T(8,128)(2,1)S(1)}, bf16[32,1152]{1,0:T(8,128)(2,1)S(1)}, u32[]{:S(2)}, u32[]{:S(2)}) collective-permute-start(bf16[32,1152]{1,0:T(8,128)(2,1)S(1)} %add_convert_fusion.1), channel_id=1, source_target_pairs={{0,6},{1,7},{2,4},{3,5},{4,2},{5,3},{6,0},{7,1},{8,14},{9,15},{10,... | collective-permute-start | bytes 221192 | tf_op jit(solution)/shard_map/ppermute | solution.py:508
  78.6 5.6 %latent.2._ = bf16[1024,1152]{1,0:T(8,128)(2,1)} custom-call(bf16[2,512,512]{2,1,0:T(8,128)(2,1)} %get-tuple-element.38.score_ref.refs_0_, bf16[64,1152]{1,0:T(8,128)(2,1)} %get-tuple-element.39.key_ref.refs_1_, bf16[1152,1152]{1,0:T(8,128)(2,1)} %refs_2_.3), custom_call_target="tpu_custom_call" | custom-call | flops 3000000000 | bytes 4000000 | tf_op jit(solution)/shard_map/latent/pallas_call | solution.py:663
  84.3 0.8 collective-permute-start.26
  85.1 2.3 %collective-permute-start.27 = (bf16[32,1152]{1,0:T(8,128)(2,1)S(1)}, bf16[32,1152]{1,0:T(8,128)(2,1)S(1)}, u32[]{:S(2)}, u32[]{:S(2)}) collective-permute-start(bf16[32,1152]{1,0:T(8,128)(2,1)S(1)} %add_convert_fusion.refs_0_), channel_id=1, source_target_pairs={{0,16},{8,24},{16,0},{24,8},{1,17},{9,25},{17,1},{25,9},{2,18},{10... | collective-permute-start | bytes 221192 | tf_op jit(solution)/shard_map/ppermute | solution.py:522
  87.4 1.4 %collective-permute-start.28 = (bf16[32,1152]{1,0:T(8,128)(2,1)S(1)}, bf16[32,1152]{1,0:T(8,128)(2,1)S(1)}, u32[]{:S(2)}, u32[]{:S(2)}) collective-permute-start(bf16[32,1152]{1,0:T(8,128)(2,1)S(1)} %add_convert_fusion.refs_0_), channel_id=1, source_target_pairs={{0,24},{8,16},{16,8},{24,0},{1,25},{9,17},{17,9},{25,1},{2,26},{10... | collective-permute-start | bytes 221192 | tf_op jit(solution)/shard_map/ppermute | solution.py:522
  88.8 1.9 %constant_dynamic-slice_fusion = (bf16[256,144]{1,0:T(8,128)(2,1)}, bf16[256,144]{1,0:T(8,128)(2,1)}) fusion(bf16[256,1152]{1,0:T(8,128)(2,1)} %get-tuple-element.44, s32[]{:T(128)S(6)} %select_n.41, bf16[256,1152]{1,0:T(8,128)(2,1)} %get-tuple-element.43), kind=kLoop, calls=%fused_computation.14 | loop fusion | bytes 294916 | tf_op jit(solution)/shard_map/dynamic_slice | solution.py:688
  91.2 1.2 %collective-permute-done.27.refs_2_ = bf16[32,1152]{1,0:T(8,128)(2,1)S(1)} collective-permute-done((bf16[32,1152]{1,0:T(8,128)(2,1)S(1)}, bf16[32,1152]{1,0:T(8,128)(2,1)S(1)}, u32[]{:S(2)}, u32[]{:S(2)}) %collective-permute-start.27) | collective-permute-done | bytes 73760 | tf_op jit(solution)/shard_map/ppermute | solution.py:522
  92.4 1.3 %collective-permute-done.28.refs_3_ = bf16[32,1152]{1,0:T(8,128)(2,1)S(1)} collective-permute-done((bf16[32,1152]{1,0:T(8,128)(2,1)S(1)}, bf16[32,1152]{1,0:T(8,128)(2,1)S(1)}, u32[]{:S(2)}, u32[]{:S(2)}) %collective-permute-start.28) | collective-permute-done | bytes 73760 | tf_op jit(solution)/shard_map/ppermute | solution.py:522
  93.6 5.7 %latent.3 = bf16[1024,1152]{1,0:T(8,128)(2,1)} custom-call(bf16[1024,1152]{1,0:T(8,128)(2,1)} %latent.2._, bf16[2,512,512]{2,1,0:T(8,128)(2,1)} %get-tuple-element.38.score_ref.refs_0_, bf16[64,1152]{1,0:T(8,128)(2,1)} %get-tuple-element.39.key_ref.refs_1_, bf16[1152,1152]{1,0:T(8,128)(2,1)} %refs_2_.3), custom_call_target="tpu_custom_call", output_to_operand_aliasing={{}: (0, {})} | custom-call | flops 3000000000 | bytes 4000000 | tf_op jit(solution)/shard_map/latent/pallas_call | solution.py:663
  100.0 7.5 %weight_grads.1 = (f32[144,1152]{1,0:T(8,128)}, f32[144,1152]{1,0:T(8,128)}, bf16[64,1152]{1,0:T(8,128)(2,1)}) custom-call(s32[3]{0:T(128)} %pad_add_fusion.place_ref, bf16[32,1152]{1,0:T(8,128)(2,1)} %copy-done.5, bf16[32,1152]{1,0:T(8,128)(2,1)} %copy-done.6, bf16[32,1152]{1,0:T(8,128)(2,1)} %copy-done.7, bf16[32,1152]{1,0:T(8,128)(2,1)} %copy-done.8, ...), custom_call_target="tpu_custom_call" | custom-call | tf_op jit(solution)/shard_map/weight_grads/pallas_call | solution.py:693
  (95 shorter events, 7.2 us)
Async XLA Ops:
  3.2 12.1 %collective-permute-start.2 = (bf16[288,1152]{1,0:T(8,128)(2,1)}, bf16[288,1152]{1,0:T(8,128)(2,1)}, u32[]{:S(2)}, u32[]{:S(2)}) collective-permute-start(bf16[288,1152]{1,0:T(8,128)(2,1)} %get-tuple-element.26.refs_6_.refs_8_), channel_id=1, source_target_pairs={{0,1},{1,0},{2,3},{3,2},{4,5},{5,4},{6,7},{7,6},{8,9},{9,8},{10,11... | collective-permute-start | bytes 1990664 | tf_op jit(solution)/shard_map/ppermute | solution.py:508
  3.7 18.4 %collective-permute-start = (bf16[288,1152]{1,0:T(8,128)(2,1)}, bf16[288,1152]{1,0:T(8,128)(2,1)}, u32[]{:S(2)}, u32[]{:S(2)}) collective-permute-start(bf16[288,1152]{1,0:T(8,128)(2,1)} %get-tuple-element.26.refs_6_.refs_8_), channel_id=1, source_target_pairs={{0,2},{1,3},{2,0},{3,1},{4,6},{5,7},{6,4},{7,5},{8,12},{9,13},{10,... | collective-permute-start | bytes 1990664 | tf_op jit(solution)/shard_map/ppermute | solution.py:516
  6.1 9.2 %collective-permute-start.3 = (bf16[288,1152]{1,0:T(8,128)(2,1)}, bf16[288,1152]{1,0:T(8,128)(2,1)}, u32[]{:S(2)}, u32[]{:S(2)}) collective-permute-start(bf16[288,1152]{1,0:T(8,128)(2,1)} %get-tuple-element.27.refs_8_.refs_10_), channel_id=1, source_target_pairs={{0,1},{1,0},{2,3},{3,2},{4,5},{5,4},{6,7},{7,6},{8,9},{9,8},{10,11... | collective-permute-start | bytes 1990664 | tf_op jit(solution)/shard_map/ppermute | solution.py:508
  6.4 17.3 %collective-permute-start.1 = (bf16[288,1152]{1,0:T(8,128)(2,1)}, bf16[288,1152]{1,0:T(8,128)(2,1)S(1)}, u32[]{:S(2)}, u32[]{:S(2)}) collective-permute-start(bf16[288,1152]{1,0:T(8,128)(2,1)} %get-tuple-element.27.refs_8_.refs_10_), channel_id=1, source_target_pairs={{0,4},{1,5},{2,6},{3,7},{4,0},{5,1},{6,2},{7,3},{8,10},{9,11},{10,... | collective-permute-start | bytes 1990664 | tf_op jit(solution)/shard_map/ppermute | solution.py:516
  15.4 8.3 %collective-permute-start.4 = (bf16[32,1152]{1,0:T(8,128)(2,1)S(1)}, bf16[32,1152]{1,0:T(8,128)(2,1)S(1)}, u32[]{:S(2)}, u32[]{:S(2)}) collective-permute-start(bf16[32,1152]{1,0:T(8,128)(2,1)S(1)} %constant_dynamic-slice_fusion.2), channel_id=1, source_target_pairs={{0,8},{8,0},{16,24},{24,16},{1,9},{9,1},{17,25},{25,17},{2,10},{10... | collective-permute-start | bytes 221192 | tf_op jit(solution)/shard_map/ppermute | solution.py:522
  17.0 8.0 %collective-permute-start.5 = (bf16[32,1152]{1,0:T(8,128)(2,1)S(1)}, bf16[32,1152]{1,0:T(8,128)(2,1)S(1)}, u32[]{:S(2)}, u32[]{:S(2)}) collective-permute-start(bf16[32,1152]{1,0:T(8,128)(2,1)S(1)} %constant_dynamic-slice_fusion.2), channel_id=1, source_target_pairs={{0,16},{8,24},{16,0},{24,8},{1,17},{9,25},{17,1},{25,9},{2,18},{10... | collective-permute-start | bytes 221192 | tf_op jit(solution)/shard_map/ppermute | solution.py:522
  19.6 6.3 %collective-permute-start.6 = (bf16[32,1152]{1,0:T(8,128)(2,1)S(1)}, bf16[32,1152]{1,0:T(8,128)(2,1)S(1)}, u32[]{:S(2)}, u32[]{:S(2)}) collective-permute-start(bf16[32,1152]{1,0:T(8,128)(2,1)S(1)} %constant_dynamic-slice_fusion.2), channel_id=1, source_target_pairs={{0,24},{8,16},{16,8},{24,0},{1,25},{9,17},{17,9},{25,1},{2,26},{10... | collective-permute-start | bytes 221192 | tf_op jit(solution)/shard_map/ppermute | solution.py:522
  25.9 1.5 %collective-permute-start.8 = (bf16[32,1152]{1,0:T(8,128)(2,1)S(1)}, bf16[32,1152]{1,0:T(8,128)(2,1)S(1)}, u32[]{:S(2)}, u32[]{:S(2)}) collective-permute-start(bf16[32,1152]{1,0:T(8,128)(2,1)S(1)} %collective-permute-done.5.refs_1_), channel_id=1, source_target_pairs={{0,1},{1,0},{2,3},{3,2},{4,5},{5,4},{6,7},{7,6},{8,9},{9,8},{10,11... | collective-permute-start | bytes 221192 | tf_op jit(solution)/shard_map/ppermute | solution.py:508
  26.4 2.4 %collective-permute-start.9 = (bf16[32,1152]{1,0:T(8,128)(2,1)S(1)}, bf16[32,1152]{1,0:T(8,128)(2,1)S(1)}, u32[]{:S(2)}, u32[]{:S(2)}) collective-permute-start(bf16[32,1152]{1,0:T(8,128)(2,1)S(1)} %collective-permute-done.6.refs_2_), channel_id=1, source_target_pairs={{0,1},{1,0},{2,3},{3,2},{4,5},{5,4},{6,7},{7,6},{8,9},{9,8},{10,11... | collective-permute-start | bytes 221192 | tf_op jit(solution)/shard_map/ppermute | solution.py:508
  26.4 17.6 %collective-permute-start.10 = (bf16[288,1152]{1,0:T(8,128)(2,1)}, bf16[288,1152]{1,0:T(8,128)(2,1)}, u32[]{:S(2)}, u32[]{:S(2)}) collective-permute-start(bf16[288,1152]{1,0:T(8,128)(2,1)} %collective-permute-done.refs_7_.refs_9_), channel_id=1, source_target_pairs={{0,4},{1,5},{2,6},{3,7},{4,0},{5,1},{6,2},{7,3},{8,10},{9,11},{10,... | collective-permute-start | bytes 1990664 | tf_op jit(solution)/shard_map/ppermute | solution.py:516
  26.9 18.4 %collective-permute-start.15 = (bf16[288,1152]{1,0:T(8,128)(2,1)}, bf16[288,1152]{1,0:T(8,128)(2,1)S(1)}, u32[]{:S(2)}, u32[]{:S(2)}) collective-permute-start(bf16[288,1152]{1,0:T(8,128)(2,1)} %collective-permute-done.refs_7_.refs_9_), channel_id=1, source_target_pairs={{0,1},{1,0},{2,3},{3,2},{4,5},{5,4},{6,7},{7,6},{8,9},{9,8},{10,11... | collective-permute-start | bytes 1990664 | tf_op jit(solution)/shard_map/ppermute | solution.py:508
  27.1 18.7 %collective-permute-start.16 = (bf16[288,1152]{1,0:T(8,128)(2,1)S(1)}, bf16[288,1152]{1,0:T(8,128)(2,1)S(1)}, u32[]{:S(2)}, u32[]{:S(2)}) collective-permute-start(bf16[288,1152]{1,0:T(8,128)(2,1)S(1)} %collective-permute-done.1.refs_9_.refs_11_), channel_id=1, source_target_pairs={{0,1},{1,0},{2,3},{3,2},{4,5},{5,4},{6,7},{7,6},{8,9},{9,8},{10,11... | collective-permute-start | bytes 1990664 | tf_op jit(solution)/shard_map/ppermute | solution.py:508
  27.4 18.5 %collective-permute-start.11 = (bf16[288,1152]{1,0:T(8,128)(2,1)}, bf16[288,1152]{1,0:T(8,128)(2,1)}, u32[]{:S(2)}, u32[]{:S(2)}) collective-permute-start(bf16[288,1152]{1,0:T(8,128)(2,1)} %collective-permute-done.refs_7_.refs_9_), channel_id=1, source_target_pairs={{0,8},{8,0},{16,24},{24,16},{1,9},{9,1},{17,25},{25,17},{2,10},{10... | collective-permute-start | bytes 1990664 | tf_op jit(solution)/shard_map/ppermute | solution.py:522
  29.4 17.0 %collective-permute-start.12 = (bf16[288,1152]{1,0:T(8,128)(2,1)S(1)}, bf16[288,1152]{1,0:T(8,128)(2,1)}, u32[]{:S(2)}, u32[]{:S(2)}) collective-permute-start(bf16[288,1152]{1,0:T(8,128)(2,1)S(1)} %collective-permute-done.1.refs_9_.refs_11_), channel_id=1, source_target_pairs={{0,2},{1,3},{2,0},{3,1},{4,6},{5,7},{6,4},{7,5},{8,12},{9,13},{10,... | collective-permute-start | bytes 1990664 | tf_op jit(solution)/shard_map/ppermute | solution.py:516
  44.0 9.4 %collective-permute-start.13 = (bf16[144,1152]{1,0:T(8,128)(2,1)S(1)}, bf16[144,1152]{1,0:T(8,128)(2,1)S(1)}, u32[]{:S(2)}, u32[]{:S(2)}) collective-permute-start(bf16[144,1152]{1,0:T(8,128)(2,1)S(1)} %slice.3), channel_id=1, source_target_pairs={{0,8},{8,0},{16,24},{24,16},{1,9},{9,1},{17,25},{25,17},{2,10},{10... | collective-permute-start | bytes 995336 | tf_op jit(solution)/shard_map/ppermute | solution.py:522
  45.3 9.5 %collective-permute-start.14 = (bf16[144,1152]{1,0:T(8,128)(2,1)}, bf16[144,1152]{1,0:T(8,128)(2,1)}, u32[]{:S(2)}, u32[]{:S(2)}) collective-permute-start(bf16[144,1152]{1,0:T(8,128)(2,1)} %refs_3_.1), channel_id=1, source_target_pairs={{0,2},{1,3},{2,0},{3,1},{4,6},{5,7},{6,4},{7,5},{8,12},{9,13},{10,... | collective-permute-start | bytes 995336 | tf_op jit(solution)/shard_map/ppermute | solution.py:516
  45.9 10.9 %collective-permute-start.17 = (bf16[288,1152]{1,0:T(8,128)(2,1)}, bf16[288,1152]{1,0:T(8,128)(2,1)}, u32[]{:S(2)}, u32[]{:S(2)}) collective-permute-start(bf16[288,1152]{1,0:T(8,128)(2,1)} %collective-permute-done.10.refs_10_.refs_12_), channel_id=1, source_target_pairs={{0,1},{1,0},{2,3},{3,2},{4,5},{5,4},{6,7},{7,6},{8,9},{9,8},{10,11... | collective-permute-start | bytes 1990664 | tf_op jit(solution)/shard_map/ppermute | solution.py:508
  45.9 10.9 %collective-permute-start.18 = (bf16[288,1152]{1,0:T(8,128)(2,1)}, bf16[288,1152]{1,0:T(8,128)(2,1)}, u32[]{:S(2)}, u32[]{:S(2)}) collective-permute-start(bf16[288,1152]{1,0:T(8,128)(2,1)} %collective-permute-done.11.refs_11_.refs_13_), channel_id=1, source_target_pairs={{0,1},{1,0},{2,3},{3,2},{4,5},{5,4},{6,7},{7,6},{8,9},{9,8},{10,11... | collective-permute-start | bytes 1990664 | tf_op jit(solution)/shard_map/ppermute | solution.py:508
  46.4 10.4 %collective-permute-start.19 = (bf16[288,1152]{1,0:T(8,128)(2,1)}, bf16[288,1152]{1,0:T(8,128)(2,1)}, u32[]{:S(2)}, u32[]{:S(2)}) collective-permute-start(bf16[288,1152]{1,0:T(8,128)(2,1)} %collective-permute-done.12.refs_12_.refs_14_), channel_id=1, source_target_pairs={{0,1},{1,0},{2,3},{3,2},{4,5},{5,4},{6,7},{7,6},{8,9},{9,8},{10,11... | collective-permute-start | bytes 1990664 | tf_op jit(solution)/shard_map/ppermute | solution.py:508
  53.4 2.0 %collective-permute-start.20 = (bf16[144,1152]{1,0:T(8,128)(2,1)S(1)}, bf16[144,1152]{1,0:T(8,128)(2,1)}, u32[]{:S(2)}, u32[]{:S(2)}) collective-permute-start(bf16[144,1152]{1,0:T(8,128)(2,1)S(1)} %collective-permute-done.13.refs_13_.refs_15_), channel_id=1, source_target_pairs={{0,1},{1,0},{2,3},{3,2},{4,5},{5,4},{6,7},{7,6},{8,9},{9,8},{10,11... | collective-permute-start | bytes 995336 | tf_op jit(solution)/shard_map/ppermute | solution.py:508
  54.8 2.0 %collective-permute-start.21 = (bf16[144,1152]{1,0:T(8,128)(2,1)}, bf16[144,1152]{1,0:T(8,128)(2,1)}, u32[]{:S(2)}, u32[]{:S(2)}) collective-permute-start(bf16[144,1152]{1,0:T(8,128)(2,1)} %collective-permute-done.14.refs_14_.refs_16_), channel_id=1, source_target_pairs={{0,1},{1,0},{2,3},{3,2},{4,5},{5,4},{6,7},{7,6},{8,9},{9,8},{10,11... | collective-permute-start | bytes 995336 | tf_op jit(solution)/shard_map/ppermute | solution.py:508
  72.5 1.6 %collective-permute-start.22 = (f32[32,1152]{1,0:T(8,128)}, f32[32,1152]{1,0:T(8,128)S(1)}, u32[]{:S(2)}, u32[]{:S(2)}) collective-permute-start(f32[32,1152]{1,0:T(8,128)} %get-tuple-element.37), channel_id=1, source_target_pairs={{0,1},{1,0},{2,3},{3,2},{4,5},{5,4},{6,7},{7,6},{8,9},{9,8},{10,11... | collective-permute-start | bytes 442376 | tf_op jit(solution)/shard_map/ppermute | solution.py:508
  75.1 9.2 %collective-permute-start.23 = (bf16[32,1152]{1,0:T(8,128)(2,1)S(1)}, bf16[32,1152]{1,0:T(8,128)(2,1)S(1)}, u32[]{:S(2)}, u32[]{:S(2)}) collective-permute-start(bf16[32,1152]{1,0:T(8,128)(2,1)S(1)} %add_convert_fusion.1), channel_id=1, source_target_pairs={{0,2},{1,3},{2,0},{3,1},{4,6},{5,7},{6,4},{7,5},{8,10},{9,11},{10,... | collective-permute-start | bytes 221192 | tf_op jit(solution)/shard_map/ppermute | solution.py:508
  75.7 8.6 %collective-permute-start.24 = (bf16[32,1152]{1,0:T(8,128)(2,1)S(1)}, bf16[32,1152]{1,0:T(8,128)(2,1)S(1)}, u32[]{:S(2)}, u32[]{:S(2)}) collective-permute-start(bf16[32,1152]{1,0:T(8,128)(2,1)S(1)} %add_convert_fusion.1), channel_id=1, source_target_pairs={{0,4},{1,5},{2,6},{3,7},{4,0},{5,1},{6,2},{7,3},{8,12},{9,13},{10,... | collective-permute-start | bytes 221192 | tf_op jit(solution)/shard_map/ppermute | solution.py:508
  76.2 8.1 %collective-permute-start.25 = (bf16[32,1152]{1,0:T(8,128)(2,1)S(1)}, bf16[32,1152]{1,0:T(8,128)(2,1)S(1)}, u32[]{:S(2)}, u32[]{:S(2)}) collective-permute-start(bf16[32,1152]{1,0:T(8,128)(2,1)S(1)} %add_convert_fusion.1), channel_id=1, source_target_pairs={{0,6},{1,7},{2,4},{3,5},{4,2},{5,3},{6,0},{7,1},{8,14},{9,15},{10,... | collective-permute-start | bytes 221192 | tf_op jit(solution)/shard_map/ppermute | solution.py:508
  84.3 6.3 %collective-permute-start.26 = (bf16[32,1152]{1,0:T(8,128)(2,1)S(1)}, bf16[32,1152]{1,0:T(8,128)(2,1)S(1)}, u32[]{:S(2)}, u32[]{:S(2)}) collective-permute-start(bf16[32,1152]{1,0:T(8,128)(2,1)S(1)} %add_convert_fusion.refs_0_), channel_id=1, source_target_pairs={{0,8},{8,0},{16,24},{24,16},{1,9},{9,1},{17,25},{25,17},{2,10},{10... | collective-permute-start | bytes 221192 | tf_op jit(solution)/shard_map/ppermute | solution.py:522
  85.1 7.3 %collective-permute-start.27 = (bf16[32,1152]{1,0:T(8,128)(2,1)S(1)}, bf16[32,1152]{1,0:T(8,128)(2,1)S(1)}, u32[]{:S(2)}, u32[]{:S(2)}) collective-permute-start(bf16[32,1152]{1,0:T(8,128)(2,1)S(1)} %add_convert_fusion.refs_0_), channel_id=1, source_target_pairs={{0,16},{8,24},{16,0},{24,8},{1,17},{9,25},{17,1},{25,9},{2,18},{10... | collective-permute-start | bytes 221192 | tf_op jit(solution)/shard_map/ppermute | solution.py:522
  87.4 6.3 %collective-permute-start.28 = (bf16[32,1152]{1,0:T(8,128)(2,1)S(1)}, bf16[32,1152]{1,0:T(8,128)(2,1)S(1)}, u32[]{:S(2)}, u32[]{:S(2)}) collective-permute-start(bf16[32,1152]{1,0:T(8,128)(2,1)S(1)} %add_convert_fusion.refs_0_), channel_id=1, source_target_pairs={{0,24},{8,16},{16,8},{24,0},{1,25},{9,17},{17,9},{25,1},{2,26},{10... | collective-permute-start | bytes 221192 | tf_op jit(solution)/shard_map/ppermute | solution.py:522
  90.6 8.7 %collective-permute-start.29 = (bf16[32,1152]{1,0:T(8,128)(2,1)S(1)}, bf16[32,1152]{1,0:T(8,128)(2,1)S(1)}, u32[]{:S(2)}, u32[]{:S(2)}) collective-permute-start(bf16[32,1152]{1,0:T(8,128)(2,1)S(1)} %add_convert_fusion.refs_0_), channel_id=1, source_target_pairs={{0,1},{1,0},{2,3},{3,2},{4,5},{5,4},{6,7},{7,6},{8,9},{9,8},{10,11... | collective-permute-start | bytes 221192 | tf_op jit(solution)/shard_map/ppermute | solution.py:508
  90.7 8.7 %collective-permute-start.30 = (bf16[32,1152]{1,0:T(8,128)(2,1)S(1)}, bf16[32,1152]{1,0:T(8,128)(2,1)S(1)}, u32[]{:S(2)}, u32[]{:S(2)}) collective-permute-start(bf16[32,1152]{1,0:T(8,128)(2,1)S(1)} %collective-permute-done.26.refs_1_), channel_id=1, source_target_pairs={{0,1},{1,0},{2,3},{3,2},{4,5},{5,4},{6,7},{7,6},{8,9},{9,8},{10,11... | collective-permute-start | bytes 221192 | tf_op jit(solution)/shard_map/ppermute | solution.py:508
  92.4 7.0 %collective-permute-start.31 = (bf16[32,1152]{1,0:T(8,128)(2,1)S(1)}, bf16[32,1152]{1,0:T(8,128)(2,1)S(1)}, u32[]{:S(2)}, u32[]{:S(2)}) collective-permute-start(bf16[32,1152]{1,0:T(8,128)(2,1)S(1)} %collective-permute-done.27.refs_2_), channel_id=1, source_target_pairs={{0,1},{1,0},{2,3},{3,2},{4,5},{5,4},{6,7},{7,6},{8,9},{9,8},{10,11... | collective-permute-start | bytes 221192 | tf_op jit(solution)/shard_map/ppermute | solution.py:508
  93.6 5.7 %collective-permute-start.32 = (bf16[32,1152]{1,0:T(8,128)(2,1)S(1)}, bf16[32,1152]{1,0:T(8,128)(2,1)S(1)}, u32[]{:S(2)}, u32[]{:S(2)}) collective-permute-start(bf16[32,1152]{1,0:T(8,128)(2,1)S(1)} %collective-permute-done.28.refs_3_), channel_id=1, source_target_pairs={{0,1},{1,0},{2,3},{3,2},{4,5},{5,4},{6,7},{7,6},{8,9},{9,8},{10,11... | collective-permute-start | bytes 221192 | tf_op jit(solution)/shard_map/ppermute | solution.py:508
  (24 other events, 184.4 us)

commit v2 on v1

--- a/solution.py
+++ b/solution.py
@@ -13,7 +13,6 @@
 VMEM = pl.BlockSpec(memory_space=pltpu.VMEM)
 SMEM = pl.BlockSpec(memory_space=pltpu.SMEM)
 ANY = pl.BlockSpec(memory_space=pl.ANY)
-HBM = pl.BlockSpec(memory_space=pltpu.HBM)
 
 
 def vmem(mebibytes):
@@ -87,30 +86,11 @@
     return [2 * (chip ^ step) + other for other in (core, 1 - core) for step in steps]
 
 
-def load_blocks(blocks, offsets, whole, places, sem):
+def load_weight(name, layout, arrays, place_ref, chips, whole):
+    scheme, blocks = layout[name]
     rows = whole.shape[0] // len(blocks)
-    copies = [
-        pltpu.make_async_copy(
-            block.at[pl.ds(offset, rows)],
-            whole.at[pl.ds(pl.multiple_of(place * rows, 16), rows)],
-            sem.at[i],
-        )
-        for i, (block, offset, place) in enumerate(zip(blocks, offsets, places))
-    ]
-    for copy in copies:
-        copy.start()
-    return copies
-
-
-def load_weight(name, layout, arrays, place_ref, chips, whole, sem):
-    scheme, blocks = layout[name]
-    return load_blocks(
-        [arrays[array] for array, _ in blocks],
-        [offset for _, offset in blocks],
-        whole,
-        block_places(place_ref, scheme, chips),
-        sem,
-    )
+    for (array, offset), place in zip(blocks, block_places(place_ref, scheme, chips)):
+        whole[pl.ds(pl.multiple_of(place * rows, 16), rows)] = arrays[array][offset : offset + rows]
 
 
 def project(left_arg, right_arg):
@@ -137,6 +117,43 @@
         out_ref[pl.ds(pl.multiple_of(first + (1 - core) * half, 16), half)] = far[plane][...]
 
 
+def wait_all(copies):
+    for copy in copies:
+        copy.wait()
+
+
+def encode_kernel(chips, planes, layout, place_ref, phrase_ref, *refs):
+    others = planes - 1
+    mine, far = refs[:others], refs[others : 2 * others]
+    arrays = refs[2 * others : 2 * others + layout["arrays"]]
+    (
+        encoded_out,
+        slope_out,
+        own_hidden_out,
+        own_phrase_out,
+        first_weight,
+        second_weight,
+        phrases,
+    ) = refs[2 * others + layout["arrays"] :]
+    own_rows = phrase_ref.shape[0]
+    phrases[:own_rows] = phrase_ref[...]
+    join_halves(phrases, place_ref[1], own_rows, mine, far)
+    load_weight("first", layout, arrays, place_ref, chips, first_weight)
+    load_weight("second", layout, arrays, place_ref, chips, second_weight)
+    columns = own_phrase_out.shape[1]
+    selected = lax.broadcasted_iota(jnp.int32, (phrases.shape[1], columns), 0)
+    selected -= (2 * place_ref[0] + place_ref[1]) * columns
+    select = selected == lax.broadcasted_iota(jnp.int32, selected.shape, 1)
+    select = jnp.where(select, 1.0, 0.0).astype(jnp.bfloat16)
+    own_phrase_out[...] = project(phrases[...], select).astype(jnp.bfloat16)
+    pre_act = project(phrases[...], first_weight[...])
+    sigmoid = jax.nn.sigmoid(pre_act)
+    hidden = (pre_act * sigmoid).astype(jnp.bfloat16)
+    slope_out[...] = sigmoid * (1.0 + pre_act * (1.0 - sigmoid))
+    own_hidden_out[...] = project(hidden, select).astype(jnp.bfloat16)
+    encoded_out[...] = project(hidden[:own_rows], second_weight[...]).astype(jnp.bfloat16)
+
+
 def head_parts(slots):
     return [slice(head * slots, (head + 1) * slots) for head in range(GROUP)]
 
@@ -152,78 +169,28 @@
     )
 
 
-def attend_kernel(chips, planes, images, layout, place_ref, phrase_ref, *refs):
-    others = planes - 1
-    mine, far = refs[:others], refs[others : 2 * others]
-    arrays = refs[2 * others : 2 * others + layout["arrays"]]
+def attend_kernel(chips, images, layout, place_ref, encoded_ref, *refs):
+    arrays = refs[: layout["arrays"]]
     (
-        query_ref,
-        grad_ref,
+        query,
+        grad,
         bias_ref,
         key_out,
         score_out,
         mine_out,
         other_out,
-        slope_out,
-        hidden_out,
-        phrase_out,
-        first_weight,
-        second_weight,
         key_weight,
         value_weight,
-        query,
-        grad,
-        slope,
-        hidden,
-        all_phrases,
-        all_scores,
         value_rows,
         key_sum,
         value_sum,
         total,
-        first_sem,
-        second_sem,
-        key_sem,
-        value_sem,
-        row_sem,
-        out_sem,
-    ) = refs[2 * others + layout["arrays"] :]
-    first_copies = load_weight("first", layout, arrays, place_ref, chips, first_weight, first_sem)
-    second_copies = load_weight(
-        "second", layout, arrays, place_ref, chips, second_weight, second_sem
-    )
-    key_copies = load_weight("key", layout, arrays, place_ref, chips, key_weight, key_sem)
-    value_copies = load_weight("value", layout, arrays, place_ref, chips, value_weight, value_sem)
-    query_copy = pltpu.make_async_copy(query_ref, query, row_sem.at[0])
-    query_copy.start()
-    grad_copy = pltpu.make_async_copy(grad_ref, grad, row_sem.at[1])
-    grad_copy.start()
-    own_rows = phrase_ref.shape[0]
-    all_phrases[:own_rows] = phrase_ref[...]
-    join_halves(all_phrases, place_ref[1], own_rows, mine, far)
-    out_copies = [pltpu.make_async_copy(all_phrases, phrase_out, out_sem.at[0])]
-    out_copies[0].start()
-    for copy in first_copies:
-        copy.wait()
-    pre_act = project(all_phrases[...], first_weight[...])
-    sigmoid = jax.nn.sigmoid(pre_act)
-    hidden[...] = (pre_act * sigmoid).astype(jnp.bfloat16)
-    slope[...] = sigmoid * (1.0 + pre_act * (1.0 - sigmoid))
-    out_copies.append(pltpu.make_async_copy(hidden, hidden_out, out_sem.at[1]))
-    out_copies.append(pltpu.make_async_copy(slope, slope_out, out_sem.at[2]))
-    out_copies[1].start()
-    out_copies[2].start()
-    for copy in second_copies:
-        copy.wait()
-    encoded = project(hidden[:own_rows], second_weight[...]).astype(jnp.bfloat16)
-    for copy in key_copies:
-        copy.wait()
-    key_out[...] = project(encoded, key_weight[...]).astype(jnp.bfloat16)
-    for copy in value_copies:
-        copy.wait()
-    value_rows[...] = project(encoded, value_weight[...]).astype(jnp.bfloat16)
-    query_copy.wait()
-    grad_copy.wait()
+    ) = refs[layout["arrays"] :]
+    own_rows = encoded_ref.shape[0]
+    load_weight("key", layout, arrays, place_ref, chips, key_weight)
+    load_weight("value", layout, arrays, place_ref, chips, value_weight)
+    key_out[...] = project(encoded_ref[...], key_weight[...]).astype(jnp.bfloat16)
+    value_rows[...] = project(encoded_ref[...], value_weight[...]).astype(jnp.bfloat16)
 
     slots = own_rows // images
     features = query.shape[1]
@@ -256,17 +223,13 @@
                 score_grad.append((probs * (upstream - inner) * scale).astype(jnp.bfloat16))
             probs_low = jnp.concatenate(probs_low, axis=0)
             score_grad = jnp.concatenate(score_grad, axis=0)
-            all_scores[image, pl.ds(group * GROUP * slots, GROUP * slots)] = score_grad
+            score_out[image, pl.ds(group * GROUP * slots, GROUP * slots)] = score_grad
             key_sum[rows, columns] += own_head_sum(
                 project(score_grad, queries), group, head_size, low
             )
             value_sum[rows, columns] += own_head_sum(
                 project(probs_low, grads), group, head_size, low
             )
-        out_copies.append(
-            pltpu.make_async_copy(all_scores.at[image], score_out.at[image], out_sem.at[3 + image])
-        )
-        out_copies[-1].start()
     total[...] = split_times_transposed(key_sum[...], key_weight[...]) + split_times_transposed(
         value_sum[...], value_weight[...]
     )
@@ -274,75 +237,66 @@
     half = mine_out.shape[0]
     mine_out[...] = total[pl.ds(pl.multiple_of(core * half, 8), half)]
     other_out[...] = total[pl.ds(pl.multiple_of((1 - core) * half, 8), half)]
-    for copy in out_copies:
-        copy.wait()
-
-
-def latent_kernel(score_ref, key_ref, weight_ref, out_ref, query_grad):
-    features = weight_ref.shape[1]
+
+
+def latent_kernel(image, score_ref, key_ref, weight, out_ref, result, out_sem):
+    slots, features = key_ref.shape[0] // score_ref.shape[0], weight.shape[0]
+    tokens = score_ref.shape[2]
     head_size = features // H
-    slots = key_ref.shape[0]
-
-    @pl.when(pl.program_id(0) == 0)
-    def _():
-        parts = []
-        for group in range(H // GROUP):
-            low, high = window(group, head_size)
-            keys = block_diagonal(key_ref[:, low:high], group, head_size, low)
-            score_grad = score_ref[0, group * GROUP * slots : (group + 1) * GROUP * slots]
-            part = transposed_times(score_grad, keys)
-            if low:
-                part = jnp.concatenate([jnp.zeros((part.shape[0], low), jnp.float32), part], axis=1)
-            if high < features:
-                part = jnp.concatenate(
-                    [part, jnp.zeros((part.shape[0], features - high), jnp.float32)], axis=1
-                )
-            parts.append(part)
-        query_grad[...] = functools.reduce(jnp.add, parts).astype(jnp.bfloat16)
-
-    out_ref[...] = times_transposed(query_grad[...], weight_ref[...]).astype(jnp.bfloat16)
-
-
-def weight_grad_kernel(chips, planes, layout, place_ref, *refs):
+    parts = []
+    for group in range(H // GROUP):
+        low, high = window(group, head_size)
+        rows = key_ref[image * slots : (image + 1) * slots, low:high]
+        keys = block_diagonal(rows, group, head_size, low)
+        score_grad = score_ref[image, group * GROUP * slots : (group + 1) * GROUP * slots]
+        part = transposed_times(score_grad, keys)
+        if low:
+            part = jnp.concatenate([jnp.zeros((part.shape[0], low), jnp.float32), part], axis=1)
+        if high < features:
+            part = jnp.concatenate(
+                [part, jnp.zeros((part.shape[0], features - high), jnp.float32)], axis=1
+            )
+        parts.append(part)
+    query_grad = functools.reduce(jnp.add, parts).astype(jnp.bfloat16)
+    tile = tokens // out_sem.shape[0]
+    copies = []
+    for step in range(out_sem.shape[0]):
+        rows = slice(step * tile, (step + 1) * tile)
+        result[rows] = times_transposed(query_grad[rows], weight[...]).astype(jnp.bfloat16)
+        copies.append(
+            pltpu.make_async_copy(
+                result.at[rows], out_ref.at[pl.ds(image * tokens + step * tile, tile)], out_sem.at[step]
+            )
+        )
+        copies[-1].start()
+    wait_all(copies)
+
+
+def weight_grad_kernel(planes, place_ref, *refs):
     mine, far = refs[:planes], refs[planes : 2 * planes]
-    arrays = refs[2 * planes : 2 * planes + layout["arrays"]]
     (
+        first_weight,
+        second_weight,
         slope_ref,
         hidden_ref,
         phrase_ref,
         second_out,
         first_out,
         phrase_out,
-        first_weight,
-        second_weight,
         encoded_grad,
-        slope,
         second_grad,
         first_grad,
-        first_sem,
-        second_sem,
-        row_sem,
-    ) = refs[2 * planes + layout["arrays"] :]
-    second_copies = load_weight(
-        "second", layout, arrays, place_ref, chips, second_weight, second_sem
-    )
-    slope_copy = pltpu.make_async_copy(slope_ref, slope, row_sem.at[0])
-    slope_copy.start()
-    first_copies = load_weight("first", layout, arrays, place_ref, chips, first_weight, first_sem)
+        out_sem,
+    ) = refs[2 * planes :]
     join_halves(encoded_grad, place_ref[1], 0, mine, far)
     second_grad[...] = transposed_times(hidden_ref[...], encoded_grad[...])
-    second_copy = pltpu.make_async_copy(second_grad, second_out, row_sem.at[1])
+    second_copy = pltpu.make_async_copy(second_grad, second_out, out_sem.at[0])
     second_copy.start()
-    for copy in second_copies:
-        copy.wait()
     hidden_grad = times_transposed(encoded_grad[...], second_weight[...])
-    slope_copy.wait()
-    act_grad = (hidden_grad * slope[...]).astype(jnp.bfloat16)
+    act_grad = (hidden_grad * slope_ref[...]).astype(jnp.bfloat16)
     first_grad[...] = transposed_times(phrase_ref[...], act_grad)
-    first_copy = pltpu.make_async_copy(first_grad, first_out, row_sem.at[2])
+    first_copy = pltpu.make_async_copy(first_grad, first_out, out_sem.at[1])
     first_copy.start()
-    for copy in first_copies:
-        copy.wait()
     phrase_out[...] = times_transposed(
         act_grad[: phrase_out.shape[0]], first_weight[...]
     ).astype(jnp.bfloat16)
@@ -524,6 +478,9 @@
     def plane_peers(array):
         return [plane_swap(array, k) for k in range(1, planes)]
 
+    def after_all(parts, *others):
+        return lax.optimization_barrier((*parts, *others))[: len(parts)]
+
     def after(array, *others):
         return lax.optimization_barrier((array, *others))[0]
 
@@ -543,9 +500,7 @@
     phrase_rows = phrases.reshape(rows, features)
     bias = visible_bias(region_first, region_last, phrase_counts, shard * tokens, tokens)
     weight_shape = pltpu.VMEM((features, features), jnp.bfloat16)
-    row_shape = pltpu.VMEM((images * tokens, features), jnp.bfloat16)
     sum_shape = pltpu.VMEM((rows, features), jnp.float32)
-    block_sems = pltpu.SemaphoreType.DMA((2 * chips,))
     def join(parts, lengths, whole_rows):
         return pl.pallas_call(
             join_kernel,
@@ -561,30 +516,30 @@
     if chips == 4:
         encoder_near = swap_by_plane(encoder, 1, 2)
         projector_near = swap_by_plane(projector, 2, 1)
-        queries = project_queries(latents)
         encoder_own, projector_own = swap(encoder, 1), swap(projector, 1)
         own_half = lax.dynamic_slice_in_dim(
-            after(phrase_rows, queries, encoder_own, projector_own, bias), core * half, half, 0
+            after(phrase_rows, encoder_own, projector_own), core * half, half, 0
         )
+        queries = project_queries(after(latents, encoder_own, projector_own))
         plane_phrases = plane_peers(own_half)
-        encoder_next, projector_next, plane_phrases, value_next = lax.optimization_barrier(
-            (encoder_near, projector_near, plane_phrases, value_weight)
+        far_phrases = [swap(part, 1) for part in after_all(plane_phrases, queries)]
+        encoder_next, projector_next, value_next, far_phrases, queries, bias, place = (
+            lax.optimization_barrier(
+                (encoder_near, projector_near, value_weight, far_phrases, queries, bias, place)
+            )
         )
+        value_third = swap_by_plane(value_next, 1, 2)
         encoder_far = swap_by_plane(encoder_next, 2, 1)
         encoder_third = plane_swap(encoder_next, 1)
+        pairs = [swap(encoder_next, 1), swap(projector_next, 1)]
+        projector_next = after(projector_next, *pairs)
         projector_far = swap_by_plane(projector_next, 1, 2)
-        value_third = swap_by_plane(value_next, 1, 2)
         key_third = plane_swap(projector_next[:shard_rows], 1)
-        far_phrases = [swap(part, 1) for part in plane_phrases]
         arrays = [encoder, encoder_near, projector, projector_near]
         arrays += [encoder_far, encoder_third, projector_far, key_third, value_third]
-        swapped = [encoder_own, swap(encoder_next, 1), projector_own, swap(projector_next, 1)]
-        encoder_far = after(encoder_far, *swapped, *far_phrases)
-        arrays += swapped
-        arrays += [
-            swap(block, 1)
-            for block in (encoder_far, encoder_third, projector_far, key_third, value_third)
-        ]
+        arrays += [encoder_own, pairs[0], projector_own, pairs[1]]
+        arrays += [swap(block, 1) for block in arrays[4:9]]
+        arrays = list(lax.optimization_barrier(tuple(arrays)))
         layout = {
             "first": (0, [(0, 0), (1, 0), (5, 0), (4, 0)]),
             "second": (0, [(i, shard_rows) for i in (0, 1, 5, 4)]),
@@ -607,73 +562,80 @@
                 ("value", chips, shard_rows),
             )
         }
-    near_count = len(arrays) // 2
+    near_count = chips == 4 and 9 or len(arrays) // 2
     for name, (scheme, blocks) in layout.items():
         layout[name] = (scheme, blocks + [(near_count + i, offset) for i, offset in blocks])
-    layout["arrays"] = len(arrays)
+
+    def weights(*names):
+        used = sorted({i for name in names for i, _ in layout[name][1]})
+        own_layout = {
+            name: (layout[name][0], [(used.index(i), offset) for i, offset in layout[name][1]])
+            for name in names
+        }
+        return [arrays[i] for i in used], {**own_layout, "arrays": len(used)}
+
+    all_rows = planes * rows
+    encoder_arrays, encoder_layout = weights("first", "second")
+    encoded, slope, own_hidden, own_phrases, whole_first, whole_second = pl.pallas_call(
+        functools.partial(encode_kernel, chips, planes, encoder_layout),
+        out_shape=[
+            shape((rows, features), jnp.bfloat16),
+            shape((all_rows, features), jnp.float32),
+            shape((all_rows, shard_rows), jnp.bfloat16),
+            shape((all_rows, shard_rows), jnp.bfloat16),
+            shape((features, features), jnp.bfloat16),
+            shape((features, features), jnp.bfloat16),
+        ],
+        in_specs=[SMEM] + [VMEM] * (2 * planes - 1 + len(encoder_arrays)),
+        out_specs=[VMEM] * 6,
+        scratch_shapes=[pltpu.VMEM((all_rows, features), jnp.bfloat16)],
+        compiler_params=vmem(18),
+        cost_estimate=pl.CostEstimate(
+            flops=2 * 10**9, bytes_accessed=8 * 10**6, transcendentals=10**5
+        ),
+        name="encode",
+    )(place, phrase_rows, *plane_phrases, *far_phrases, *encoder_arrays)
     grads = out_grad.reshape(images * tokens, features)
-
-    all_rows = planes * rows
-    key_rows, score_grad, grad_mine, grad_other, slope, all_hidden, all_phrases = pl.pallas_call(
-        functools.partial(attend_kernel, chips, planes, images, layout),
+    projector_arrays, projector_layout = weights("key", "value")
+    key_rows, score_grad, grad_mine, grad_other = pl.pallas_call(
+        functools.partial(attend_kernel, chips, images, projector_layout),
         out_shape=[
             shape((rows, features), jnp.bfloat16),
             shape((images, H * slots, tokens), jnp.bfloat16),
             shape((half, features), jnp.float32),
             shape((half, features), jnp.float32),
-            shape((all_rows, features), jnp.float32),
-            shape((all_rows, features), jnp.bfloat16),
-            shape((all_rows, features), jnp.bfloat16),
         ],
-        in_specs=[SMEM] + [VMEM] * (2 * planes - 1) + [HBM] * len(arrays) + [ANY] * 2 + [VMEM],
-        out_specs=[VMEM, ANY, VMEM, VMEM, ANY, ANY, ANY],
+        in_specs=[SMEM] + [VMEM] * (len(projector_arrays) + 4),
+        out_specs=[VMEM] * 4,
         scratch_shapes=[
             weight_shape,
             weight_shape,
-            weight_shape,
-            weight_shape,
-            row_shape,
-            row_shape,
-            pltpu.VMEM((all_rows, features), jnp.float32),
-            pltpu.VMEM((all_rows, features), jnp.bfloat16),
-            pltpu.VMEM((all_rows, features), jnp.bfloat16),
-            pltpu.VMEM((images, H * slots, tokens), jnp.bfloat16),
             pltpu.VMEM((rows, features), jnp.bfloat16),
             sum_shape,
             sum_shape,
             sum_shape,
-            block_sems,
-            block_sems,
-            block_sems,
-            block_sems,
-            pltpu.SemaphoreType.DMA((2,)),
-            pltpu.SemaphoreType.DMA((3 + images,)),
         ],
-        compiler_params=vmem(60),
+        compiler_params=vmem(28),
         cost_estimate=pl.CostEstimate(
-            flops=10**10, bytes_accessed=18 * 10**6, transcendentals=10**6
+            flops=10**10, bytes_accessed=12 * 10**6, transcendentals=10**6
         ),
         name="attend",
-    )(place, phrase_rows, *plane_phrases, *far_phrases, *arrays, queries, grads, bias)
-    steps = 3 if features % 384 == 0 else 1
-    tile = features // steps
+    )(place, encoded, *projector_arrays, queries, grads, bias)
 
     def latent_part(image, scores_in, whole=None):
         given = [] if whole is None else [whole]
+        kernel = functools.partial(latent_kernel, image)
         return pl.pallas_call(
-            latent_kernel if whole is None else lambda _, *refs: latent_kernel(*refs),
+            kernel if whole is None else lambda _, *refs: kernel(*refs),
             out_shape=shape((images * tokens, features), jnp.bfloat16),
-            grid=(steps,),
-            in_specs=[ANY] * len(given)
-            + [
-                pl.BlockSpec((1, H * slots, tokens), lambda t: (image, 0, 0)),
-                pl.BlockSpec((slots, features), lambda t: (image, 0)),
-                pl.BlockSpec((tile, features), lambda t: (t, 0)),
+            in_specs=[ANY] * len(given) + [VMEM] * 3,
+            out_specs=ANY,
+            scratch_shapes=[
+                pltpu.VMEM((tokens, features), jnp.bfloat16),
+                pltpu.SemaphoreType.DMA((2,)),
             ],
-            out_specs=pl.BlockSpec((tokens, tile), lambda t: (image, t)),
-            scratch_shapes=[pltpu.VMEM((tokens, features), jnp.bfloat16)],
             input_output_aliases={0: 0} if given else {},
-            compiler_params=vmem(60),
+            compiler_params=vmem(12),
             cost_estimate=pl.CostEstimate(
                 flops=3 * 10**9, bytes_accessed=4 * 10**6, transcendentals=0
             ),
@@ -684,42 +646,37 @@
     grad_own = total_of([grad_pair] + chip_peers(grad_pair)).astype(jnp.bfloat16)
     latent_grad = latent_part(0, score_grad)
     grad_own, latent_grad = lax.optimization_barrier((grad_own, latent_grad))
-    own_hidden = lax.dynamic_slice_in_dim(all_hidden, shard * shard_rows, shard_rows, 1)
-    all_own_phrases = lax.dynamic_slice_in_dim(all_phrases, shard * shard_rows, shard_rows, 1)
     for image in range(1, images):
         latent_grad = latent_part(image, score_grad, latent_grad)
     grad_mines = [grad_own] + plane_peers(grad_own)
-    grad_fars = [swap(part, 1) for part in grad_mines]
+    grad_fars = [swap(grad_own, 1)]
+    grad_fars += [swap(part, 1) for part in after_all(grad_mines[1:], latent_grad)]
     second_grad, first_grad, phrase_grad = pl.pallas_call(
-        functools.partial(weight_grad_kernel, chips, planes, layout),
+        functools.partial(weight_grad_kernel, planes),
         out_shape=[
             shape((shard_rows, features), jnp.float32),
             shape((shard_rows, features), jnp.float32),
             shape((rows, features), jnp.bfloat16),
         ],
-        in_specs=[SMEM] + [VMEM] * (2 * planes) + [ANY] * (len(arrays) + 1) + [VMEM] * 2,
+        in_specs=[SMEM] + [VMEM] * (2 * planes + 5),
         out_specs=[ANY, ANY, VMEM],
         scratch_shapes=[
-            weight_shape,
-            weight_shape,
             pltpu.VMEM((all_rows, features), jnp.bfloat16),
-            pltpu.VMEM((all_rows, features), jnp.float32),
             pltpu.VMEM((shard_rows, features), jnp.float32),
             pltpu.VMEM((shard_rows, features), jnp.float32),
-            block_sems,
-            block_sems,
-            pltpu.SemaphoreType.DMA((3,)),
+            pltpu.SemaphoreType.DMA((2,)),
         ],
-        compiler_params=vmem(60),
+        compiler_params=vmem(20),
         name="weight_grads",
     )(
         place,
         *grad_mines,
         *grad_fars,
-        *arrays,
+        whole_first,
+        whole_second,
         slope,
         own_hidden,
-        all_own_phrases,
+        own_phrases,
     )
     return (
         latent_grad.reshape(images, tokens, features),

time: 108 us -> 90.4 us (0.84)
  Pallas kernels: 37 us -> 24.9 us
  waiting for transfers between devices: 32.5 us -> 29.8 us
  local copies, waits for them, and re-layouts: 3.47 us -> 0.96 us
  starting transfers between devices: 24.6 us -> 26.1 us
    pallas_call x4 -> x5, Pallas kernels: 34.5 us -> 22.4 us  [the longest x1 8.25 us: tiled(): pl.pallas_call(functools.partial(attend_kernel, chips, images, projector_...]
    ppermute x5, waiting for transfers between devices: 18.3 us -> 10.6 us  [swap_by_plane(): return lax.ppermute(array, ('dp', 'seq'), pairs)]
    ppermute x8, waiting for transfers between devices: 11.4 us -> 14.2 us  [plane_swap(): return lax.ppermute(array, 'dp', [(i, i ^ distance) for i in range(planes)])]
    ppermute x20, waiting for transfers between devices: 2.83 us -> 4.94 us  [swap(): lax.ppermute(array, 'seq', [(i, i ^ distance) for i in range(shards)])]
    unnamed x46 -> x14, local copies, waits for them, and re-layouts: 1.57 us -> 0.04 us
  transfers between devices with their start and end apart: 33 -> 33, of which waited for: 11 -> 16; matrix products, arithmetic and copies ran while one was open for 9% -> 9% of each run, Pallas kernels for 10% -> 7%
where the time goes in v2:
time: 90.4 us; the launch traced here: 90.2 us
  waiting for transfers between devices  29.8 us (33%)
  starting transfers between devices  26.1 us (29%)
  Pallas kernels  24.9 us (28%)
  matrix products  5.73 us (6%)
  other arithmetic  1.67 us (2%)
  between operations  1.05 us (1%)
  local copies, waits for them, and re-layouts  0.96 us (1%)
    ppermute x8, waiting for transfers between devices, plane_swap(): return lax.ppermute(array, 'dp', [(i, i ^ distance) for i in range(planes)])  14.2 us
    ppermute x8, starting transfers between devices, plane_swap(): return lax.ppermute(array, 'dp', [(i, i ^ distance) for i in range(planes)])  12.5 us
    ppermute x5, waiting for transfers between devices, swap_by_plane(): return lax.ppermute(array, ('dp', 'seq'), pairs)  10.6 us
    pallas_call x1, Pallas kernels, tiled(): pl.pallas_call(functools.partial(attend_kernel, chips, images, projector_...  8.25 us
    ppermute x5, starting transfers between devices, swap_by_plane(): return lax.ppermute(array, ('dp', 'seq'), pairs)  6.99 us
    ppermute x20, starting transfers between devices, swap(): lax.ppermute(array, 'seq', [(i, i ^ distance) for i in range(shards)])  6.64 us
    pallas_call x2, Pallas kernels, latent_part(): pl.pallas_call(kernel if whole is None else lambda _, *refs: kernel(*refs...  6.55 us
    dot_general x1, matrix products, project_queries(): jnp.dot(tokens_in.reshape(images * tokens, features), query_weight, prefe...  5.73 us
  transfers between devices with their start and end apart: 33, of which 16 were waited for; matrix products, arithmetic and copies ran while one was open for 9% of the time, Pallas kernels for 7%

profile of v2, /device:TPU:0, one launch (start us, length us, event | category | flops | bytes accessed | tf_op | source)
XLA Modules:
  0.0 90.2 jit_solution(3137449874615355200)
XLA Ops:
  0.6 2.5 %join.1 = (bf16[288,1152]{1,0:T(8,128)(2,1)}, bf16[288,1152]{1,0:T(8,128)(2,1)}) custom-call(bf16[144,1152]{1,0:T(8,128)(2,1)} %refs_0_.1, bf16[144,1152]{1,0:T(8,128)(2,1)} %refs_1_.1, bf16[144,1152]{1,0:T(8,128)(2,1)} %refs_2_.2, bf16[144,1152]{1,0:T(8,128)(2,1)} %refs_3_.1), custom_call_target="tpu_custom_call" | custom-call | tf_op jit(solution)/shard_map/join/pallas_call | solution.py:505
  3.7 2.9 %collective-permute-start = (bf16[288,1152]{1,0:T(8,128)(2,1)}, bf16[288,1152]{1,0:T(8,128)(2,1)}, u32[]{:S(2)}, u32[]{:S(2)}) collective-permute-start(bf16[288,1152]{1,0:T(8,128)(2,1)} %get-tuple-element.72.refs_6_), channel_id=1, source_target_pairs={{0,2},{1,3},{2,0},{3,1},{4,6},{5,7},{6,4},{7,5},{8,12},{9,13},{10,... | collective-permute-start | bytes 1990664 | tf_op jit(solution)/shard_map/ppermute | solution.py:470
  6.6 1.5 %collective-permute-start.1 = (bf16[288,1152]{1,0:T(8,128)(2,1)}, bf16[288,1152]{1,0:T(8,128)(2,1)S(1)}, u32[]{:S(2)}, u32[]{:S(2)}) collective-permute-start(bf16[288,1152]{1,0:T(8,128)(2,1)} %get-tuple-element.81.refs_0_), channel_id=1, source_target_pairs={{0,4},{1,5},{2,6},{3,7},{4,0},{5,1},{6,2},{7,3},{8,10},{9,11},{10,... | collective-permute-start | bytes 1990664 | tf_op jit(solution)/shard_map/ppermute | solution.py:470
  8.2 0.7 iota_compare_fusion
  8.9 0.8 and_select_fusion.refs_12_
  9.7 0.9 constant_dynamic-slice_fusion
  10.6 3.6 %collective-permute-start.6 = (bf16[32,1152]{1,0:T(8,128)(2,1)S(1)}, bf16[32,1152]{1,0:T(8,128)(2,1)S(1)}, u32[]{:S(2)}, u32[]{:S(2)}) collective-permute-start(bf16[32,1152]{1,0:T(8,128)(2,1)S(1)} %constant_dynamic-slice_fusion), channel_id=1, source_target_pairs={{0,24},{8,16},{16,8},{24,0},{1,25},{9,17},{17,9},{25,1},{2,26},{10... | collective-permute-start | bytes 221192 | tf_op jit(solution)/shard_map/ppermute | solution.py:476
  14.2 0.8 collective-permute-start.4
  15.0 5.7 %convolution_convert_fusion.refs_10_ = bf16[1024,1152]{1,0:T(8,128)(2,1)S(1)} fusion(bf16[1024,1152]{1,0:T(8,128)(2,1)S(1)} %bitcast.10, bf16[1152,1152]{1,0:T(8,128)(2,1)} %refs_2_.3), kind=kOutput, calls=%fused_computation | convolution fusion | flops 2719088640 | bytes 7372800 | tf_op jit(solution)/shard_map/dot_general | solution.py:494
  22.0 1.4 %collective-permute-done.1.refs_1_ = bf16[288,1152]{1,0:T(8,128)(2,1)S(1)} collective-permute-done((bf16[288,1152]{1,0:T(8,128)(2,1)}, bf16[288,1152]{1,0:T(8,128)(2,1)S(1)}, u32[]{:S(2)}, u32[]{:S(2)}) %collective-permute-start.1) | collective-permute-done | bytes 663584 | tf_op jit(solution)/shard_map/ppermute | solution.py:470
  24.0 1.6 %collective-permute-start.11 = (bf16[288,1152]{1,0:T(8,128)(2,1)}, bf16[288,1152]{1,0:T(8,128)(2,1)S(1)}, u32[]{:S(2)}, u32[]{:S(2)}) collective-permute-start(bf16[288,1152]{1,0:T(8,128)(2,1)} %collective-permute-done.refs_7_), channel_id=1, source_target_pairs={{0,8},{8,0},{16,24},{24,16},{1,9},{9,1},{17,25},{25,17},{2,10},{10... | collective-permute-start | bytes 1990664 | tf_op jit(solution)/shard_map/ppermute | solution.py:476
  26.1 0.6 collective-permute-done.12.refs_11_
  26.7 0.9 collective-permute-start.14
  27.6 1.2 %collective-permute-start.16 = (bf16[144,1152]{1,0:T(8,128)(2,1)S(1)}, bf16[144,1152]{1,0:T(8,128)(2,1)S(1)}, u32[]{:S(2)}, u32[]{:S(2)}) collective-permute-start(bf16[144,1152]{1,0:T(8,128)(2,1)S(1)} %copy-done.6), channel_id=1, source_target_pairs={{0,2},{1,3},{2,0},{3,1},{4,6},{5,7},{6,4},{7,5},{8,12},{9,13},{10,... | collective-permute-start | bytes 995336 | tf_op jit(solution)/shard_map/ppermute | solution.py:470
  28.8 1.7 %collective-permute-start.15 = (bf16[144,1152]{1,0:T(8,128)(2,1)S(1)}, bf16[144,1152]{1,0:T(8,128)(2,1)S(1)}, u32[]{:S(2)}, u32[]{:S(2)}) collective-permute-start(bf16[144,1152]{1,0:T(8,128)(2,1)S(1)} %slice.3), channel_id=1, source_target_pairs={{0,8},{8,0},{16,24},{24,16},{1,9},{9,1},{17,25},{25,17},{2,10},{10... | collective-permute-start | bytes 995336 | tf_op jit(solution)/shard_map/ppermute | solution.py:476
  30.5 11.4 %collective-permute-done.11.refs_9_ = bf16[288,1152]{1,0:T(8,128)(2,1)S(1)} collective-permute-done((bf16[288,1152]{1,0:T(8,128)(2,1)}, bf16[288,1152]{1,0:T(8,128)(2,1)S(1)}, u32[]{:S(2)}, u32[]{:S(2)}) %collective-permute-start.11) | collective-permute-done | bytes 663584 | tf_op jit(solution)/shard_map/ppermute | solution.py:476
  42.5 2.0 %collective-permute-done.14.refs_2_ = bf16[288,1152]{1,0:T(8,128)(2,1)S(1)} collective-permute-done((bf16[288,1152]{1,0:T(8,128)(2,1)S(1)}, bf16[288,1152]{1,0:T(8,128)(2,1)S(1)}, u32[]{:S(2)}, u32[]{:S(2)}) %collective-permute-start.14) | collective-permute-done | bytes 663584 | tf_op jit(solution)/shard_map/ppermute | solution.py:470
  44.5 6.3 %collective-permute-done.16.refs_4_ = bf16[144,1152]{1,0:T(8,128)(2,1)S(1)} collective-permute-done((bf16[144,1152]{1,0:T(8,128)(2,1)S(1)}, bf16[144,1152]{1,0:T(8,128)(2,1)S(1)}, u32[]{:S(2)}, u32[]{:S(2)}) %collective-permute-start.16) | collective-permute-done | bytes 331808 | tf_op jit(solution)/shard_map/ppermute | solution.py:470
  51.3 1.1 %collective-permute-done.21.refs_9_ = bf16[144,1152]{1,0:T(8,128)(2,1)S(1)} collective-permute-done((bf16[144,1152]{1,0:T(8,128)(2,1)S(1)}, bf16[144,1152]{1,0:T(8,128)(2,1)S(1)}, u32[]{:S(2)}, u32[]{:S(2)}) %collective-permute-start.21) | collective-permute-done | bytes 331808 | tf_op jit(solution)/shard_map/ppermute | solution.py:462
  52.9 3.5 %encode.1 = (bf16[64,1152]{1,0:T(8,128)(2,1)S(1)}, f32[256,1152]{1,0:T(8,128)S(1)}, bf16[256,144]{1,0:T(8,128)(2,1)S(1)}, bf16[256,144]{1,0:T(8,128)(2,1)S(1)}, ...) custom-call(s32[3]{0:T(128)S(1)} %pad_add_fusion.place_ref, bf16[64,1152]{1,0:T(8,128)(2,1)S(1)} %bitcast.12, ...), custom_call_target="tpu_custom_call" | custom-call | flops 2000000000 | bytes 8000000 | tf_op jit(solution)/shard_map/encode/pallas_call | solution.py:579
  56.4 8.2 %attend.1 = (bf16[64,1152]{1,0:T(8,128)(2,1)S(1)}, bf16[2,512,512]{2,1,0:T(8,128)(2,1)S(1)}, f32[32,1152]{1,0:T(8,128)S(1)}, f32[32,1152]{1,0:T(8,128)S(1)}) custom-call(s32[3]{0:T(128)S(1)} %pad_add_fusion.place_ref, bf16[64,1152]{1,0:T(8,128)(2,1)S(1)} %get-tuple-element.80.encoded_ref, bf16[288,1152]{1,0:T(8,128)(2,1)S(1)} %copy-done.4, ...), custom_call_target="tpu_custom_call" | custom-call | flops 10000000000 | bytes 12000000 | tf_op jit(solution)/shard_map/attend/pallas_call | solution.py:600
  64.9 1.2 %collective-permute-done.22 = f32[32,1152]{1,0:T(8,128)S(1)} collective-permute-done((f32[32,1152]{1,0:T(8,128)S(1)}, f32[32,1152]{1,0:T(8,128)S(1)}, u32[]{:S(2)}, u32[]{:S(2)}) %collective-permute-start.22) | collective-permute-done | bytes 147488 | tf_op jit(solution)/shard_map/ppermute | solution.py:462
  66.2 1.6 %collective-permute-start.25 = (bf16[32,1152]{1,0:T(8,128)(2,1)S(1)}, bf16[32,1152]{1,0:T(8,128)(2,1)S(1)}, u32[]{:S(2)}, u32[]{:S(2)}) collective-permute-start(bf16[32,1152]{1,0:T(8,128)(2,1)S(1)} %add_convert_fusion.1), channel_id=1, source_target_pairs={{0,6},{1,7},{2,4},{3,5},{4,2},{5,3},{6,0},{7,1},{8,14},{9,15},{10,... | collective-permute-start | bytes 221192 | tf_op jit(solution)/shard_map/ppermute | solution.py:462
  68.1 1.6 %collective-permute-start.23 = (bf16[32,1152]{1,0:T(8,128)(2,1)S(1)}, bf16[32,1152]{1,0:T(8,128)(2,1)S(1)}, u32[]{:S(2)}, u32[]{:S(2)}) collective-permute-start(bf16[32,1152]{1,0:T(8,128)(2,1)S(1)} %add_convert_fusion.1), channel_id=1, source_target_pairs={{0,2},{1,3},{2,0},{3,1},{4,6},{5,7},{6,4},{7,5},{8,10},{9,11},{10,... | collective-permute-start | bytes 221192 | tf_op jit(solution)/shard_map/ppermute | solution.py:462
  69.7 3.2 %latent.2._ = bf16[1024,1152]{1,0:T(8,128)(2,1)} custom-call(bf16[2,512,512]{2,1,0:T(8,128)(2,1)S(1)} %get-tuple-element.95.score_ref.refs_0_, bf16[64,1152]{1,0:T(8,128)(2,1)S(1)} %get-tuple-element.96.key_ref.refs_1_, bf16[1152,1152]{1,0:T(8,128)(2,1)S(1)} %copy-done.2), custom_call_target="tpu_custom_call" | custom-call | flops 3000000000 | bytes 4000000 | tf_op jit(solution)/shard_map/latent/pallas_call | solution.py:628
  73.2 4.2 %collective-permute-start.28 = (bf16[32,1152]{1,0:T(8,128)(2,1)S(1)}, bf16[32,1152]{1,0:T(8,128)(2,1)S(1)}, u32[]{:S(2)}, u32[]{:S(2)}) collective-permute-start(bf16[32,1152]{1,0:T(8,128)(2,1)S(1)} %add_convert_fusion.refs_0_), channel_id=1, source_target_pairs={{0,24},{8,16},{16,8},{24,0},{1,25},{9,17},{17,9},{25,1},{2,26},{10... | collective-permute-start | bytes 221192 | tf_op jit(solution)/shard_map/ppermute | solution.py:476
  77.4 0.6 collective-permute-start.26
  78.0 3.4 %latent.3 = bf16[1024,1152]{1,0:T(8,128)(2,1)} custom-call(bf16[1024,1152]{1,0:T(8,128)(2,1)} %latent.2._, bf16[2,512,512]{2,1,0:T(8,128)(2,1)S(1)} %get-tuple-element.95.score_ref.refs_0_, bf16[64,1152]{1,0:T(8,128)(2,1)S(1)} %get-tuple-element.96.key_ref.refs_1_, bf16[1152,1152]{1,0:T(8,128)(2,1)S(1)} %copy-done.2), custom_call_target="tpu_custom_call", output_to_operand_aliasing={{}: (0, {})} | custom-call | flops 3000000000 | bytes 4000000 | tf_op jit(solution)/shard_map/latent/pallas_call | solution.py:628
  81.4 2.7 %collective-permute-done.27.refs_2_ = bf16[32,1152]{1,0:T(8,128)(2,1)S(1)} collective-permute-done((bf16[32,1152]{1,0:T(8,128)(2,1)S(1)}, bf16[32,1152]{1,0:T(8,128)(2,1)S(1)}, u32[]{:S(2)}, u32[]{:S(2)}) %collective-permute-start.27) | collective-permute-done | bytes 73760 | tf_op jit(solution)/shard_map/ppermute | solution.py:476
  84.1 0.5 collective-permute-start.31
  84.6 0.7 collective-permute-done.30.refs_5_
  85.9 4.2 %weight_grads.1 = (f32[144,1152]{1,0:T(8,128)}, f32[144,1152]{1,0:T(8,128)}, bf16[64,1152]{1,0:T(8,128)(2,1)}) custom-call(s32[3]{0:T(128)S(1)} %pad_add_fusion.place_ref, bf16[32,1152]{1,0:T(8,128)(2,1)S(1)} %add_convert_fusion.refs_0_, bf16[32,1152]{1,0:T(8,128)(2,1)S(1)} %collective-permute-done.26.refs_1_, ...), custom_call_target="tpu_custom_call" | custom-call | tf_op jit(solution)/shard_map/weight_grads/pallas_call | solution.py:654
  (63 shorter events, 5.8 us)
Async XLA Ops:
  3.2 6.5 %collective-permute-start.2 = (bf16[288,1152]{1,0:T(8,128)(2,1)}, bf16[288,1152]{1,0:T(8,128)(2,1)}, u32[]{:S(2)}, u32[]{:S(2)}) collective-permute-start(bf16[288,1152]{1,0:T(8,128)(2,1)} %get-tuple-element.72.refs_6_), channel_id=1, source_target_pairs={{0,1},{1,0},{2,3},{3,2},{4,5},{5,4},{6,7},{7,6},{8,9},{9,8},{10,11... | collective-permute-start | bytes 1990664 | tf_op jit(solution)/shard_map/ppermute | solution.py:462
  3.6 6.1 %collective-permute-start.3 = (bf16[288,1152]{1,0:T(8,128)(2,1)}, bf16[288,1152]{1,0:T(8,128)(2,1)}, u32[]{:S(2)}, u32[]{:S(2)}) collective-permute-start(bf16[288,1152]{1,0:T(8,128)(2,1)} %get-tuple-element.81.refs_0_), channel_id=1, source_target_pairs={{0,1},{1,0},{2,3},{3,2},{4,5},{5,4},{6,7},{7,6},{8,9},{9,8},{10,11... | collective-permute-start | bytes 1990664 | tf_op jit(solution)/shard_map/ppermute | solution.py:462
  3.7 18.3 %collective-permute-start = (bf16[288,1152]{1,0:T(8,128)(2,1)}, bf16[288,1152]{1,0:T(8,128)(2,1)}, u32[]{:S(2)}, u32[]{:S(2)}) collective-permute-start(bf16[288,1152]{1,0:T(8,128)(2,1)} %get-tuple-element.72.refs_6_), channel_id=1, source_target_pairs={{0,2},{1,3},{2,0},{3,1},{4,6},{5,7},{6,4},{7,5},{8,12},{9,13},{10,... | collective-permute-start | bytes 1990664 | tf_op jit(solution)/shard_map/ppermute | solution.py:470
  6.6 16.7 %collective-permute-start.1 = (bf16[288,1152]{1,0:T(8,128)(2,1)}, bf16[288,1152]{1,0:T(8,128)(2,1)S(1)}, u32[]{:S(2)}, u32[]{:S(2)}) collective-permute-start(bf16[288,1152]{1,0:T(8,128)(2,1)} %get-tuple-element.81.refs_0_), channel_id=1, source_target_pairs={{0,4},{1,5},{2,6},{3,7},{4,0},{5,1},{6,2},{7,3},{8,10},{9,11},{10,... | collective-permute-start | bytes 1990664 | tf_op jit(solution)/shard_map/ppermute | solution.py:470
  10.6 10.1 %collective-permute-start.6 = (bf16[32,1152]{1,0:T(8,128)(2,1)S(1)}, bf16[32,1152]{1,0:T(8,128)(2,1)S(1)}, u32[]{:S(2)}, u32[]{:S(2)}) collective-permute-start(bf16[32,1152]{1,0:T(8,128)(2,1)S(1)} %constant_dynamic-slice_fusion), channel_id=1, source_target_pairs={{0,24},{8,16},{16,8},{24,0},{1,25},{9,17},{17,9},{25,1},{2,26},{10... | collective-permute-start | bytes 221192 | tf_op jit(solution)/shard_map/ppermute | solution.py:476
  14.2 6.5 %collective-permute-start.5 = (bf16[32,1152]{1,0:T(8,128)(2,1)S(1)}, bf16[32,1152]{1,0:T(8,128)(2,1)S(1)}, u32[]{:S(2)}, u32[]{:S(2)}) collective-permute-start(bf16[32,1152]{1,0:T(8,128)(2,1)S(1)} %constant_dynamic-slice_fusion), channel_id=1, source_target_pairs={{0,16},{8,24},{16,0},{24,8},{1,17},{9,25},{17,1},{25,9},{2,18},{10... | collective-permute-start | bytes 221192 | tf_op jit(solution)/shard_map/ppermute | solution.py:476
  14.2 6.6 %collective-permute-start.4 = (bf16[32,1152]{1,0:T(8,128)(2,1)S(1)}, bf16[32,1152]{1,0:T(8,128)(2,1)S(1)}, u32[]{:S(2)}, u32[]{:S(2)}) collective-permute-start(bf16[32,1152]{1,0:T(8,128)(2,1)S(1)} %constant_dynamic-slice_fusion), channel_id=1, source_target_pairs={{0,8},{8,0},{16,24},{24,16},{1,9},{9,1},{17,25},{25,17},{2,10},{10... | collective-permute-start | bytes 221192 | tf_op jit(solution)/shard_map/ppermute | solution.py:476
  20.8 2.6 %collective-permute-start.7 = (bf16[32,1152]{1,0:T(8,128)(2,1)S(1)}, bf16[32,1152]{1,0:T(8,128)(2,1)S(1)}, u32[]{:S(2)}, u32[]{:S(2)}) collective-permute-start(bf16[32,1152]{1,0:T(8,128)(2,1)S(1)} %collective-permute-done.4.refs_0_), channel_id=1, source_target_pairs={{0,1},{1,0},{2,3},{3,2},{4,5},{5,4},{6,7},{7,6},{8,9},{9,8},{10,11... | collective-permute-start | bytes 221192 | tf_op jit(solution)/shard_map/ppermute | solution.py:462
  20.9 2.5 %collective-permute-start.8 = (bf16[32,1152]{1,0:T(8,128)(2,1)S(1)}, bf16[32,1152]{1,0:T(8,128)(2,1)S(1)}, u32[]{:S(2)}, u32[]{:S(2)}) collective-permute-start(bf16[32,1152]{1,0:T(8,128)(2,1)S(1)} %collective-permute-done.5.refs_1_), channel_id=1, source_target_pairs={{0,1},{1,0},{2,3},{3,2},{4,5},{5,4},{6,7},{7,6},{8,9},{9,8},{10,11... | collective-permute-start | bytes 221192 | tf_op jit(solution)/shard_map/ppermute | solution.py:462
  21.4 2.0 %collective-permute-start.9 = (bf16[32,1152]{1,0:T(8,128)(2,1)S(1)}, bf16[32,1152]{1,0:T(8,128)(2,1)S(1)}, u32[]{:S(2)}, u32[]{:S(2)}) collective-permute-start(bf16[32,1152]{1,0:T(8,128)(2,1)S(1)} %collective-permute-done.6.refs_2_), channel_id=1, source_target_pairs={{0,1},{1,0},{2,3},{3,2},{4,5},{5,4},{6,7},{7,6},{8,9},{9,8},{10,11... | collective-permute-start | bytes 221192 | tf_op jit(solution)/shard_map/ppermute | solution.py:462
  23.4 2.7 %collective-permute-start.13 = (bf16[288,1152]{1,0:T(8,128)(2,1)S(1)}, bf16[288,1152]{1,0:T(8,128)(2,1)S(1)}, u32[]{:S(2)}, u32[]{:S(2)}) collective-permute-start(bf16[288,1152]{1,0:T(8,128)(2,1)S(1)} %collective-permute-done.1.refs_1_), channel_id=1, source_target_pairs={{0,1},{1,0},{2,3},{3,2},{4,5},{5,4},{6,7},{7,6},{8,9},{9,8},{10,11... | collective-permute-start | bytes 1990664 | tf_op jit(solution)/shard_map/ppermute | solution.py:462
  23.5 3.3 %collective-permute-start.12 = (bf16[288,1152]{1,0:T(8,128)(2,1)}, bf16[288,1152]{1,0:T(8,128)(2,1)S(1)}, u32[]{:S(2)}, u32[]{:S(2)}) collective-permute-start(bf16[288,1152]{1,0:T(8,128)(2,1)} %collective-permute-done.refs_7_), channel_id=1, source_target_pairs={{0,1},{1,0},{2,3},{3,2},{4,5},{5,4},{6,7},{7,6},{8,9},{9,8},{10,11... | collective-permute-start | bytes 1990664 | tf_op jit(solution)/shard_map/ppermute | solution.py:462
  24.0 18.0 %collective-permute-start.11 = (bf16[288,1152]{1,0:T(8,128)(2,1)}, bf16[288,1152]{1,0:T(8,128)(2,1)S(1)}, u32[]{:S(2)}, u32[]{:S(2)}) collective-permute-start(bf16[288,1152]{1,0:T(8,128)(2,1)} %collective-permute-done.refs_7_), channel_id=1, source_target_pairs={{0,8},{8,0},{16,24},{24,16},{1,9},{9,1},{17,25},{25,17},{2,10},{10... | collective-permute-start | bytes 1990664 | tf_op jit(solution)/shard_map/ppermute | solution.py:476
  25.6 16.8 %collective-permute-start.10 = (bf16[288,1152]{1,0:T(8,128)(2,1)}, bf16[288,1152]{1,0:T(8,128)(2,1)S(1)}, u32[]{:S(2)}, u32[]{:S(2)}) collective-permute-start(bf16[288,1152]{1,0:T(8,128)(2,1)} %collective-permute-done.refs_7_), channel_id=1, source_target_pairs={{0,4},{1,5},{2,6},{3,7},{4,0},{5,1},{6,2},{7,3},{8,10},{9,11},{10,... | collective-permute-start | bytes 1990664 | tf_op jit(solution)/shard_map/ppermute | solution.py:470
  26.7 17.8 %collective-permute-start.14 = (bf16[288,1152]{1,0:T(8,128)(2,1)S(1)}, bf16[288,1152]{1,0:T(8,128)(2,1)S(1)}, u32[]{:S(2)}, u32[]{:S(2)}) collective-permute-start(bf16[288,1152]{1,0:T(8,128)(2,1)S(1)} %collective-permute-done.1.refs_1_), channel_id=1, source_target_pairs={{0,2},{1,3},{2,0},{3,1},{4,6},{5,7},{6,4},{7,5},{8,12},{9,13},{10,... | collective-permute-start | bytes 1990664 | tf_op jit(solution)/shard_map/ppermute | solution.py:470
  27.6 23.2 %collective-permute-start.16 = (bf16[144,1152]{1,0:T(8,128)(2,1)S(1)}, bf16[144,1152]{1,0:T(8,128)(2,1)S(1)}, u32[]{:S(2)}, u32[]{:S(2)}) collective-permute-start(bf16[144,1152]{1,0:T(8,128)(2,1)S(1)} %copy-done.6), channel_id=1, source_target_pairs={{0,2},{1,3},{2,0},{3,1},{4,6},{5,7},{6,4},{7,5},{8,12},{9,13},{10,... | collective-permute-start | bytes 995336 | tf_op jit(solution)/shard_map/ppermute | solution.py:470
  28.8 22.0 %collective-permute-start.15 = (bf16[144,1152]{1,0:T(8,128)(2,1)S(1)}, bf16[144,1152]{1,0:T(8,128)(2,1)S(1)}, u32[]{:S(2)}, u32[]{:S(2)}) collective-permute-start(bf16[144,1152]{1,0:T(8,128)(2,1)S(1)} %slice.3), channel_id=1, source_target_pairs={{0,8},{8,0},{16,24},{24,16},{1,9},{9,1},{17,25},{25,17},{2,10},{10... | collective-permute-start | bytes 995336 | tf_op jit(solution)/shard_map/ppermute | solution.py:476
  41.9 11.0 %collective-permute-start.18 = (bf16[288,1152]{1,0:T(8,128)(2,1)S(1)}, bf16[288,1152]{1,0:T(8,128)(2,1)S(1)}, u32[]{:S(2)}, u32[]{:S(2)}) collective-permute-start(bf16[288,1152]{1,0:T(8,128)(2,1)S(1)} %collective-permute-done.11.refs_9_), channel_id=1, source_target_pairs={{0,1},{1,0},{2,3},{3,2},{4,5},{5,4},{6,7},{7,6},{8,9},{9,8},{10,11... | collective-permute-start | bytes 1990664 | tf_op jit(solution)/shard_map/ppermute | solution.py:462
  42.4 10.5 %collective-permute-start.17 = (bf16[288,1152]{1,0:T(8,128)(2,1)S(1)}, bf16[288,1152]{1,0:T(8,128)(2,1)S(1)}, u32[]{:S(2)}, u32[]{:S(2)}) collective-permute-start(bf16[288,1152]{1,0:T(8,128)(2,1)S(1)} %collective-permute-done.10.refs_8_), channel_id=1, source_target_pairs={{0,1},{1,0},{2,3},{3,2},{4,5},{5,4},{6,7},{7,6},{8,9},{9,8},{10,11... | collective-permute-start | bytes 1990664 | tf_op jit(solution)/shard_map/ppermute | solution.py:462
  44.5 8.4 %collective-permute-start.19 = (bf16[288,1152]{1,0:T(8,128)(2,1)S(1)}, bf16[288,1152]{1,0:T(8,128)(2,1)S(1)}, u32[]{:S(2)}, u32[]{:S(2)}) collective-permute-start(bf16[288,1152]{1,0:T(8,128)(2,1)S(1)} %collective-permute-done.14.refs_2_), channel_id=1, source_target_pairs={{0,1},{1,0},{2,3},{3,2},{4,5},{5,4},{6,7},{7,6},{8,9},{9,8},{10,11... | collective-permute-start | bytes 1990664 | tf_op jit(solution)/shard_map/ppermute | solution.py:462
  50.8 1.6 %collective-permute-start.21 = (bf16[144,1152]{1,0:T(8,128)(2,1)S(1)}, bf16[144,1152]{1,0:T(8,128)(2,1)S(1)}, u32[]{:S(2)}, u32[]{:S(2)}) collective-permute-start(bf16[144,1152]{1,0:T(8,128)(2,1)S(1)} %collective-permute-done.16.refs_4_), channel_id=1, source_target_pairs={{0,1},{1,0},{2,3},{3,2},{4,5},{5,4},{6,7},{7,6},{8,9},{9,8},{10,11... | collective-permute-start | bytes 995336 | tf_op jit(solution)/shard_map/ppermute | solution.py:462
  50.8 2.1 %collective-permute-start.20 = (bf16[144,1152]{1,0:T(8,128)(2,1)S(1)}, bf16[144,1152]{1,0:T(8,128)(2,1)S(1)}, u32[]{:S(2)}, u32[]{:S(2)}) collective-permute-start(bf16[144,1152]{1,0:T(8,128)(2,1)S(1)} %collective-permute-done.15.refs_3_), channel_id=1, source_target_pairs={{0,1},{1,0},{2,3},{3,2},{4,5},{5,4},{6,7},{7,6},{8,9},{9,8},{10,11... | collective-permute-start | bytes 995336 | tf_op jit(solution)/shard_map/ppermute | solution.py:462
  64.7 1.4 %collective-permute-start.22 = (f32[32,1152]{1,0:T(8,128)S(1)}, f32[32,1152]{1,0:T(8,128)S(1)}, u32[]{:S(2)}, u32[]{:S(2)}) collective-permute-start(f32[32,1152]{1,0:T(8,128)S(1)} %get-tuple-element.94), channel_id=1, source_target_pairs={{0,1},{1,0},{2,3},{3,2},{4,5},{5,4},{6,7},{7,6},{8,9},{9,8},{10,11... | collective-permute-start | bytes 442376 | tf_op jit(solution)/shard_map/ppermute | solution.py:462
  66.2 6.7 %collective-permute-start.25 = (bf16[32,1152]{1,0:T(8,128)(2,1)S(1)}, bf16[32,1152]{1,0:T(8,128)(2,1)S(1)}, u32[]{:S(2)}, u32[]{:S(2)}) collective-permute-start(bf16[32,1152]{1,0:T(8,128)(2,1)S(1)} %add_convert_fusion.1), channel_id=1, source_target_pairs={{0,6},{1,7},{2,4},{3,5},{4,2},{5,3},{6,0},{7,1},{8,14},{9,15},{10,... | collective-permute-start | bytes 221192 | tf_op jit(solution)/shard_map/ppermute | solution.py:462
  67.7 5.3 %collective-permute-start.24 = (bf16[32,1152]{1,0:T(8,128)(2,1)S(1)}, bf16[32,1152]{1,0:T(8,128)(2,1)S(1)}, u32[]{:S(2)}, u32[]{:S(2)}) collective-permute-start(bf16[32,1152]{1,0:T(8,128)(2,1)S(1)} %add_convert_fusion.1), channel_id=1, source_target_pairs={{0,4},{1,5},{2,6},{3,7},{4,0},{5,1},{6,2},{7,3},{8,12},{9,13},{10,... | collective-permute-start | bytes 221192 | tf_op jit(solution)/shard_map/ppermute | solution.py:462
  68.1 5.0 %collective-permute-start.23 = (bf16[32,1152]{1,0:T(8,128)(2,1)S(1)}, bf16[32,1152]{1,0:T(8,128)(2,1)S(1)}, u32[]{:S(2)}, u32[]{:S(2)}) collective-permute-start(bf16[32,1152]{1,0:T(8,128)(2,1)S(1)} %add_convert_fusion.1), channel_id=1, source_target_pairs={{0,2},{1,3},{2,0},{3,1},{4,6},{5,7},{6,4},{7,5},{8,10},{9,11},{10,... | collective-permute-start | bytes 221192 | tf_op jit(solution)/shard_map/ppermute | solution.py:462
  73.1 11.5 %collective-permute-start.29 = (bf16[32,1152]{1,0:T(8,128)(2,1)S(1)}, bf16[32,1152]{1,0:T(8,128)(2,1)S(1)}, u32[]{:S(2)}, u32[]{:S(2)}) collective-permute-start(bf16[32,1152]{1,0:T(8,128)(2,1)S(1)} %add_convert_fusion.refs_0_), channel_id=1, source_target_pairs={{0,1},{1,0},{2,3},{3,2},{4,5},{5,4},{6,7},{7,6},{8,9},{9,8},{10,11... | collective-permute-start | bytes 221192 | tf_op jit(solution)/shard_map/ppermute | solution.py:462
  73.2 8.2 %collective-permute-start.28 = (bf16[32,1152]{1,0:T(8,128)(2,1)S(1)}, bf16[32,1152]{1,0:T(8,128)(2,1)S(1)}, u32[]{:S(2)}, u32[]{:S(2)}) collective-permute-start(bf16[32,1152]{1,0:T(8,128)(2,1)S(1)} %add_convert_fusion.refs_0_), channel_id=1, source_target_pairs={{0,24},{8,16},{16,8},{24,0},{1,25},{9,17},{17,9},{25,1},{2,26},{10... | collective-permute-start | bytes 221192 | tf_op jit(solution)/shard_map/ppermute | solution.py:476
  77.4 6.8 %collective-permute-start.27 = (bf16[32,1152]{1,0:T(8,128)(2,1)S(1)}, bf16[32,1152]{1,0:T(8,128)(2,1)S(1)}, u32[]{:S(2)}, u32[]{:S(2)}) collective-permute-start(bf16[32,1152]{1,0:T(8,128)(2,1)S(1)} %add_convert_fusion.refs_0_), channel_id=1, source_target_pairs={{0,16},{8,24},{16,0},{24,8},{1,17},{9,25},{17,1},{25,9},{2,18},{10... | collective-permute-start | bytes 221192 | tf_op jit(solution)/shard_map/ppermute | solution.py:476
  77.4 6.8 %collective-permute-start.26 = (bf16[32,1152]{1,0:T(8,128)(2,1)S(1)}, bf16[32,1152]{1,0:T(8,128)(2,1)S(1)}, u32[]{:S(2)}, u32[]{:S(2)}) collective-permute-start(bf16[32,1152]{1,0:T(8,128)(2,1)S(1)} %add_convert_fusion.refs_0_), channel_id=1, source_target_pairs={{0,8},{8,0},{16,24},{24,16},{1,9},{9,1},{17,25},{25,17},{2,10},{10... | collective-permute-start | bytes 221192 | tf_op jit(solution)/shard_map/ppermute | solution.py:476
  84.1 1.3 %collective-permute-start.30 = (bf16[32,1152]{1,0:T(8,128)(2,1)S(1)}, bf16[32,1152]{1,0:T(8,128)(2,1)S(1)}, u32[]{:S(2)}, u32[]{:S(2)}) collective-permute-start(bf16[32,1152]{1,0:T(8,128)(2,1)S(1)} %collective-permute-done.26.refs_1_), channel_id=1, source_target_pairs={{0,1},{1,0},{2,3},{3,2},{4,5},{5,4},{6,7},{7,6},{8,9},{9,8},{10,11... | collective-permute-start | bytes 221192 | tf_op jit(solution)/shard_map/ppermute | solution.py:462
  84.1 1.4 %collective-permute-start.31 = (bf16[32,1152]{1,0:T(8,128)(2,1)S(1)}, bf16[32,1152]{1,0:T(8,128)(2,1)S(1)}, u32[]{:S(2)}, u32[]{:S(2)}) collective-permute-start(bf16[32,1152]{1,0:T(8,128)(2,1)S(1)} %collective-permute-done.27.refs_2_), channel_id=1, source_target_pairs={{0,1},{1,0},{2,3},{3,2},{4,5},{5,4},{6,7},{7,6},{8,9},{9,8},{10,11... | collective-permute-start | bytes 221192 | tf_op jit(solution)/shard_map/ppermute | solution.py:462
  (8 other events, 172.6 us)

commit v3 on v2

--- a/solution.py
+++ b/solution.py
@@ -523,28 +523,30 @@
         queries = project_queries(after(latents, encoder_own, projector_own))
         plane_phrases = plane_peers(own_half)
         far_phrases = [swap(part, 1) for part in after_all(plane_phrases, queries)]
-        encoder_next, projector_next, value_next, far_phrases, queries, bias, place = (
+        encoder_next, projector_near, far_phrases, queries, bias, place = (
             lax.optimization_barrier(
-                (encoder_near, projector_near, value_weight, far_phrases, queries, bias, place)
+                (encoder_near, projector_near, far_phrases, queries, bias, place)
             )
         )
-        value_third = swap_by_plane(value_next, 1, 2)
+        key_third, value_third = [
+            swap_by_plane(block, 1, 2) for block in (key_weight, value_weight)
+        ]
         encoder_far = swap_by_plane(encoder_next, 2, 1)
         encoder_third = plane_swap(encoder_next, 1)
-        pairs = [swap(encoder_next, 1), swap(projector_next, 1)]
-        projector_next = after(projector_next, *pairs)
-        projector_far = swap_by_plane(projector_next, 1, 2)
-        key_third = plane_swap(projector_next[:shard_rows], 1)
+        key_near = projector_near[:shard_rows]
+        pairs = [swap(after(encoder_next, key_near), 1), swap(projector_near, 1)]
+        key_far = swap_by_plane(after(key_near, value_third), 1, 2)
+        value_far = swap_by_plane(value_third, 2, 1)
         arrays = [encoder, encoder_near, projector, projector_near]
-        arrays += [encoder_far, encoder_third, projector_far, key_third, value_third]
+        arrays += [encoder_far, encoder_third, key_third, value_third, key_far, value_far]
         arrays += [encoder_own, pairs[0], projector_own, pairs[1]]
-        arrays += [swap(block, 1) for block in arrays[4:9]]
-        arrays = list(lax.optimization_barrier(tuple(arrays)))
+        early = after_all([encoder_far, encoder_third], key_third, value_third)
+        arrays += [swap(block, 1) for block in (*early, key_third, value_third)]
         layout = {
             "first": (0, [(0, 0), (1, 0), (5, 0), (4, 0)]),
             "second": (0, [(i, shard_rows) for i in (0, 1, 5, 4)]),
-            "key": (1, [(2, 0), (3, 0), (7, 0), (6, 0)]),
-            "value": (1, [(2, shard_rows), (3, shard_rows), (8, 0), (6, shard_rows)]),
+            "key": (1, [(2, 0), (3, 0), (6, 0), (8, 0)]),
+            "value": (1, [(2, shard_rows), (3, shard_rows), (7, 0), (9, 0)]),
         }
     else:
         own_half = lax.dynamic_slice_in_dim(phrase_rows, core * half, half, 0)
@@ -562,7 +564,7 @@
                 ("value", chips, shard_rows),
             )
         }
-    near_count = chips == 4 and 9 or len(arrays) // 2
+    near_count = chips == 4 and 10 or len(arrays) // 2
     for name, (scheme, blocks) in layout.items():
         layout[name] = (scheme, blocks + [(near_count + i, offset) for i, offset in blocks])
 
@@ -591,11 +593,15 @@
         scratch_shapes=[pltpu.VMEM((all_rows, features), jnp.bfloat16)],
         compiler_params=vmem(18),
         cost_estimate=pl.CostEstimate(
-            flops=2 * 10**9, bytes_accessed=8 * 10**6, transcendentals=10**5
+            flops=10**6, bytes_accessed=10**4, transcendentals=0
         ),
         name="encode",
     )(place, phrase_rows, *plane_phrases, *far_phrases, *encoder_arrays)
     grads = out_grad.reshape(images * tokens, features)
+    if chips == 4:
+        *late, encoded = lax.optimization_barrier((*arrays[8:10], encoded))
+        arrays[8:10] = late
+        arrays += [swap(block, 1) for block in late]
     projector_arrays, projector_layout = weights("key", "value")
     key_rows, score_grad, grad_mine, grad_other = pl.pallas_call(
         functools.partial(attend_kernel, chips, images, projector_layout),

time: 90.4 us -> 87.5 us (0.968)
  waiting for transfers between devices: 29.8 us -> 25.6 us
  local copies, waits for them, and re-layouts: 0.96 us -> 1.94 us
    ppermute x8 -> x7, waiting for transfers between devices: 14.2 us -> 1.76 us  [plane_swap(): return lax.ppermute(array, 'dp', [(i, i ^ distance) for i in range(planes)])]
    ppermute x5 -> x7, waiting for transfers between devices: 10.6 us -> 17.9 us  [swap_by_plane(): return lax.ppermute(array, ('dp', 'seq'), pairs)]
    ppermute x5 -> x7, starting transfers between devices: 6.99 us -> 9.21 us  [swap_by_plane(): return lax.ppermute(array, ('dp', 'seq'), pairs)]
    ppermute x8 -> x7, starting transfers between devices: 12.5 us -> 10.5 us  [plane_swap(): return lax.ppermute(array, 'dp', [(i, i ^ distance) for i in range(planes)])]
    slice x1, local copies, waits for them, and re-layouts: 0.03 us -> 1 us  [tiled(): key_near = projector_near[:shard_rows]]
    ppermute x20 -> x21, waiting for transfers between devices: 4.94 us -> 5.9 us  [swap(): lax.ppermute(array, 'seq', [(i, i ^ distance) for i in range(shards)])]
    ppermute x20 -> x21, starting transfers between devices: 6.64 us -> 6.66 us  [swap(): lax.ppermute(array, 'seq', [(i, i ^ distance) for i in range(shards)])]
  transfers between devices with their start and end apart: 33 -> 35, of which waited for: 16 -> 17; matrix products, arithmetic and copies ran while one was open for 9% -> 11% of each run, Pallas kernels for 7% -> 11%
where the time goes in v3:
time: 87.5 us; the launch traced here: 87.2 us
  starting transfers between devices  26.3 us (30%)
  waiting for transfers between devices  25.6 us (29%)
  Pallas kernels  24.9 us (28%)
  matrix products  5.75 us (7%)
  local copies, waits for them, and re-layouts  1.94 us (2%)
  other arithmetic  1.67 us (2%)
  between operations  1.02 us (1%)
    ppermute x7, waiting for transfers between devices, swap_by_plane(): return lax.ppermute(array, ('dp', 'seq'), pairs)  17.9 us
    ppermute x7, starting transfers between devices, plane_swap(): return lax.ppermute(array, 'dp', [(i, i ^ distance) for i in range(planes)])  10.5 us
    ppermute x7, starting transfers between devices, swap_by_plane(): return lax.ppermute(array, ('dp', 'seq'), pairs)  9.21 us
    pallas_call x1, Pallas kernels, tiled(): pl.pallas_call(functools.partial(attend_kernel, chips, images, projector_...  8.41 us
    ppermute x21, starting transfers between devices, swap(): lax.ppermute(array, 'seq', [(i, i ^ distance) for i in range(shards)])  6.66 us
    pallas_call x2, Pallas kernels, latent_part(): pl.pallas_call(kernel if whole is None else lambda _, *refs: kernel(*refs...  6.56 us
    ppermute x21, waiting for transfers between devices, swap(): lax.ppermute(array, 'seq', [(i, i ^ distance) for i in range(shards)])  5.9 us
    dot_general x1, matrix products, project_queries(): jnp.dot(tokens_in.reshape(images * tokens, features), query_weight, prefe...  5.75 us
  transfers between devices with their start and end apart: 35, of which 17 were waited for; matrix products, arithmetic and copies ran while one was open for 11% of the time, Pallas kernels for 11%

profile of v3, /device:TPU:0, one launch (start us, length us, event | category | flops | bytes accessed | tf_op | source)
XLA Modules:
  0.0 87.2 jit_solution(16617395785348454208)
XLA Ops:
  0.6 2.5 %join.1 = (bf16[288,1152]{1,0:T(8,128)(2,1)}, bf16[288,1152]{1,0:T(8,128)(2,1)}) custom-call(bf16[144,1152]{1,0:T(8,128)(2,1)} %refs_0_.1, bf16[144,1152]{1,0:T(8,128)(2,1)} %refs_1_.1, bf16[144,1152]{1,0:T(8,128)(2,1)} %refs_2_.2, bf16[144,1152]{1,0:T(8,128)(2,1)} %refs_3_.1), custom_call_target="tpu_custom_call" | custom-call | tf_op jit(solution)/shard_map/join/pallas_call | solution.py:505
  3.7 2.9 %collective-permute-start = (bf16[288,1152]{1,0:T(8,128)(2,1)}, bf16[288,1152]{1,0:T(8,128)(2,1)}, u32[]{:S(2)}, u32[]{:S(2)}) collective-permute-start(bf16[288,1152]{1,0:T(8,128)(2,1)} %get-tuple-element.44.refs_6_), channel_id=1, source_target_pairs={{0,2},{1,3},{2,0},{3,1},{4,6},{5,7},{6,4},{7,5},{8,12},{9,13},{10,... | collective-permute-start | bytes 1990664 | tf_op jit(solution)/shard_map/ppermute | solution.py:470
  6.6 1.5 %collective-permute-start.1 = (bf16[288,1152]{1,0:T(8,128)(2,1)}, bf16[288,1152]{1,0:T(8,128)(2,1)}, u32[]{:S(2)}, u32[]{:S(2)}) collective-permute-start(bf16[288,1152]{1,0:T(8,128)(2,1)} %get-tuple-element.45.refs_0_), channel_id=1, source_target_pairs={{0,4},{1,5},{2,6},{3,7},{4,0},{5,1},{6,2},{7,3},{8,10},{9,11},{10,... | collective-permute-start | bytes 1990664 | tf_op jit(solution)/shard_map/ppermute | solution.py:470
  8.2 0.7 iota_compare_fusion
  8.9 0.8 and_select_fusion.refs_14_
  9.7 0.9 %constant_dynamic-slice_fusion = bf16[32,1152]{1,0:T(8,128)(2,1)S(1)} fusion(bf16[64,1152]{1,0:T(8,128)(2,1)} %bitcast.11, s32[]{:T(128)S(6)} %select_n.32), kind=kLoop, calls=%fused_computation.15 | loop fusion | bytes 147460 | tf_op jit(solution)/shard_map/dynamic_slice | solution.py:520
  10.6 1.6 %collective-permute-start.4 = (bf16[32,1152]{1,0:T(8,128)(2,1)S(1)}, bf16[32,1152]{1,0:T(8,128)(2,1)S(1)}, u32[]{:S(2)}, u32[]{:S(2)}) collective-permute-start(bf16[32,1152]{1,0:T(8,128)(2,1)S(1)} %constant_dynamic-slice_fusion), channel_id=1, source_target_pairs={{0,8},{8,0},{16,24},{24,16},{1,9},{9,1},{17,25},{25,17},{2,10},{10... | collective-permute-start | bytes 221192 | tf_op jit(solution)/shard_map/ppermute | solution.py:476
  12.2 2.6 %collective-permute-start.5 = (bf16[32,1152]{1,0:T(8,128)(2,1)S(1)}, bf16[32,1152]{1,0:T(8,128)(2,1)S(1)}, u32[]{:S(2)}, u32[]{:S(2)}) collective-permute-start(bf16[32,1152]{1,0:T(8,128)(2,1)S(1)} %constant_dynamic-slice_fusion), channel_id=1, source_target_pairs={{0,16},{8,24},{16,0},{24,8},{1,17},{9,25},{17,1},{25,9},{2,18},{10... | collective-permute-start | bytes 221192 | tf_op jit(solution)/shard_map/ppermute | solution.py:476
  15.0 5.7 %convolution_convert_fusion.refs_12_ = bf16[1024,1152]{1,0:T(8,128)(2,1)S(1)} fusion(bf16[1024,1152]{1,0:T(8,128)(2,1)S(1)} %bitcast.10, bf16[1152,1152]{1,0:T(8,128)(2,1)} %refs_2_.3), kind=kOutput, calls=%fused_computation | convolution fusion | flops 2719088640 | bytes 7372800 | tf_op jit(solution)/shard_map/dot_general | solution.py:494
  22.0 1.5 %collective-permute-done.1.refs_1_ = bf16[288,1152]{1,0:T(8,128)(2,1)} collective-permute-done((bf16[288,1152]{1,0:T(8,128)(2,1)}, bf16[288,1152]{1,0:T(8,128)(2,1)}, u32[]{:S(2)}, u32[]{:S(2)}) %collective-permute-start.1) | collective-permute-done | bytes 663584 | tf_op jit(solution)/shard_map/ppermute | solution.py:470
  23.5 1.6 %collective-permute-start.13 = (bf16[288,1152]{1,0:T(8,128)(2,1)}, bf16[288,1152]{1,0:T(8,128)(2,1)S(1)}, u32[]{:S(2)}, u32[]{:S(2)}) collective-permute-start(bf16[288,1152]{1,0:T(8,128)(2,1)} %collective-permute-done.refs_7_), channel_id=1, source_target_pairs={{0,4},{1,5},{2,6},{3,7},{4,0},{5,1},{6,2},{7,3},{8,10},{9,11},{10,... | collective-permute-start | bytes 1990664 | tf_op jit(solution)/shard_map/ppermute | solution.py:470
  25.1 1.6 %collective-permute-start.14 = (bf16[288,1152]{1,0:T(8,128)(2,1)}, bf16[288,1152]{1,0:T(8,128)(2,1)S(1)}, u32[]{:S(2)}, u32[]{:S(2)}) collective-permute-start(bf16[288,1152]{1,0:T(8,128)(2,1)} %collective-permute-done.refs_7_), channel_id=1, source_target_pairs={{0,8},{8,0},{16,24},{24,16},{1,9},{9,1},{17,25},{25,17},{2,10},{10... | collective-permute-start | bytes 1990664 | tf_op jit(solution)/shard_map/ppermute | solution.py:476
  27.2 1.5 %collective-permute-start.16 = (bf16[144,1152]{1,0:T(8,128)(2,1)S(1)}, bf16[144,1152]{1,0:T(8,128)(2,1)S(1)}, u32[]{:S(2)}, u32[]{:S(2)}) collective-permute-start(bf16[144,1152]{1,0:T(8,128)(2,1)S(1)} %copy-done.7), channel_id=1, source_target_pairs={{0,2},{1,3},{2,0},{3,1},{4,6},{5,7},{6,4},{7,5},{8,12},{9,13},{10,... | collective-permute-start | bytes 995336 | tf_op jit(solution)/shard_map/ppermute | solution.py:470
  28.7 1.0 %slice.3 = bf16[144,1152]{1,0:T(8,128)(2,1)S(1)} slice(bf16[288,1152]{1,0:T(8,128)(2,1)} %collective-permute-done.1.refs_1_), slice={[0:144], [0:1152]} | slice | bytes 663552 | tf_op jit(solution)/shard_map/slice | solution.py:536
  29.8 7.6 %collective-permute-done.10.refs_3_ = bf16[144,1152]{1,0:T(8,128)(2,1)S(1)} collective-permute-done((bf16[144,1152]{1,0:T(8,128)(2,1)S(1)}, bf16[144,1152]{1,0:T(8,128)(2,1)S(1)}, u32[]{:S(2)}, u32[]{:S(2)}) %collective-permute-start.10) | collective-permute-done | bytes 331808 | tf_op jit(solution)/shard_map/ppermute | solution.py:470
  37.4 4.3 %collective-permute-done.16.refs_2_ = bf16[144,1152]{1,0:T(8,128)(2,1)S(1)} collective-permute-done((bf16[144,1152]{1,0:T(8,128)(2,1)S(1)}, bf16[144,1152]{1,0:T(8,128)(2,1)S(1)}, u32[]{:S(2)}, u32[]{:S(2)}) %collective-permute-start.16) | collective-permute-done | bytes 331808 | tf_op jit(solution)/shard_map/ppermute | solution.py:470
  44.0 0.8 collective-permute-done.18.refs_13_
  45.0 3.3 %encode.1 = (bf16[64,1152]{1,0:T(8,128)(2,1)S(1)}, f32[256,1152]{1,0:T(8,128)S(1)}, bf16[256,144]{1,0:T(8,128)(2,1)S(1)}, bf16[256,144]{1,0:T(8,128)(2,1)S(1)}, ...) custom-call(s32[3]{0:T(128)S(1)} %pad_add_fusion.place_ref, bf16[64,1152]{1,0:T(8,128)(2,1)S(1)} %bitcast.12, ...), custom_call_target="tpu_custom_call" | custom-call | flops 1000000 | bytes 10000 | tf_op jit(solution)/shard_map/encode/pallas_call | solution.py:581
  48.3 3.8 %collective-permute-done.12.refs_5_ = bf16[144,1152]{1,0:T(8,128)(2,1)S(1)} collective-permute-done((bf16[144,1152]{1,0:T(8,128)(2,1)S(1)}, bf16[144,1152]{1,0:T(8,128)(2,1)S(1)}, u32[]{:S(2)}, u32[]{:S(2)}) %collective-permute-start.12) | collective-permute-done | bytes 331808 | tf_op jit(solution)/shard_map/ppermute | solution.py:470
  52.9 1.1 %collective-permute-done.22.refs_10_ = bf16[144,1152]{1,0:T(8,128)(2,1)S(1)} collective-permute-done((bf16[144,1152]{1,0:T(8,128)(2,1)S(1)}, bf16[144,1152]{1,0:T(8,128)(2,1)S(1)}, u32[]{:S(2)}, u32[]{:S(2)}) %collective-permute-start.22) | collective-permute-done | bytes 331808 | tf_op jit(solution)/shard_map/ppermute | solution.py:462
  54.5 8.4 %attend.1 = (bf16[64,1152]{1,0:T(8,128)(2,1)S(1)}, bf16[2,512,512]{2,1,0:T(8,128)(2,1)S(1)}, f32[32,1152]{1,0:T(8,128)S(1)}, f32[32,1152]{1,0:T(8,128)S(1)}) custom-call(s32[3]{0:T(128)S(1)} %pad_add_fusion.place_ref, bf16[64,1152]{1,0:T(8,128)(2,1)S(1)} %get-tuple-element.62.encoded_ref, bf16[288,1152]{1,0:T(8,128)(2,1)S(1)} %copy-done.5, ...), custom_call_target="tpu_custom_call" | custom-call | flops 10000000000 | bytes 12000000 | tf_op jit(solution)/shard_map/attend/pallas_call | solution.py:606
  63.1 1.2 %collective-permute-done.24 = f32[32,1152]{1,0:T(8,128)S(1)} collective-permute-done((f32[32,1152]{1,0:T(8,128)S(1)}, f32[32,1152]{1,0:T(8,128)S(1)}, u32[]{:S(2)}, u32[]{:S(2)}) %collective-permute-start.24) | collective-permute-done | bytes 147488 | tf_op jit(solution)/shard_map/ppermute | solution.py:462
  65.0 1.4 %collective-permute-start.26 = (bf16[32,1152]{1,0:T(8,128)(2,1)S(1)}, bf16[32,1152]{1,0:T(8,128)(2,1)S(1)}, u32[]{:S(2)}, u32[]{:S(2)}) collective-permute-start(bf16[32,1152]{1,0:T(8,128)(2,1)S(1)} %add_convert_fusion.1), channel_id=1, source_target_pairs={{0,4},{1,5},{2,6},{3,7},{4,0},{5,1},{6,2},{7,3},{8,12},{9,13},{10,... | collective-permute-start | bytes 221192 | tf_op jit(solution)/shard_map/ppermute | solution.py:462
  66.4 1.5 %collective-permute-start.27 = (bf16[32,1152]{1,0:T(8,128)(2,1)S(1)}, bf16[32,1152]{1,0:T(8,128)(2,1)S(1)}, u32[]{:S(2)}, u32[]{:S(2)}) collective-permute-start(bf16[32,1152]{1,0:T(8,128)(2,1)S(1)} %add_convert_fusion.1), channel_id=1, source_target_pairs={{0,6},{1,7},{2,4},{3,5},{4,2},{5,3},{6,0},{7,1},{8,14},{9,15},{10,... | collective-permute-start | bytes 221192 | tf_op jit(solution)/shard_map/ppermute | solution.py:462
  67.9 3.2 %latent.2._ = bf16[1024,1152]{1,0:T(8,128)(2,1)} custom-call(bf16[2,512,512]{2,1,0:T(8,128)(2,1)S(1)} %get-tuple-element.69.score_ref.refs_0_, bf16[64,1152]{1,0:T(8,128)(2,1)S(1)} %get-tuple-element.70.key_ref.refs_1_, bf16[1152,1152]{1,0:T(8,128)(2,1)S(1)} %copy-done.3), custom_call_target="tpu_custom_call" | custom-call | flops 3000000000 | bytes 4000000 | tf_op jit(solution)/shard_map/latent/pallas_call | solution.py:634
  71.7 1.1 %collective-permute-start.28 = (bf16[32,1152]{1,0:T(8,128)(2,1)S(1)}, bf16[32,1152]{1,0:T(8,128)(2,1)S(1)}, u32[]{:S(2)}, u32[]{:S(2)}) collective-permute-start(bf16[32,1152]{1,0:T(8,128)(2,1)S(1)} %add_convert_fusion.refs_0_), channel_id=1, source_target_pairs={{0,8},{8,0},{16,24},{24,16},{1,9},{9,1},{17,25},{25,17},{2,10},{10... | collective-permute-start | bytes 221192 | tf_op jit(solution)/shard_map/ppermute | solution.py:476
  72.8 2.2 %collective-permute-start.29 = (bf16[32,1152]{1,0:T(8,128)(2,1)S(1)}, bf16[32,1152]{1,0:T(8,128)(2,1)S(1)}, u32[]{:S(2)}, u32[]{:S(2)}) collective-permute-start(bf16[32,1152]{1,0:T(8,128)(2,1)S(1)} %add_convert_fusion.refs_0_), channel_id=1, source_target_pairs={{0,16},{8,24},{16,0},{24,8},{1,17},{9,25},{17,1},{25,9},{2,18},{10... | collective-permute-start | bytes 221192 | tf_op jit(solution)/shard_map/ppermute | solution.py:476
  74.9 1.3 %collective-permute-start.30 = (bf16[32,1152]{1,0:T(8,128)(2,1)S(1)}, bf16[32,1152]{1,0:T(8,128)(2,1)S(1)}, u32[]{:S(2)}, u32[]{:S(2)}) collective-permute-start(bf16[32,1152]{1,0:T(8,128)(2,1)S(1)} %add_convert_fusion.refs_0_), channel_id=1, source_target_pairs={{0,24},{8,16},{16,8},{24,0},{1,25},{9,17},{17,9},{25,1},{2,26},{10... | collective-permute-start | bytes 221192 | tf_op jit(solution)/shard_map/ppermute | solution.py:476
  76.2 3.4 %latent.3 = bf16[1024,1152]{1,0:T(8,128)(2,1)} custom-call(bf16[1024,1152]{1,0:T(8,128)(2,1)} %latent.2._, bf16[2,512,512]{2,1,0:T(8,128)(2,1)S(1)} %get-tuple-element.69.score_ref.refs_0_, bf16[64,1152]{1,0:T(8,128)(2,1)S(1)} %get-tuple-element.70.key_ref.refs_1_, bf16[1152,1152]{1,0:T(8,128)(2,1)S(1)} %copy-done.3), custom_call_target="tpu_custom_call", output_to_operand_aliasing={{}: (0, {})} | custom-call | flops 3000000000 | bytes 4000000 | tf_op jit(solution)/shard_map/latent/pallas_call | solution.py:634
  79.6 1.5 %collective-permute-done.30.refs_3_ = bf16[32,1152]{1,0:T(8,128)(2,1)S(1)} collective-permute-done((bf16[32,1152]{1,0:T(8,128)(2,1)S(1)}, bf16[32,1152]{1,0:T(8,128)(2,1)S(1)}, u32[]{:S(2)}, u32[]{:S(2)}) %collective-permute-start.30) | collective-permute-done | bytes 73760 | tf_op jit(solution)/shard_map/ppermute | solution.py:476
  81.7 0.7 collective-permute-done.32.refs_5_
  82.9 4.2 %weight_grads.1 = (f32[144,1152]{1,0:T(8,128)}, f32[144,1152]{1,0:T(8,128)}, bf16[64,1152]{1,0:T(8,128)(2,1)}) custom-call(s32[3]{0:T(128)S(1)} %pad_add_fusion.place_ref, bf16[32,1152]{1,0:T(8,128)(2,1)S(1)} %add_convert_fusion.refs_0_, bf16[32,1152]{1,0:T(8,128)(2,1)S(1)} %collective-permute-done.28.refs_1_, ...), custom_call_target="tpu_custom_call" | custom-call | tf_op jit(solution)/shard_map/weight_grads/pallas_call | solution.py:660
  (69 shorter events, 8.8 us)
Async XLA Ops:
  3.2 6.5 %collective-permute-start.2 = (bf16[288,1152]{1,0:T(8,128)(2,1)}, bf16[288,1152]{1,0:T(8,128)(2,1)S(1)}, u32[]{:S(2)}, u32[]{:S(2)}) collective-permute-start(bf16[288,1152]{1,0:T(8,128)(2,1)} %get-tuple-element.44.refs_6_), channel_id=1, source_target_pairs={{0,1},{1,0},{2,3},{3,2},{4,5},{5,4},{6,7},{7,6},{8,9},{9,8},{10,11... | collective-permute-start | bytes 1990664 | tf_op jit(solution)/shard_map/ppermute | solution.py:462
  3.6 6.1 %collective-permute-start.3 = (bf16[288,1152]{1,0:T(8,128)(2,1)}, bf16[288,1152]{1,0:T(8,128)(2,1)}, u32[]{:S(2)}, u32[]{:S(2)}) collective-permute-start(bf16[288,1152]{1,0:T(8,128)(2,1)} %get-tuple-element.45.refs_0_), channel_id=1, source_target_pairs={{0,1},{1,0},{2,3},{3,2},{4,5},{5,4},{6,7},{7,6},{8,9},{9,8},{10,11... | collective-permute-start | bytes 1990664 | tf_op jit(solution)/shard_map/ppermute | solution.py:462
  3.7 18.3 %collective-permute-start = (bf16[288,1152]{1,0:T(8,128)(2,1)}, bf16[288,1152]{1,0:T(8,128)(2,1)}, u32[]{:S(2)}, u32[]{:S(2)}) collective-permute-start(bf16[288,1152]{1,0:T(8,128)(2,1)} %get-tuple-element.44.refs_6_), channel_id=1, source_target_pairs={{0,2},{1,3},{2,0},{3,1},{4,6},{5,7},{6,4},{7,5},{8,12},{9,13},{10,... | collective-permute-start | bytes 1990664 | tf_op jit(solution)/shard_map/ppermute | solution.py:470
  6.6 16.9 %collective-permute-start.1 = (bf16[288,1152]{1,0:T(8,128)(2,1)}, bf16[288,1152]{1,0:T(8,128)(2,1)}, u32[]{:S(2)}, u32[]{:S(2)}) collective-permute-start(bf16[288,1152]{1,0:T(8,128)(2,1)} %get-tuple-element.45.refs_0_), channel_id=1, source_target_pairs={{0,4},{1,5},{2,6},{3,7},{4,0},{5,1},{6,2},{7,3},{8,10},{9,11},{10,... | collective-permute-start | bytes 1990664 | tf_op jit(solution)/shard_map/ppermute | solution.py:470
  10.6 10.2 %collective-permute-start.4 = (bf16[32,1152]{1,0:T(8,128)(2,1)S(1)}, bf16[32,1152]{1,0:T(8,128)(2,1)S(1)}, u32[]{:S(2)}, u32[]{:S(2)}) collective-permute-start(bf16[32,1152]{1,0:T(8,128)(2,1)S(1)} %constant_dynamic-slice_fusion), channel_id=1, source_target_pairs={{0,8},{8,0},{16,24},{24,16},{1,9},{9,1},{17,25},{25,17},{2,10},{10... | collective-permute-start | bytes 221192 | tf_op jit(solution)/shard_map/ppermute | solution.py:476
  12.2 8.6 %collective-permute-start.5 = (bf16[32,1152]{1,0:T(8,128)(2,1)S(1)}, bf16[32,1152]{1,0:T(8,128)(2,1)S(1)}, u32[]{:S(2)}, u32[]{:S(2)}) collective-permute-start(bf16[32,1152]{1,0:T(8,128)(2,1)S(1)} %constant_dynamic-slice_fusion), channel_id=1, source_target_pairs={{0,16},{8,24},{16,0},{24,8},{1,17},{9,25},{17,1},{25,9},{2,18},{10... | collective-permute-start | bytes 221192 | tf_op jit(solution)/shard_map/ppermute | solution.py:476
  14.8 6.3 %collective-permute-start.6 = (bf16[32,1152]{1,0:T(8,128)(2,1)S(1)}, bf16[32,1152]{1,0:T(8,128)(2,1)S(1)}, u32[]{:S(2)}, u32[]{:S(2)}) collective-permute-start(bf16[32,1152]{1,0:T(8,128)(2,1)S(1)} %constant_dynamic-slice_fusion), channel_id=1, source_target_pairs={{0,24},{8,16},{16,8},{24,0},{1,25},{9,17},{17,9},{25,1},{2,26},{10... | collective-permute-start | bytes 221192 | tf_op jit(solution)/shard_map/ppermute | solution.py:476
  21.0 2.4 %collective-permute-start.7 = (bf16[32,1152]{1,0:T(8,128)(2,1)S(1)}, bf16[32,1152]{1,0:T(8,128)(2,1)S(1)}, u32[]{:S(2)}, u32[]{:S(2)}) collective-permute-start(bf16[32,1152]{1,0:T(8,128)(2,1)S(1)} %collective-permute-done.4.refs_0_), channel_id=1, source_target_pairs={{0,1},{1,0},{2,3},{3,2},{4,5},{5,4},{6,7},{7,6},{8,9},{9,8},{10,11... | collective-permute-start | bytes 221192 | tf_op jit(solution)/shard_map/ppermute | solution.py:462
  21.0 2.4 %collective-permute-start.8 = (bf16[32,1152]{1,0:T(8,128)(2,1)S(1)}, bf16[32,1152]{1,0:T(8,128)(2,1)S(1)}, u32[]{:S(2)}, u32[]{:S(2)}) collective-permute-start(bf16[32,1152]{1,0:T(8,128)(2,1)S(1)} %collective-permute-done.5.refs_1_), channel_id=1, source_target_pairs={{0,1},{1,0},{2,3},{3,2},{4,5},{5,4},{6,7},{7,6},{8,9},{9,8},{10,11... | collective-permute-start | bytes 221192 | tf_op jit(solution)/shard_map/ppermute | solution.py:462
  21.6 1.9 %collective-permute-start.9 = (bf16[32,1152]{1,0:T(8,128)(2,1)S(1)}, bf16[32,1152]{1,0:T(8,128)(2,1)S(1)}, u32[]{:S(2)}, u32[]{:S(2)}) collective-permute-start(bf16[32,1152]{1,0:T(8,128)(2,1)S(1)} %collective-permute-done.6.refs_2_), channel_id=1, source_target_pairs={{0,1},{1,0},{2,3},{3,2},{4,5},{5,4},{6,7},{7,6},{8,9},{9,8},{10,11... | collective-permute-start | bytes 221192 | tf_op jit(solution)/shard_map/ppermute | solution.py:462
  23.5 18.3 %collective-permute-start.13 = (bf16[288,1152]{1,0:T(8,128)(2,1)}, bf16[288,1152]{1,0:T(8,128)(2,1)S(1)}, u32[]{:S(2)}, u32[]{:S(2)}) collective-permute-start(bf16[288,1152]{1,0:T(8,128)(2,1)} %collective-permute-done.refs_7_), channel_id=1, source_target_pairs={{0,4},{1,5},{2,6},{3,7},{4,0},{5,1},{6,2},{7,3},{8,10},{9,11},{10,... | collective-permute-start | bytes 1990664 | tf_op jit(solution)/shard_map/ppermute | solution.py:470
  25.1 16.7 %collective-permute-start.14 = (bf16[288,1152]{1,0:T(8,128)(2,1)}, bf16[288,1152]{1,0:T(8,128)(2,1)S(1)}, u32[]{:S(2)}, u32[]{:S(2)}) collective-permute-start(bf16[288,1152]{1,0:T(8,128)(2,1)} %collective-permute-done.refs_7_), channel_id=1, source_target_pairs={{0,8},{8,0},{16,24},{24,16},{1,9},{9,1},{17,25},{25,17},{2,10},{10... | collective-permute-start | bytes 1990664 | tf_op jit(solution)/shard_map/ppermute | solution.py:476
  26.7 10.7 %collective-permute-start.10 = (bf16[144,1152]{1,0:T(8,128)(2,1)S(1)}, bf16[144,1152]{1,0:T(8,128)(2,1)S(1)}, u32[]{:S(2)}, u32[]{:S(2)}) collective-permute-start(bf16[144,1152]{1,0:T(8,128)(2,1)S(1)} %copy-done.6), channel_id=1, source_target_pairs={{0,2},{1,3},{2,0},{3,1},{4,6},{5,7},{6,4},{7,5},{8,12},{9,13},{10,... | collective-permute-start | bytes 995336 | tf_op jit(solution)/shard_map/ppermute | solution.py:470
  27.2 14.5 %collective-permute-start.16 = (bf16[144,1152]{1,0:T(8,128)(2,1)S(1)}, bf16[144,1152]{1,0:T(8,128)(2,1)S(1)}, u32[]{:S(2)}, u32[]{:S(2)}) collective-permute-start(bf16[144,1152]{1,0:T(8,128)(2,1)S(1)} %copy-done.7), channel_id=1, source_target_pairs={{0,2},{1,3},{2,0},{3,1},{4,6},{5,7},{6,4},{7,5},{8,12},{9,13},{10,... | collective-permute-start | bytes 995336 | tf_op jit(solution)/shard_map/ppermute | solution.py:470
  29.7 13.7 %collective-permute-start.15 = (bf16[288,1152]{1,0:T(8,128)(2,1)}, bf16[288,1152]{1,0:T(8,128)(2,1)S(1)}, u32[]{:S(2)}, u32[]{:S(2)}) collective-permute-start(bf16[288,1152]{1,0:T(8,128)(2,1)} %collective-permute-done.refs_7_), channel_id=1, source_target_pairs={{0,1},{1,0},{2,3},{3,2},{4,5},{5,4},{6,7},{7,6},{8,9},{9,8},{10,11... | collective-permute-start | bytes 1990664 | tf_op jit(solution)/shard_map/ppermute | solution.py:462
  41.7 2.1 %collective-permute-start.17 = (bf16[288,1152]{1,0:T(8,128)(2,1)S(1)}, bf16[288,1152]{1,0:T(8,128)(2,1)S(1)}, u32[]{:S(2)}, u32[]{:S(2)}) collective-permute-start(bf16[288,1152]{1,0:T(8,128)(2,1)S(1)} %collective-permute-done.13.refs_8_), channel_id=1, source_target_pairs={{0,1},{1,0},{2,3},{3,2},{4,5},{5,4},{6,7},{7,6},{8,9},{9,8},{10,11... | collective-permute-start | bytes 1990664 | tf_op jit(solution)/shard_map/ppermute | solution.py:462
  41.8 3.1 %collective-permute-start.18 = (bf16[288,1152]{1,0:T(8,128)(2,1)S(1)}, bf16[288,1152]{1,0:T(8,128)(2,1)S(1)}, u32[]{:S(2)}, u32[]{:S(2)}) collective-permute-start(bf16[288,1152]{1,0:T(8,128)(2,1)S(1)} %collective-permute-done.14.refs_9_), channel_id=1, source_target_pairs={{0,1},{1,0},{2,3},{3,2},{4,5},{5,4},{6,7},{7,6},{8,9},{9,8},{10,11... | collective-permute-start | bytes 1990664 | tf_op jit(solution)/shard_map/ppermute | solution.py:462
  42.3 9.8 %collective-permute-start.12 = (bf16[144,1152]{1,0:T(8,128)(2,1)S(1)}, bf16[144,1152]{1,0:T(8,128)(2,1)S(1)}, u32[]{:S(2)}, u32[]{:S(2)}) collective-permute-start(bf16[144,1152]{1,0:T(8,128)(2,1)S(1)} %collective-permute-done.10.refs_3_), channel_id=1, source_target_pairs={{0,4},{1,5},{2,6},{3,7},{4,0},{5,1},{6,2},{7,3},{8,10},{9,11},{10,... | collective-permute-start | bytes 995336 | tf_op jit(solution)/shard_map/ppermute | solution.py:470
  42.9 9.5 %collective-permute-start.11 = (bf16[144,1152]{1,0:T(8,128)(2,1)S(1)}, bf16[144,1152]{1,0:T(8,128)(2,1)S(1)}, u32[]{:S(2)}, u32[]{:S(2)}) collective-permute-start(bf16[144,1152]{1,0:T(8,128)(2,1)S(1)} %slice.3), channel_id=1, source_target_pairs={{0,2},{1,3},{2,0},{3,1},{4,6},{5,7},{6,4},{7,5},{8,12},{9,13},{10,... | collective-permute-start | bytes 995336 | tf_op jit(solution)/shard_map/ppermute | solution.py:470
  43.4 9.5 %collective-permute-start.19 = (bf16[288,1152]{1,0:T(8,128)(2,1)}, bf16[288,1152]{1,0:T(8,128)(2,1)S(1)}, u32[]{:S(2)}, u32[]{:S(2)}) collective-permute-start(bf16[288,1152]{1,0:T(8,128)(2,1)} %collective-permute-done.1.refs_1_), channel_id=1, source_target_pairs={{0,1},{1,0},{2,3},{3,2},{4,5},{5,4},{6,7},{7,6},{8,9},{9,8},{10,11... | collective-permute-start | bytes 1990664 | tf_op jit(solution)/shard_map/ppermute | solution.py:462
  43.9 9.0 %collective-permute-start.21 = (bf16[144,1152]{1,0:T(8,128)(2,1)S(1)}, bf16[144,1152]{1,0:T(8,128)(2,1)S(1)}, u32[]{:S(2)}, u32[]{:S(2)}) collective-permute-start(bf16[144,1152]{1,0:T(8,128)(2,1)S(1)} %collective-permute-done.10.refs_3_), channel_id=1, source_target_pairs={{0,1},{1,0},{2,3},{3,2},{4,5},{5,4},{6,7},{7,6},{8,9},{9,8},{10,11... | collective-permute-start | bytes 995336 | tf_op jit(solution)/shard_map/ppermute | solution.py:462
  44.8 8.1 %collective-permute-start.20 = (bf16[144,1152]{1,0:T(8,128)(2,1)S(1)}, bf16[144,1152]{1,0:T(8,128)(2,1)S(1)}, u32[]{:S(2)}, u32[]{:S(2)}) collective-permute-start(bf16[144,1152]{1,0:T(8,128)(2,1)S(1)} %collective-permute-done.16.refs_2_), channel_id=1, source_target_pairs={{0,1},{1,0},{2,3},{3,2},{4,5},{5,4},{6,7},{7,6},{8,9},{9,8},{10,11... | collective-permute-start | bytes 995336 | tf_op jit(solution)/shard_map/ppermute | solution.py:462
  52.4 1.6 %collective-permute-start.22 = (bf16[144,1152]{1,0:T(8,128)(2,1)S(1)}, bf16[144,1152]{1,0:T(8,128)(2,1)S(1)}, u32[]{:S(2)}, u32[]{:S(2)}) collective-permute-start(bf16[144,1152]{1,0:T(8,128)(2,1)S(1)} %collective-permute-done.11.refs_4_), channel_id=1, source_target_pairs={{0,1},{1,0},{2,3},{3,2},{4,5},{5,4},{6,7},{7,6},{8,9},{9,8},{10,11... | collective-permute-start | bytes 995336 | tf_op jit(solution)/shard_map/ppermute | solution.py:462
  52.4 2.1 %collective-permute-start.23 = (bf16[144,1152]{1,0:T(8,128)(2,1)S(1)}, bf16[144,1152]{1,0:T(8,128)(2,1)S(1)}, u32[]{:S(2)}, u32[]{:S(2)}) collective-permute-start(bf16[144,1152]{1,0:T(8,128)(2,1)S(1)} %collective-permute-done.12.refs_5_), channel_id=1, source_target_pairs={{0,1},{1,0},{2,3},{3,2},{4,5},{5,4},{6,7},{7,6},{8,9},{9,8},{10,11... | collective-permute-start | bytes 995336 | tf_op jit(solution)/shard_map/ppermute | solution.py:462
  62.9 1.4 %collective-permute-start.24 = (f32[32,1152]{1,0:T(8,128)S(1)}, f32[32,1152]{1,0:T(8,128)S(1)}, u32[]{:S(2)}, u32[]{:S(2)}) collective-permute-start(f32[32,1152]{1,0:T(8,128)S(1)} %get-tuple-element.68), channel_id=1, source_target_pairs={{0,1},{1,0},{2,3},{3,2},{4,5},{5,4},{6,7},{7,6},{8,9},{9,8},{10,11... | collective-permute-start | bytes 442376 | tf_op jit(solution)/shard_map/ppermute | solution.py:462
  64.4 6.7 %collective-permute-start.25 = (bf16[32,1152]{1,0:T(8,128)(2,1)S(1)}, bf16[32,1152]{1,0:T(8,128)(2,1)S(1)}, u32[]{:S(2)}, u32[]{:S(2)}) collective-permute-start(bf16[32,1152]{1,0:T(8,128)(2,1)S(1)} %add_convert_fusion.1), channel_id=1, source_target_pairs={{0,2},{1,3},{2,0},{3,1},{4,6},{5,7},{6,4},{7,5},{8,10},{9,11},{10,... | collective-permute-start | bytes 221192 | tf_op jit(solution)/shard_map/ppermute | solution.py:462
  65.0 6.1 %collective-permute-start.26 = (bf16[32,1152]{1,0:T(8,128)(2,1)S(1)}, bf16[32,1152]{1,0:T(8,128)(2,1)S(1)}, u32[]{:S(2)}, u32[]{:S(2)}) collective-permute-start(bf16[32,1152]{1,0:T(8,128)(2,1)S(1)} %add_convert_fusion.1), channel_id=1, source_target_pairs={{0,4},{1,5},{2,6},{3,7},{4,0},{5,1},{6,2},{7,3},{8,12},{9,13},{10,... | collective-permute-start | bytes 221192 | tf_op jit(solution)/shard_map/ppermute | solution.py:462
  66.4 5.3 %collective-permute-start.27 = (bf16[32,1152]{1,0:T(8,128)(2,1)S(1)}, bf16[32,1152]{1,0:T(8,128)(2,1)S(1)}, u32[]{:S(2)}, u32[]{:S(2)}) collective-permute-start(bf16[32,1152]{1,0:T(8,128)(2,1)S(1)} %add_convert_fusion.1), channel_id=1, source_target_pairs={{0,6},{1,7},{2,4},{3,5},{4,2},{5,3},{6,0},{7,1},{8,14},{9,15},{10,... | collective-permute-start | bytes 221192 | tf_op jit(solution)/shard_map/ppermute | solution.py:462
  71.7 7.9 %collective-permute-start.28 = (bf16[32,1152]{1,0:T(8,128)(2,1)S(1)}, bf16[32,1152]{1,0:T(8,128)(2,1)S(1)}, u32[]{:S(2)}, u32[]{:S(2)}) collective-permute-start(bf16[32,1152]{1,0:T(8,128)(2,1)S(1)} %add_convert_fusion.refs_0_), channel_id=1, source_target_pairs={{0,8},{8,0},{16,24},{24,16},{1,9},{9,1},{17,25},{25,17},{2,10},{10... | collective-permute-start | bytes 221192 | tf_op jit(solution)/shard_map/ppermute | solution.py:476
  72.8 6.9 %collective-permute-start.29 = (bf16[32,1152]{1,0:T(8,128)(2,1)S(1)}, bf16[32,1152]{1,0:T(8,128)(2,1)S(1)}, u32[]{:S(2)}, u32[]{:S(2)}) collective-permute-start(bf16[32,1152]{1,0:T(8,128)(2,1)S(1)} %add_convert_fusion.refs_0_), channel_id=1, source_target_pairs={{0,16},{8,24},{16,0},{24,8},{1,17},{9,25},{17,1},{25,9},{2,18},{10... | collective-permute-start | bytes 221192 | tf_op jit(solution)/shard_map/ppermute | solution.py:476
  74.9 6.2 %collective-permute-start.30 = (bf16[32,1152]{1,0:T(8,128)(2,1)S(1)}, bf16[32,1152]{1,0:T(8,128)(2,1)S(1)}, u32[]{:S(2)}, u32[]{:S(2)}) collective-permute-start(bf16[32,1152]{1,0:T(8,128)(2,1)S(1)} %add_convert_fusion.refs_0_), channel_id=1, source_target_pairs={{0,24},{8,16},{16,8},{24,0},{1,25},{9,17},{17,9},{25,1},{2,26},{10... | collective-permute-start | bytes 221192 | tf_op jit(solution)/shard_map/ppermute | solution.py:476
  76.2 5.5 %collective-permute-start.31 = (bf16[32,1152]{1,0:T(8,128)(2,1)S(1)}, bf16[32,1152]{1,0:T(8,128)(2,1)S(1)}, u32[]{:S(2)}, u32[]{:S(2)}) collective-permute-start(bf16[32,1152]{1,0:T(8,128)(2,1)S(1)} %add_convert_fusion.refs_0_), channel_id=1, source_target_pairs={{0,1},{1,0},{2,3},{3,2},{4,5},{5,4},{6,7},{7,6},{8,9},{9,8},{10,11... | collective-permute-start | bytes 221192 | tf_op jit(solution)/shard_map/ppermute | solution.py:462
  (11 other events, 165.1 us)

commit v4 on v3

--- a/solution.py
+++ b/solution.py
@@ -152,6 +152,10 @@
     slope_out[...] = sigmoid * (1.0 + pre_act * (1.0 - sigmoid))
     own_hidden_out[...] = project(hidden, select).astype(jnp.bfloat16)
     encoded_out[...] = project(hidden[:own_rows], second_weight[...]).astype(jnp.bfloat16)
+
+
+def query_kernel(token_ref, weight_ref, out_ref):
+    out_ref[...] = project(token_ref[...], weight_ref[...]).astype(jnp.bfloat16)
 
 
 def head_parts(slots):
@@ -491,11 +495,21 @@
         return functools.reduce(jnp.add, [part.astype(jnp.float32) for part in parts])
 
     def project_queries(tokens_in):
-        return jnp.dot(
-            tokens_in.reshape(images * tokens, features),
-            query_weight,
-            preferred_element_type=jnp.float32,
-        ).astype(jnp.bfloat16)
+        return pl.pallas_call(
+            query_kernel,
+            out_shape=shape((images * tokens, features), jnp.bfloat16),
+            grid=(images * tokens // 256,),
+            in_specs=[
+                pl.BlockSpec((256, features), lambda t: (t, 0)),
+                pl.BlockSpec((features, features), lambda t: (0, 0)),
+            ],
+            out_specs=pl.BlockSpec((256, features), lambda t: (t, 0)),
+            compiler_params=vmem(12),
+            cost_estimate=pl.CostEstimate(
+                flops=3 * 10**9, bytes_accessed=8 * 10**6, transcendentals=0
+            ),
+            name="queries",
+        )(tokens_in.reshape(images * tokens, features), query_weight)
 
     phrase_rows = phrases.reshape(rows, features)
     bias = visible_bias(region_first, region_last, phrase_counts, shard * tokens, tokens)
@@ -520,33 +534,29 @@
         own_half = lax.dynamic_slice_in_dim(
             after(phrase_rows, encoder_own, projector_own), core * half, half, 0
         )
-        queries = project_queries(after(latents, encoder_own, projector_own))
         plane_phrases = plane_peers(own_half)
-        far_phrases = [swap(part, 1) for part in after_all(plane_phrases, queries)]
-        encoder_next, projector_near, far_phrases, queries, bias, place = (
-            lax.optimization_barrier(
-                (encoder_near, projector_near, far_phrases, queries, bias, place)
-            )
+        far_phrases = [swap(part, 1) for part in plane_phrases]
+        encoder_next, projector_near, far_phrases, bias, place = lax.optimization_barrier(
+            (encoder_near, projector_near, far_phrases, bias, place)
         )
-        key_third, value_third = [
-            swap_by_plane(block, 1, 2) for block in (key_weight, value_weight)
-        ]
+        projector_third = swap_by_plane(projector, 1, 2)
         encoder_far = swap_by_plane(encoder_next, 2, 1)
         encoder_third = plane_swap(encoder_next, 1)
         key_near = projector_near[:shard_rows]
+        queries = project_queries(after(latents, key_near))
         pairs = [swap(after(encoder_next, key_near), 1), swap(projector_near, 1)]
-        key_far = swap_by_plane(after(key_near, value_third), 1, 2)
-        value_far = swap_by_plane(value_third, 2, 1)
+        key_far = swap_by_plane(after(key_near, projector_third), 1, 2)
+        value_far = swap_by_plane(projector_third[shard_rows:], 2, 1)
         arrays = [encoder, encoder_near, projector, projector_near]
-        arrays += [encoder_far, encoder_third, key_third, value_third, key_far, value_far]
+        arrays += [encoder_far, encoder_third, projector_third, key_far, value_far]
         arrays += [encoder_own, pairs[0], projector_own, pairs[1]]
-        early = after_all([encoder_far, encoder_third], key_third, value_third)
-        arrays += [swap(block, 1) for block in (*early, key_third, value_third)]
+        early = after_all([encoder_far, encoder_third], projector_third, queries)
+        arrays += [swap(block, 1) for block in (*early, projector_third)]
         layout = {
             "first": (0, [(0, 0), (1, 0), (5, 0), (4, 0)]),
             "second": (0, [(i, shard_rows) for i in (0, 1, 5, 4)]),
-            "key": (1, [(2, 0), (3, 0), (6, 0), (8, 0)]),
-            "value": (1, [(2, shard_rows), (3, shard_rows), (7, 0), (9, 0)]),
+            "key": (1, [(2, 0), (3, 0), (6, 0), (7, 0)]),
+            "value": (1, [(2, shard_rows), (3, shard_rows), (6, shard_rows), (8, 0)]),
         }
     else:
         own_half = lax.dynamic_slice_in_dim(phrase_rows, core * half, half, 0)
@@ -564,7 +574,7 @@
                 ("value", chips, shard_rows),
             )
         }
-    near_count = chips == 4 and 10 or len(arrays) // 2
+    near_count = chips == 4 and 9 or len(arrays) // 2
     for name, (scheme, blocks) in layout.items():
         layout[name] = (scheme, blocks + [(near_count + i, offset) for i, offset in blocks])
 
@@ -599,8 +609,8 @@
     )(place, phrase_rows, *plane_phrases, *far_phrases, *encoder_arrays)
     grads = out_grad.reshape(images * tokens, features)
     if chips == 4:
-        *late, encoded = lax.optimization_barrier((*arrays[8:10], encoded))
-        arrays[8:10] = late
+        *late, encoded = lax.optimization_barrier((*arrays[7:9], encoded))
+        arrays[7:9] = late
         arrays += [swap(block, 1) for block in late]
     projector_arrays, projector_layout = weights("key", "value")
     key_rows, score_grad, grad_mine, grad_other = pl.pallas_call(

time: 87.5 us -> 86.5 us (0.989)
  matrix products: 5.75 us -> 0 us
  local copies, waits for them, and re-layouts: 1.94 us -> 4.38 us
  Pallas kernels: 24.9 us -> 27.3 us
    ppermute x7, waiting for transfers between devices: 1.76 us -> 9.25 us  [plane_swap(): return lax.ppermute(array, 'dp', [(i, i ^ distance) for i in range(planes)])]
    ppermute x7 -> x6, waiting for transfers between devices: 17.9 us -> 11.2 us  [swap_by_plane(): return lax.ppermute(array, ('dp', 'seq'), pairs)]
    dot_general x1 -> x0, matrix products: 5.75 us -> none  [project_queries(): jnp.dot(tokens_in.reshape(images * tokens, features), query_weight, prefe...]
    pallas_call x0 -> x1, Pallas kernels: none -> 4.19 us  [project_queries(): pl.pallas_call(query_kernel, out_shape=shape((images * tokens, features),...]
    unnamed x16 -> x14, local copies, waits for them, and re-layouts: 0.04 us -> 3.43 us
    slice x1, local copies, waits for them, and re-layouts: 1 us -> 0.03 us  [tiled(): key_near = projector_near[:shard_rows]]
    ppermute x21 -> x20, starting transfers between devices: 6.66 us -> 6.08 us  [swap(): lax.ppermute(array, 'seq', [(i, i ^ distance) for i in range(shards)])]
    ppermute x7 -> x6, starting transfers between devices: 9.21 us -> 8.96 us  [swap_by_plane(): return lax.ppermute(array, ('dp', 'seq'), pairs)]
  transfers between devices with their start and end apart: 35 -> 33, of which waited for: 17 -> 19; matrix products, arithmetic and copies ran while one was open for 11% -> 3% of each run, Pallas kernels for 11% -> 15%
where the time goes in v4:
time: 86.5 us; the launch traced here: 86.2 us
  Pallas kernels  27.3 us (32%)
  waiting for transfers between devices  26.4 us (31%)
  starting transfers between devices  25.5 us (29%)
  local copies, waits for them, and re-layouts  4.38 us (5%)
  other arithmetic  1.67 us (2%)
  between operations  1.01 us (1%)
    ppermute x6, waiting for transfers between devices, swap_by_plane(): return lax.ppermute(array, ('dp', 'seq'), pairs)  11.2 us
    ppermute x7, starting transfers between devices, plane_swap(): return lax.ppermute(array, 'dp', [(i, i ^ distance) for i in range(planes)])  10.4 us
    ppermute x7, waiting for transfers between devices, plane_swap(): return lax.ppermute(array, 'dp', [(i, i ^ distance) for i in range(planes)])  9.25 us
    ppermute x6, starting transfers between devices, swap_by_plane(): return lax.ppermute(array, ('dp', 'seq'), pairs)  8.96 us
    pallas_call x1, Pallas kernels, tiled(): pl.pallas_call(functools.partial(attend_kernel, chips, images, projector_...  7.54 us
    pallas_call x2, Pallas kernels, latent_part(): pl.pallas_call(kernel if whole is None else lambda _, *refs: kernel(*refs...  6.33 us
    ppermute x20, starting transfers between devices, swap(): lax.ppermute(array, 'seq', [(i, i ^ distance) for i in range(shards)])  6.08 us
    ppermute x20, waiting for transfers between devices, swap(): lax.ppermute(array, 'seq', [(i, i ^ distance) for i in range(shards)])  5.92 us
  transfers between devices with their start and end apart: 33, of which 19 were waited for; matrix products, arithmetic and copies ran while one was open for 3% of the time, Pallas kernels for 15%

profile of v4, /device:TPU:0, one launch (start us, length us, event | category | flops | bytes accessed | tf_op | source)
XLA Modules:
  0.0 86.2 jit_solution(13041183525977121231)
XLA Ops:
  0.6 2.4 %join.1 = (bf16[288,1152]{1,0:T(8,128)(2,1)}, bf16[288,1152]{1,0:T(8,128)(2,1)}) custom-call(bf16[144,1152]{1,0:T(8,128)(2,1)} %refs_0_.1, bf16[144,1152]{1,0:T(8,128)(2,1)} %refs_1_.1, bf16[144,1152]{1,0:T(8,128)(2,1)} %refs_2_.2, bf16[144,1152]{1,0:T(8,128)(2,1)} %refs_3_.1), custom_call_target="tpu_custom_call" | custom-call | tf_op jit(solution)/shard_map/join/pallas_call | solution.py:519
  3.5 2.9 %collective-permute-start = (bf16[288,1152]{1,0:T(8,128)(2,1)}, bf16[288,1152]{1,0:T(8,128)(2,1)S(1)}, u32[]{:S(2)}, u32[]{:S(2)}) collective-permute-start(bf16[288,1152]{1,0:T(8,128)(2,1)} %get-tuple-element.40.refs_6_), channel_id=1, source_target_pairs={{0,2},{1,3},{2,0},{3,1},{4,6},{5,7},{6,4},{7,5},{8,12},{9,13},{10,... | collective-permute-start | bytes 1990664 | tf_op jit(solution)/shard_map/ppermute | solution.py:474
  6.5 1.5 %collective-permute-start.1 = (bf16[288,1152]{1,0:T(8,128)(2,1)}, bf16[288,1152]{1,0:T(8,128)(2,1)S(1)}, u32[]{:S(2)}, u32[]{:S(2)}) collective-permute-start(bf16[288,1152]{1,0:T(8,128)(2,1)} %get-tuple-element.41.refs_0_), channel_id=1, source_target_pairs={{0,4},{1,5},{2,6},{3,7},{4,0},{5,1},{6,2},{7,3},{8,10},{9,11},{10,... | collective-permute-start | bytes 1990664 | tf_op jit(solution)/shard_map/ppermute | solution.py:474
  8.7 0.9 %constant_dynamic-slice_fusion = bf16[32,1152]{1,0:T(8,128)(2,1)S(1)} fusion(bf16[64,1152]{1,0:T(8,128)(2,1)} %bitcast.8, s32[]{:T(128)S(6)} %select_n.32), kind=kLoop, calls=%fused_computation.14 | loop fusion | bytes 147460 | tf_op jit(solution)/shard_map/dynamic_slice | solution.py:534
  9.6 1.6 %collective-permute-start.4 = (bf16[32,1152]{1,0:T(8,128)(2,1)S(1)}, bf16[32,1152]{1,0:T(8,128)(2,1)S(1)}, u32[]{:S(2)}, u32[]{:S(2)}) collective-permute-start(bf16[32,1152]{1,0:T(8,128)(2,1)S(1)} %constant_dynamic-slice_fusion), channel_id=1, source_target_pairs={{0,8},{8,0},{16,24},{24,16},{1,9},{9,1},{17,25},{25,17},{2,10},{10... | collective-permute-start | bytes 221192 | tf_op jit(solution)/shard_map/ppermute | solution.py:480
  11.2 2.6 %collective-permute-start.6 = (bf16[32,1152]{1,0:T(8,128)(2,1)S(1)}, bf16[32,1152]{1,0:T(8,128)(2,1)S(1)}, u32[]{:S(2)}, u32[]{:S(2)}) collective-permute-start(bf16[32,1152]{1,0:T(8,128)(2,1)S(1)} %constant_dynamic-slice_fusion), channel_id=1, source_target_pairs={{0,16},{8,24},{16,0},{24,8},{1,17},{9,25},{17,1},{25,9},{2,18},{10... | collective-permute-start | bytes 221192 | tf_op jit(solution)/shard_map/ppermute | solution.py:480
  14.9 3.7 %collective-permute-done.6.refs_1_ = bf16[32,1152]{1,0:T(8,128)(2,1)S(1)} collective-permute-done((bf16[32,1152]{1,0:T(8,128)(2,1)S(1)}, bf16[32,1152]{1,0:T(8,128)(2,1)S(1)}, u32[]{:S(2)}, u32[]{:S(2)}) %collective-permute-start.6) | collective-permute-done | bytes 73760 | tf_op jit(solution)/shard_map/ppermute | solution.py:480
  18.6 1.5 %collective-permute-done.8.refs_2_ = bf16[32,1152]{1,0:T(8,128)(2,1)S(1)} collective-permute-done((bf16[32,1152]{1,0:T(8,128)(2,1)S(1)}, bf16[32,1152]{1,0:T(8,128)(2,1)S(1)}, u32[]{:S(2)}, u32[]{:S(2)}) %collective-permute-start.8) | collective-permute-done | bytes 73760 | tf_op jit(solution)/shard_map/ppermute | solution.py:480
  20.1 1.6 %collective-permute-done.refs_7_ = bf16[288,1152]{1,0:T(8,128)(2,1)S(1)} collective-permute-done((bf16[288,1152]{1,0:T(8,128)(2,1)}, bf16[288,1152]{1,0:T(8,128)(2,1)S(1)}, u32[]{:S(2)}, u32[]{:S(2)}) %collective-permute-start) | collective-permute-done | bytes 663584 | tf_op jit(solution)/shard_map/ppermute | solution.py:474
  21.7 1.7 %collective-permute-start.10 = (bf16[288,1152]{1,0:T(8,128)(2,1)}, bf16[288,1152]{1,0:T(8,128)(2,1)S(1)}, u32[]{:S(2)}, u32[]{:S(2)}) collective-permute-start(bf16[288,1152]{1,0:T(8,128)(2,1)} %get-tuple-element.41.refs_0_), channel_id=1, source_target_pairs={{0,2},{1,3},{2,0},{3,1},{4,6},{5,7},{6,4},{7,5},{8,12},{9,13},{10,... | collective-permute-start | bytes 1990664 | tf_op jit(solution)/shard_map/ppermute | solution.py:474
  23.5 1.6 %collective-permute-start.13 = (bf16[288,1152]{1,0:T(8,128)(2,1)S(1)}, bf16[288,1152]{1,0:T(8,128)(2,1)S(1)}, u32[]{:S(2)}, u32[]{:S(2)}) collective-permute-start(bf16[288,1152]{1,0:T(8,128)(2,1)S(1)} %collective-permute-done.refs_7_), channel_id=1, source_target_pairs={{0,4},{1,5},{2,6},{3,7},{4,0},{5,1},{6,2},{7,3},{8,10},{9,11},{10,... | collective-permute-start | bytes 1990664 | tf_op jit(solution)/shard_map/ppermute | solution.py:474
  25.1 1.6 %collective-permute-start.14 = (bf16[288,1152]{1,0:T(8,128)(2,1)S(1)}, bf16[288,1152]{1,0:T(8,128)(2,1)S(1)}, u32[]{:S(2)}, u32[]{:S(2)}) collective-permute-start(bf16[288,1152]{1,0:T(8,128)(2,1)S(1)} %collective-permute-done.refs_7_), channel_id=1, source_target_pairs={{0,8},{8,0},{16,24},{24,16},{1,9},{9,1},{17,25},{25,17},{2,10},{10... | collective-permute-start | bytes 1990664 | tf_op jit(solution)/shard_map/ppermute | solution.py:480
  26.8 1.7 %copy-done.2 = bf16[1152,1152]{1,0:T(8,128)(2,1)S(1)} copy-done((bf16[1152,1152]{1,0:T(8,128)(2,1)S(1)}, bf16[1152,1152]{1,0:T(8,128)(2,1)}, u32[]{:S(2)}) %copy-start.2) | copy-done | bytes 2654232
  28.5 1.7 %copy-done.4 = bf16[2,512,1152]{2,1,0:T(8,128)(2,1)S(1)} copy-done((bf16[2,512,1152]{2,1,0:T(8,128)(2,1)S(1)}, bf16[2,512,1152]{2,1,0:T(8,128)(2,1)}, u32[]{:S(2)}) %copy-start.4) | copy-done | bytes 2359320
  30.2 4.2 %queries.1.refs_10_ = bf16[1024,1152]{1,0:T(8,128)(2,1)S(1)} custom-call(bf16[1024,1152]{1,0:T(8,128)(2,1)S(1)} %bitcast.10, bf16[1152,1152]{1,0:T(8,128)(2,1)S(1)} %copy-done.2), custom_call_target="tpu_custom_call" | custom-call | flops 3000000000 | bytes 8000000 | tf_op jit(solution)/shard_map/queries/pallas_call | solution.py:498
  34.4 3.8 %collective-permute-done.10.refs_2_ = bf16[288,1152]{1,0:T(8,128)(2,1)S(1)} collective-permute-done((bf16[288,1152]{1,0:T(8,128)(2,1)}, bf16[288,1152]{1,0:T(8,128)(2,1)S(1)}, u32[]{:S(2)}, u32[]{:S(2)}) %collective-permute-start.10) | collective-permute-done | bytes 663584 | tf_op jit(solution)/shard_map/ppermute | solution.py:474
  38.2 1.0 %collective-permute-done.13.refs_8_ = bf16[288,1152]{1,0:T(8,128)(2,1)S(1)} collective-permute-done((bf16[288,1152]{1,0:T(8,128)(2,1)S(1)}, bf16[288,1152]{1,0:T(8,128)(2,1)S(1)}, u32[]{:S(2)}, u32[]{:S(2)}) %collective-permute-start.13) | collective-permute-done | bytes 663584 | tf_op jit(solution)/shard_map/ppermute | solution.py:474
  39.3 1.2 %collective-permute-done.14.refs_9_ = bf16[288,1152]{1,0:T(8,128)(2,1)S(1)} collective-permute-done((bf16[288,1152]{1,0:T(8,128)(2,1)S(1)}, bf16[288,1152]{1,0:T(8,128)(2,1)S(1)}, u32[]{:S(2)}, u32[]{:S(2)}) %collective-permute-start.14) | collective-permute-done | bytes 663584 | tf_op jit(solution)/shard_map/ppermute | solution.py:480
  43.6 2.7 %encode.1 = (bf16[64,1152]{1,0:T(8,128)(2,1)S(1)}, f32[256,1152]{1,0:T(8,128)S(1)}, bf16[256,144]{1,0:T(8,128)(2,1)S(1)}, bf16[256,144]{1,0:T(8,128)(2,1)S(1)}, ...) custom-call(s32[3]{0:T(128)S(1)} %pad_add_fusion.place_ref, bf16[64,1152]{1,0:T(8,128)(2,1)S(1)} %bitcast.9, ...), custom_call_target="tpu_custom_call" | custom-call | flops 1000000 | bytes 10000 | tf_op jit(solution)/shard_map/encode/pallas_call | solution.py:591
  46.3 4.5 %collective-permute-done.12.refs_4_ = bf16[144,1152]{1,0:T(8,128)(2,1)S(1)} collective-permute-done((bf16[144,1152]{1,0:T(8,128)(2,1)S(1)}, bf16[144,1152]{1,0:T(8,128)(2,1)S(1)}, u32[]{:S(2)}, u32[]{:S(2)}) %collective-permute-start.12) | collective-permute-done | bytes 331808 | tf_op jit(solution)/shard_map/ppermute | solution.py:474
  51.6 1.1 %collective-permute-done.20.refs_8_ = bf16[144,1152]{1,0:T(8,128)(2,1)S(1)} collective-permute-done((bf16[144,1152]{1,0:T(8,128)(2,1)S(1)}, bf16[144,1152]{1,0:T(8,128)(2,1)S(1)}, u32[]{:S(2)}, u32[]{:S(2)}) %collective-permute-start.20) | collective-permute-done | bytes 331808 | tf_op jit(solution)/shard_map/ppermute | solution.py:466
  53.2 7.5 %attend.1 = (bf16[64,1152]{1,0:T(8,128)(2,1)S(1)}, bf16[2,512,512]{2,1,0:T(8,128)(2,1)S(1)}, f32[32,1152]{1,0:T(8,128)S(1)}, f32[32,1152]{1,0:T(8,128)S(1)}) custom-call(s32[3]{0:T(128)S(1)} %pad_add_fusion.place_ref, bf16[64,1152]{1,0:T(8,128)(2,1)S(1)} %get-tuple-element.55.encoded_ref, bf16[288,1152]{1,0:T(8,128)(2,1)S(1)} %copy-done.6, ...), custom_call_target="tpu_custom_call" | custom-call | flops 10000000000 | bytes 12000000 | tf_op jit(solution)/shard_map/attend/pallas_call | solution.py:616
  60.9 1.2 %collective-permute-done.22 = f32[32,1152]{1,0:T(8,128)S(1)} collective-permute-done((f32[32,1152]{1,0:T(8,128)S(1)}, f32[32,1152]{1,0:T(8,128)S(1)}, u32[]{:S(2)}, u32[]{:S(2)}) %collective-permute-start.22) | collective-permute-done | bytes 147488 | tf_op jit(solution)/shard_map/ppermute | solution.py:466
  62.8 1.5 %collective-permute-start.24 = (bf16[32,1152]{1,0:T(8,128)(2,1)S(1)}, bf16[32,1152]{1,0:T(8,128)(2,1)S(1)}, u32[]{:S(2)}, u32[]{:S(2)}) collective-permute-start(bf16[32,1152]{1,0:T(8,128)(2,1)S(1)} %add_convert_fusion.1), channel_id=1, source_target_pairs={{0,4},{1,5},{2,6},{3,7},{4,0},{5,1},{6,2},{7,3},{8,12},{9,13},{10,... | collective-permute-start | bytes 221192 | tf_op jit(solution)/shard_map/ppermute | solution.py:466
  64.3 1.4 %collective-permute-start.25 = (bf16[32,1152]{1,0:T(8,128)(2,1)S(1)}, bf16[32,1152]{1,0:T(8,128)(2,1)S(1)}, u32[]{:S(2)}, u32[]{:S(2)}) collective-permute-start(bf16[32,1152]{1,0:T(8,128)(2,1)S(1)} %add_convert_fusion.1), channel_id=1, source_target_pairs={{0,6},{1,7},{2,4},{3,5},{4,2},{5,3},{6,0},{7,1},{8,14},{9,15},{10,... | collective-permute-start | bytes 221192 | tf_op jit(solution)/shard_map/ppermute | solution.py:466
  65.7 3.2 %latent.2._ = bf16[1024,1152]{1,0:T(8,128)(2,1)} custom-call(bf16[2,512,512]{2,1,0:T(8,128)(2,1)S(1)} %get-tuple-element.61.score_ref.refs_0_, bf16[64,1152]{1,0:T(8,128)(2,1)S(1)} %get-tuple-element.62.key_ref.refs_1_, bf16[1152,1152]{1,0:T(8,128)(2,1)S(1)} %copy-done.3), custom_call_target="tpu_custom_call" | custom-call | flops 3000000000 | bytes 4000000 | tf_op jit(solution)/shard_map/latent/pallas_call | solution.py:644
  69.6 1.8 %collective-permute-start.26 = (bf16[32,1152]{1,0:T(8,128)(2,1)S(1)}, bf16[32,1152]{1,0:T(8,128)(2,1)S(1)}, u32[]{:S(2)}, u32[]{:S(2)}) collective-permute-start(bf16[32,1152]{1,0:T(8,128)(2,1)S(1)} %add_convert_fusion.refs_0_), channel_id=1, source_target_pairs={{0,8},{8,0},{16,24},{24,16},{1,9},{9,1},{17,25},{25,17},{2,10},{10... | collective-permute-start | bytes 221192 | tf_op jit(solution)/shard_map/ppermute | solution.py:480
  71.4 2.6 %collective-permute-start.27 = (bf16[32,1152]{1,0:T(8,128)(2,1)S(1)}, bf16[32,1152]{1,0:T(8,128)(2,1)S(1)}, u32[]{:S(2)}, u32[]{:S(2)}) collective-permute-start(bf16[32,1152]{1,0:T(8,128)(2,1)S(1)} %add_convert_fusion.refs_0_), channel_id=1, source_target_pairs={{0,16},{8,24},{16,0},{24,8},{1,17},{9,25},{17,1},{25,9},{2,18},{10... | collective-permute-start | bytes 221192 | tf_op jit(solution)/shard_map/ppermute | solution.py:480
  74.1 3.2 %latent.3 = bf16[1024,1152]{1,0:T(8,128)(2,1)} custom-call(bf16[1024,1152]{1,0:T(8,128)(2,1)} %latent.2._, bf16[2,512,512]{2,1,0:T(8,128)(2,1)S(1)} %get-tuple-element.61.score_ref.refs_0_, bf16[64,1152]{1,0:T(8,128)(2,1)S(1)} %get-tuple-element.62.key_ref.refs_1_, bf16[1152,1152]{1,0:T(8,128)(2,1)S(1)} %copy-done.3), custom_call_target="tpu_custom_call", output_to_operand_aliasing={{}: (0, {})} | custom-call | flops 3000000000 | bytes 4000000 | tf_op jit(solution)/shard_map/latent/pallas_call | solution.py:644
  77.2 1.0 %collective-permute-done.27.refs_2_ = bf16[32,1152]{1,0:T(8,128)(2,1)S(1)} collective-permute-done((bf16[32,1152]{1,0:T(8,128)(2,1)S(1)}, bf16[32,1152]{1,0:T(8,128)(2,1)S(1)}, u32[]{:S(2)}, u32[]{:S(2)}) %collective-permute-start.27) | collective-permute-done | bytes 73760 | tf_op jit(solution)/shard_map/ppermute | solution.py:480
  78.2 1.9 %collective-permute-done.28.refs_3_ = bf16[32,1152]{1,0:T(8,128)(2,1)S(1)} collective-permute-done((bf16[32,1152]{1,0:T(8,128)(2,1)S(1)}, bf16[32,1152]{1,0:T(8,128)(2,1)S(1)}, u32[]{:S(2)}, u32[]{:S(2)}) %collective-permute-start.28) | collective-permute-done | bytes 73760 | tf_op jit(solution)/shard_map/ppermute | solution.py:480
  81.9 4.2 %weight_grads.1 = (f32[144,1152]{1,0:T(8,128)}, f32[144,1152]{1,0:T(8,128)}, bf16[64,1152]{1,0:T(8,128)(2,1)}) custom-call(s32[3]{0:T(128)S(1)} %pad_add_fusion.place_ref, bf16[32,1152]{1,0:T(8,128)(2,1)S(1)} %add_convert_fusion.refs_0_, bf16[32,1152]{1,0:T(8,128)(2,1)S(1)} %collective-permute-done.26.refs_1_, ...), custom_call_target="tpu_custom_call" | custom-call | tf_op jit(solution)/shard_map/weight_grads/pallas_call | solution.py:670
  (64 shorter events, 10.2 us)
Async XLA Ops:
  3.0 5.7 %collective-permute-start.3 = (bf16[288,1152]{1,0:T(8,128)(2,1)}, bf16[288,1152]{1,0:T(8,128)(2,1)S(1)}, u32[]{:S(2)}, u32[]{:S(2)}) collective-permute-start(bf16[288,1152]{1,0:T(8,128)(2,1)} %get-tuple-element.41.refs_0_), channel_id=1, source_target_pairs={{0,1},{1,0},{2,3},{3,2},{4,5},{5,4},{6,7},{7,6},{8,9},{9,8},{10,11... | collective-permute-start | bytes 1990664 | tf_op jit(solution)/shard_map/ppermute | solution.py:466
  3.5 5.3 %collective-permute-start.2 = (bf16[288,1152]{1,0:T(8,128)(2,1)}, bf16[288,1152]{1,0:T(8,128)(2,1)S(1)}, u32[]{:S(2)}, u32[]{:S(2)}) collective-permute-start(bf16[288,1152]{1,0:T(8,128)(2,1)} %get-tuple-element.40.refs_6_), channel_id=1, source_target_pairs={{0,1},{1,0},{2,3},{3,2},{4,5},{5,4},{6,7},{7,6},{8,9},{9,8},{10,11... | collective-permute-start | bytes 1990664 | tf_op jit(solution)/shard_map/ppermute | solution.py:466
  3.5 18.2 %collective-permute-start = (bf16[288,1152]{1,0:T(8,128)(2,1)}, bf16[288,1152]{1,0:T(8,128)(2,1)S(1)}, u32[]{:S(2)}, u32[]{:S(2)}) collective-permute-start(bf16[288,1152]{1,0:T(8,128)(2,1)} %get-tuple-element.40.refs_6_), channel_id=1, source_target_pairs={{0,2},{1,3},{2,0},{3,1},{4,6},{5,7},{6,4},{7,5},{8,12},{9,13},{10,... | collective-permute-start | bytes 1990664 | tf_op jit(solution)/shard_map/ppermute | solution.py:474
  6.5 17.0 %collective-permute-start.1 = (bf16[288,1152]{1,0:T(8,128)(2,1)}, bf16[288,1152]{1,0:T(8,128)(2,1)S(1)}, u32[]{:S(2)}, u32[]{:S(2)}) collective-permute-start(bf16[288,1152]{1,0:T(8,128)(2,1)} %get-tuple-element.41.refs_0_), channel_id=1, source_target_pairs={{0,4},{1,5},{2,6},{3,7},{4,0},{5,1},{6,2},{7,3},{8,10},{9,11},{10,... | collective-permute-start | bytes 1990664 | tf_op jit(solution)/shard_map/ppermute | solution.py:474
  9.6 5.2 %collective-permute-start.4 = (bf16[32,1152]{1,0:T(8,128)(2,1)S(1)}, bf16[32,1152]{1,0:T(8,128)(2,1)S(1)}, u32[]{:S(2)}, u32[]{:S(2)}) collective-permute-start(bf16[32,1152]{1,0:T(8,128)(2,1)S(1)} %constant_dynamic-slice_fusion), channel_id=1, source_target_pairs={{0,8},{8,0},{16,24},{24,16},{1,9},{9,1},{17,25},{25,17},{2,10},{10... | collective-permute-start | bytes 221192 | tf_op jit(solution)/shard_map/ppermute | solution.py:480
  11.2 7.4 %collective-permute-start.6 = (bf16[32,1152]{1,0:T(8,128)(2,1)S(1)}, bf16[32,1152]{1,0:T(8,128)(2,1)S(1)}, u32[]{:S(2)}, u32[]{:S(2)}) collective-permute-start(bf16[32,1152]{1,0:T(8,128)(2,1)S(1)} %constant_dynamic-slice_fusion), channel_id=1, source_target_pairs={{0,16},{8,24},{16,0},{24,8},{1,17},{9,25},{17,1},{25,9},{2,18},{10... | collective-permute-start | bytes 221192 | tf_op jit(solution)/shard_map/ppermute | solution.py:480
  13.8 6.3 %collective-permute-start.8 = (bf16[32,1152]{1,0:T(8,128)(2,1)S(1)}, bf16[32,1152]{1,0:T(8,128)(2,1)S(1)}, u32[]{:S(2)}, u32[]{:S(2)}) collective-permute-start(bf16[32,1152]{1,0:T(8,128)(2,1)S(1)} %constant_dynamic-slice_fusion), channel_id=1, source_target_pairs={{0,24},{8,16},{16,8},{24,0},{1,25},{9,17},{17,9},{25,1},{2,26},{10... | collective-permute-start | bytes 221192 | tf_op jit(solution)/shard_map/ppermute | solution.py:480
  14.9 8.6 %collective-permute-start.5 = (bf16[32,1152]{1,0:T(8,128)(2,1)S(1)}, bf16[32,1152]{1,0:T(8,128)(2,1)S(1)}, u32[]{:S(2)}, u32[]{:S(2)}) collective-permute-start(bf16[32,1152]{1,0:T(8,128)(2,1)S(1)} %collective-permute-done.4.refs_0_), channel_id=1, source_target_pairs={{0,1},{1,0},{2,3},{3,2},{4,5},{5,4},{6,7},{7,6},{8,9},{9,8},{10,11... | collective-permute-start | bytes 221192 | tf_op jit(solution)/shard_map/ppermute | solution.py:466
  18.6 4.9 %collective-permute-start.7 = (bf16[32,1152]{1,0:T(8,128)(2,1)S(1)}, bf16[32,1152]{1,0:T(8,128)(2,1)S(1)}, u32[]{:S(2)}, u32[]{:S(2)}) collective-permute-start(bf16[32,1152]{1,0:T(8,128)(2,1)S(1)} %collective-permute-done.6.refs_1_), channel_id=1, source_target_pairs={{0,1},{1,0},{2,3},{3,2},{4,5},{5,4},{6,7},{7,6},{8,9},{9,8},{10,11... | collective-permute-start | bytes 221192 | tf_op jit(solution)/shard_map/ppermute | solution.py:466
  20.1 3.4 %collective-permute-start.9 = (bf16[32,1152]{1,0:T(8,128)(2,1)S(1)}, bf16[32,1152]{1,0:T(8,128)(2,1)S(1)}, u32[]{:S(2)}, u32[]{:S(2)}) collective-permute-start(bf16[32,1152]{1,0:T(8,128)(2,1)S(1)} %collective-permute-done.8.refs_2_), channel_id=1, source_target_pairs={{0,1},{1,0},{2,3},{3,2},{4,5},{5,4},{6,7},{7,6},{8,9},{9,8},{10,11... | collective-permute-start | bytes 221192 | tf_op jit(solution)/shard_map/ppermute | solution.py:466
  21.7 16.5 %collective-permute-start.10 = (bf16[288,1152]{1,0:T(8,128)(2,1)}, bf16[288,1152]{1,0:T(8,128)(2,1)S(1)}, u32[]{:S(2)}, u32[]{:S(2)}) collective-permute-start(bf16[288,1152]{1,0:T(8,128)(2,1)} %get-tuple-element.41.refs_0_), channel_id=1, source_target_pairs={{0,2},{1,3},{2,0},{3,1},{4,6},{5,7},{6,4},{7,5},{8,12},{9,13},{10,... | collective-permute-start | bytes 1990664 | tf_op jit(solution)/shard_map/ppermute | solution.py:474
  23.5 15.7 %collective-permute-start.13 = (bf16[288,1152]{1,0:T(8,128)(2,1)S(1)}, bf16[288,1152]{1,0:T(8,128)(2,1)S(1)}, u32[]{:S(2)}, u32[]{:S(2)}) collective-permute-start(bf16[288,1152]{1,0:T(8,128)(2,1)S(1)} %collective-permute-done.refs_7_), channel_id=1, source_target_pairs={{0,4},{1,5},{2,6},{3,7},{4,0},{5,1},{6,2},{7,3},{8,10},{9,11},{10,... | collective-permute-start | bytes 1990664 | tf_op jit(solution)/shard_map/ppermute | solution.py:474
  25.1 15.4 %collective-permute-start.14 = (bf16[288,1152]{1,0:T(8,128)(2,1)S(1)}, bf16[288,1152]{1,0:T(8,128)(2,1)S(1)}, u32[]{:S(2)}, u32[]{:S(2)}) collective-permute-start(bf16[288,1152]{1,0:T(8,128)(2,1)S(1)} %collective-permute-done.refs_7_), channel_id=1, source_target_pairs={{0,8},{8,0},{16,24},{24,16},{1,9},{9,1},{17,25},{25,17},{2,10},{10... | collective-permute-start | bytes 1990664 | tf_op jit(solution)/shard_map/ppermute | solution.py:480
  26.7 15.5 %collective-permute-start.15 = (bf16[288,1152]{1,0:T(8,128)(2,1)S(1)}, bf16[288,1152]{1,0:T(8,128)(2,1)S(1)}, u32[]{:S(2)}, u32[]{:S(2)}) collective-permute-start(bf16[288,1152]{1,0:T(8,128)(2,1)S(1)} %collective-permute-done.refs_7_), channel_id=1, source_target_pairs={{0,1},{1,0},{2,3},{3,2},{4,5},{5,4},{6,7},{7,6},{8,9},{9,8},{10,11... | collective-permute-start | bytes 1990664 | tf_op jit(solution)/shard_map/ppermute | solution.py:466
  40.5 2.1 %collective-permute-start.16 = (bf16[288,1152]{1,0:T(8,128)(2,1)S(1)}, bf16[288,1152]{1,0:T(8,128)(2,1)S(1)}, u32[]{:S(2)}, u32[]{:S(2)}) collective-permute-start(bf16[288,1152]{1,0:T(8,128)(2,1)S(1)} %collective-permute-done.13.refs_8_), channel_id=1, source_target_pairs={{0,1},{1,0},{2,3},{3,2},{4,5},{5,4},{6,7},{7,6},{8,9},{9,8},{10,11... | collective-permute-start | bytes 1990664 | tf_op jit(solution)/shard_map/ppermute | solution.py:466
  40.5 3.1 %collective-permute-start.17 = (bf16[288,1152]{1,0:T(8,128)(2,1)S(1)}, bf16[288,1152]{1,0:T(8,128)(2,1)S(1)}, u32[]{:S(2)}, u32[]{:S(2)}) collective-permute-start(bf16[288,1152]{1,0:T(8,128)(2,1)S(1)} %collective-permute-done.14.refs_9_), channel_id=1, source_target_pairs={{0,1},{1,0},{2,3},{3,2},{4,5},{5,4},{6,7},{7,6},{8,9},{9,8},{10,11... | collective-permute-start | bytes 1990664 | tf_op jit(solution)/shard_map/ppermute | solution.py:466
  41.1 9.8 %collective-permute-start.12 = (bf16[144,1152]{1,0:T(8,128)(2,1)S(1)}, bf16[144,1152]{1,0:T(8,128)(2,1)S(1)}, u32[]{:S(2)}, u32[]{:S(2)}) collective-permute-start(bf16[144,1152]{1,0:T(8,128)(2,1)S(1)} %slice.8), channel_id=1, source_target_pairs={{0,4},{1,5},{2,6},{3,7},{4,0},{5,1},{6,2},{7,3},{8,10},{9,11},{10,... | collective-permute-start | bytes 995336 | tf_op jit(solution)/shard_map/ppermute | solution.py:474
  41.6 9.4 %collective-permute-start.11 = (bf16[144,1152]{1,0:T(8,128)(2,1)S(1)}, bf16[144,1152]{1,0:T(8,128)(2,1)S(1)}, u32[]{:S(2)}, u32[]{:S(2)}) collective-permute-start(bf16[144,1152]{1,0:T(8,128)(2,1)S(1)} %slice.6), channel_id=1, source_target_pairs={{0,2},{1,3},{2,0},{3,1},{4,6},{5,7},{6,4},{7,5},{8,12},{9,13},{10,... | collective-permute-start | bytes 995336 | tf_op jit(solution)/shard_map/ppermute | solution.py:474
  42.2 9.3 %collective-permute-start.19 = (bf16[288,1152]{1,0:T(8,128)(2,1)S(1)}, bf16[288,1152]{1,0:T(8,128)(2,1)S(1)}, u32[]{:S(2)}, u32[]{:S(2)}) collective-permute-start(bf16[288,1152]{1,0:T(8,128)(2,1)S(1)} %collective-permute-done.10.refs_2_), channel_id=1, source_target_pairs={{0,1},{1,0},{2,3},{3,2},{4,5},{5,4},{6,7},{7,6},{8,9},{9,8},{10,11... | collective-permute-start | bytes 1990664 | tf_op jit(solution)/shard_map/ppermute | solution.py:466
  42.6 9.0 %collective-permute-start.18 = (bf16[288,1152]{1,0:T(8,128)(2,1)S(1)}, bf16[288,1152]{1,0:T(8,128)(2,1)S(1)}, u32[]{:S(2)}, u32[]{:S(2)}) collective-permute-start(bf16[288,1152]{1,0:T(8,128)(2,1)S(1)} %collective-permute-done.1.refs_1_), channel_id=1, source_target_pairs={{0,1},{1,0},{2,3},{3,2},{4,5},{5,4},{6,7},{7,6},{8,9},{9,8},{10,11... | collective-permute-start | bytes 1990664 | tf_op jit(solution)/shard_map/ppermute | solution.py:466
  51.1 1.6 %collective-permute-start.20 = (bf16[144,1152]{1,0:T(8,128)(2,1)S(1)}, bf16[144,1152]{1,0:T(8,128)(2,1)S(1)}, u32[]{:S(2)}, u32[]{:S(2)}) collective-permute-start(bf16[144,1152]{1,0:T(8,128)(2,1)S(1)} %collective-permute-done.11.refs_3_), channel_id=1, source_target_pairs={{0,1},{1,0},{2,3},{3,2},{4,5},{5,4},{6,7},{7,6},{8,9},{9,8},{10,11... | collective-permute-start | bytes 995336 | tf_op jit(solution)/shard_map/ppermute | solution.py:466
  51.1 2.1 %collective-permute-start.21 = (bf16[144,1152]{1,0:T(8,128)(2,1)S(1)}, bf16[144,1152]{1,0:T(8,128)(2,1)S(1)}, u32[]{:S(2)}, u32[]{:S(2)}) collective-permute-start(bf16[144,1152]{1,0:T(8,128)(2,1)S(1)} %collective-permute-done.12.refs_4_), channel_id=1, source_target_pairs={{0,1},{1,0},{2,3},{3,2},{4,5},{5,4},{6,7},{7,6},{8,9},{9,8},{10,11... | collective-permute-start | bytes 995336 | tf_op jit(solution)/shard_map/ppermute | solution.py:466
  60.7 1.4 %collective-permute-start.22 = (f32[32,1152]{1,0:T(8,128)S(1)}, f32[32,1152]{1,0:T(8,128)S(1)}, u32[]{:S(2)}, u32[]{:S(2)}) collective-permute-start(f32[32,1152]{1,0:T(8,128)S(1)} %get-tuple-element.60), channel_id=1, source_target_pairs={{0,1},{1,0},{2,3},{3,2},{4,5},{5,4},{6,7},{7,6},{8,9},{9,8},{10,11... | collective-permute-start | bytes 442376 | tf_op jit(solution)/shard_map/ppermute | solution.py:466
  62.2 6.7 %collective-permute-start.23 = (bf16[32,1152]{1,0:T(8,128)(2,1)S(1)}, bf16[32,1152]{1,0:T(8,128)(2,1)S(1)}, u32[]{:S(2)}, u32[]{:S(2)}) collective-permute-start(bf16[32,1152]{1,0:T(8,128)(2,1)S(1)} %add_convert_fusion.1), channel_id=1, source_target_pairs={{0,2},{1,3},{2,0},{3,1},{4,6},{5,7},{6,4},{7,5},{8,10},{9,11},{10,... | collective-permute-start | bytes 221192 | tf_op jit(solution)/shard_map/ppermute | solution.py:466
  62.8 6.1 %collective-permute-start.24 = (bf16[32,1152]{1,0:T(8,128)(2,1)S(1)}, bf16[32,1152]{1,0:T(8,128)(2,1)S(1)}, u32[]{:S(2)}, u32[]{:S(2)}) collective-permute-start(bf16[32,1152]{1,0:T(8,128)(2,1)S(1)} %add_convert_fusion.1), channel_id=1, source_target_pairs={{0,4},{1,5},{2,6},{3,7},{4,0},{5,1},{6,2},{7,3},{8,12},{9,13},{10,... | collective-permute-start | bytes 221192 | tf_op jit(solution)/shard_map/ppermute | solution.py:466
  64.3 5.3 %collective-permute-start.25 = (bf16[32,1152]{1,0:T(8,128)(2,1)S(1)}, bf16[32,1152]{1,0:T(8,128)(2,1)S(1)}, u32[]{:S(2)}, u32[]{:S(2)}) collective-permute-start(bf16[32,1152]{1,0:T(8,128)(2,1)S(1)} %add_convert_fusion.1), channel_id=1, source_target_pairs={{0,6},{1,7},{2,4},{3,5},{4,2},{5,3},{6,0},{7,1},{8,14},{9,15},{10,... | collective-permute-start | bytes 221192 | tf_op jit(solution)/shard_map/ppermute | solution.py:466
  69.6 7.6 %collective-permute-start.26 = (bf16[32,1152]{1,0:T(8,128)(2,1)S(1)}, bf16[32,1152]{1,0:T(8,128)(2,1)S(1)}, u32[]{:S(2)}, u32[]{:S(2)}) collective-permute-start(bf16[32,1152]{1,0:T(8,128)(2,1)S(1)} %add_convert_fusion.refs_0_), channel_id=1, source_target_pairs={{0,8},{8,0},{16,24},{24,16},{1,9},{9,1},{17,25},{25,17},{2,10},{10... | collective-permute-start | bytes 221192 | tf_op jit(solution)/shard_map/ppermute | solution.py:480
  71.4 6.8 %collective-permute-start.27 = (bf16[32,1152]{1,0:T(8,128)(2,1)S(1)}, bf16[32,1152]{1,0:T(8,128)(2,1)S(1)}, u32[]{:S(2)}, u32[]{:S(2)}) collective-permute-start(bf16[32,1152]{1,0:T(8,128)(2,1)S(1)} %add_convert_fusion.refs_0_), channel_id=1, source_target_pairs={{0,16},{8,24},{16,0},{24,8},{1,17},{9,25},{17,1},{25,9},{2,18},{10... | collective-permute-start | bytes 221192 | tf_op jit(solution)/shard_map/ppermute | solution.py:480
  74.0 6.2 %collective-permute-start.28 = (bf16[32,1152]{1,0:T(8,128)(2,1)S(1)}, bf16[32,1152]{1,0:T(8,128)(2,1)S(1)}, u32[]{:S(2)}, u32[]{:S(2)}) collective-permute-start(bf16[32,1152]{1,0:T(8,128)(2,1)S(1)} %add_convert_fusion.refs_0_), channel_id=1, source_target_pairs={{0,24},{8,16},{16,8},{24,0},{1,25},{9,17},{17,9},{25,1},{2,26},{10... | collective-permute-start | bytes 221192 | tf_op jit(solution)/shard_map/ppermute | solution.py:480
  74.1 6.6 %collective-permute-start.29 = (bf16[32,1152]{1,0:T(8,128)(2,1)S(1)}, bf16[32,1152]{1,0:T(8,128)(2,1)S(1)}, u32[]{:S(2)}, u32[]{:S(2)}) collective-permute-start(bf16[32,1152]{1,0:T(8,128)(2,1)S(1)} %add_convert_fusion.refs_0_), channel_id=1, source_target_pairs={{0,1},{1,0},{2,3},{3,2},{4,5},{5,4},{6,7},{7,6},{8,9},{9,8},{10,11... | collective-permute-start | bytes 221192 | tf_op jit(solution)/shard_map/ppermute | solution.py:466
  80.1 1.4 %collective-permute-start.31 = (bf16[32,1152]{1,0:T(8,128)(2,1)S(1)}, bf16[32,1152]{1,0:T(8,128)(2,1)S(1)}, u32[]{:S(2)}, u32[]{:S(2)}) collective-permute-start(bf16[32,1152]{1,0:T(8,128)(2,1)S(1)} %collective-permute-done.27.refs_2_), channel_id=1, source_target_pairs={{0,1},{1,0},{2,3},{3,2},{4,5},{5,4},{6,7},{7,6},{8,9},{9,8},{10,11... | collective-permute-start | bytes 221192 | tf_op jit(solution)/shard_map/ppermute | solution.py:466
  80.6 1.3 %collective-permute-start.32 = (bf16[32,1152]{1,0:T(8,128)(2,1)S(1)}, bf16[32,1152]{1,0:T(8,128)(2,1)S(1)}, u32[]{:S(2)}, u32[]{:S(2)}) collective-permute-start(bf16[32,1152]{1,0:T(8,128)(2,1)S(1)} %collective-permute-done.28.refs_3_), channel_id=1, source_target_pairs={{0,1},{1,0},{2,3},{3,2},{4,5},{5,4},{6,7},{7,6},{8,9},{9,8},{10,11... | collective-permute-start | bytes 221192 | tf_op jit(solution)/shard_map/ppermute | solution.py:466
  (8 other events, 68.2 us)

commit v5 on v4

--- a/solution.py
+++ b/solution.py
@@ -276,18 +276,25 @@
     wait_all(copies)
 
 
+def own_kernel(place_ref, mine, far, first_weight, second_weight, slope_ref, phrase_out, act_out, grad):
+    join_halves(grad, place_ref[1], 0, [mine], [far])
+    hidden_grad = times_transposed(grad[...], second_weight[...])
+    act_out[...] = (hidden_grad * slope_ref[: act_out.shape[0]]).astype(jnp.bfloat16)
+    phrase_out[...] = times_transposed(act_out[...], first_weight[...]).astype(jnp.bfloat16)
+
+
 def weight_grad_kernel(planes, place_ref, *refs):
     mine, far = refs[:planes], refs[planes : 2 * planes]
     (
-        first_weight,
         second_weight,
+        act_ref,
         slope_ref,
         hidden_ref,
         phrase_ref,
         second_out,
         first_out,
-        phrase_out,
         encoded_grad,
+        act_grad,
         second_grad,
         first_grad,
         out_sem,
@@ -296,14 +303,13 @@
     second_grad[...] = transposed_times(hidden_ref[...], encoded_grad[...])
     second_copy = pltpu.make_async_copy(second_grad, second_out, out_sem.at[0])
     second_copy.start()
-    hidden_grad = times_transposed(encoded_grad[...], second_weight[...])
-    act_grad = (hidden_grad * slope_ref[...]).astype(jnp.bfloat16)
-    first_grad[...] = transposed_times(phrase_ref[...], act_grad)
+    own = act_ref.shape[0]
+    hidden_grad = times_transposed(encoded_grad[own:], second_weight[...])
+    act_grad[:own] = act_ref[...]
+    act_grad[own:] = (hidden_grad * slope_ref[own:]).astype(jnp.bfloat16)
+    first_grad[...] = transposed_times(phrase_ref[...], act_grad[...])
     first_copy = pltpu.make_async_copy(first_grad, first_out, out_sem.at[1])
     first_copy.start()
-    phrase_out[...] = times_transposed(
-        act_grad[: phrase_out.shape[0]], first_weight[...]
-    ).astype(jnp.bfloat16)
     second_copy.wait()
     first_copy.wait()
 
@@ -666,17 +672,27 @@
         latent_grad = latent_part(image, score_grad, latent_grad)
     grad_mines = [grad_own] + plane_peers(grad_own)
     grad_fars = [swap(grad_own, 1)]
-    grad_fars += [swap(part, 1) for part in after_all(grad_mines[1:], latent_grad)]
-    second_grad, first_grad, phrase_grad = pl.pallas_call(
+    phrase_grad, act_own = pl.pallas_call(
+        own_kernel,
+        out_shape=[shape((rows, features), jnp.bfloat16)] * 2,
+        in_specs=[SMEM] + [VMEM] * 5,
+        out_specs=[VMEM] * 2,
+        scratch_shapes=[pltpu.VMEM((rows, features), jnp.bfloat16)],
+        compiler_params=vmem(12),
+        cost_estimate=pl.CostEstimate(flops=10**9, bytes_accessed=6 * 10**6, transcendentals=0),
+        name="own_grads",
+    )(place, grad_own, grad_fars[0], whole_first, whole_second, slope)
+    grad_fars += [swap(part, 1) for part in after_all(grad_mines[1:], latent_grad, act_own)]
+    second_grad, first_grad = pl.pallas_call(
         functools.partial(weight_grad_kernel, planes),
         out_shape=[
             shape((shard_rows, features), jnp.float32),
             shape((shard_rows, features), jnp.float32),
-            shape((rows, features), jnp.bfloat16),
         ],
         in_specs=[SMEM] + [VMEM] * (2 * planes + 5),
-        out_specs=[ANY, ANY, VMEM],
+        out_specs=[ANY, ANY],
         scratch_shapes=[
+            pltpu.VMEM((all_rows, features), jnp.bfloat16),
             pltpu.VMEM((all_rows, features), jnp.bfloat16),
             pltpu.VMEM((shard_rows, features), jnp.float32),
             pltpu.VMEM((shard_rows, features), jnp.float32),
@@ -688,8 +704,8 @@
         place,
         *grad_mines,
         *grad_fars,
-        whole_first,
         whole_second,
+        act_own,
         slope,
         own_hidden,
         own_phrases,

time: 86.5 us -> 85.7 us (level)
  waiting for transfers between devices: 26.4 us -> 23.4 us
  Pallas kernels: 27.3 us -> 29.2 us
    pallas_call x0 -> x1, Pallas kernels: none -> 2.94 us  [tiled(): pl.pallas_call(own_kernel, out_shape=[shape((rows, features), jnp.bfloat1...]
    ppermute x7, waiting for transfers between devices: 9.25 us -> 6.37 us  [plane_swap(): return lax.ppermute(array, 'dp', [(i, i ^ distance) for i in range(planes)])]
    pallas_call x1, Pallas kernels: 4.15 us -> 2.84 us  [tiled(): pl.pallas_call(functools.partial(weight_grad_kernel, planes), out_shape=[...]
  transfers between devices with their start and end apart: 33 -> 33, of which waited for: 19 -> 17; matrix products, arithmetic and copies ran while one was open for 3% -> 3% of each run, Pallas kernels for 15% -> 19%
where the time goes in v5:
time: 85.7 us; the launch traced here: 85.4 us
  Pallas kernels  29.2 us (34%)
  starting transfers between devices  25.7 us (30%)
  waiting for transfers between devices  23.4 us (27%)
  local copies, waits for them, and re-layouts  4.38 us (5%)
  other arithmetic  1.67 us (2%)
  between operations  1.05 us (1%)
    ppermute x6, waiting for transfers between devices, swap_by_plane(): return lax.ppermute(array, ('dp', 'seq'), pairs)  11.2 us
    ppermute x7, starting transfers between devices, plane_swap(): return lax.ppermute(array, 'dp', [(i, i ^ distance) for i in range(planes)])  10.4 us
    ppermute x6, starting transfers between devices, swap_by_plane(): return lax.ppermute(array, ('dp', 'seq'), pairs)  8.96 us
    pallas_call x1, Pallas kernels, tiled(): pl.pallas_call(functools.partial(attend_kernel, chips, images, projector_...  7.54 us
    pallas_call x2, Pallas kernels, latent_part(): pl.pallas_call(kernel if whole is None else lambda _, *refs: kernel(*refs...  6.57 us
    ppermute x7, waiting for transfers between devices, plane_swap(): return lax.ppermute(array, 'dp', [(i, i ^ distance) for i in range(planes)])  6.37 us
    ppermute x20, starting transfers between devices, swap(): lax.ppermute(array, 'seq', [(i, i ^ distance) for i in range(shards)])  6.29 us
    ppermute x20, waiting for transfers between devices, swap(): lax.ppermute(array, 'seq', [(i, i ^ distance) for i in range(shards)])  5.85 us
  transfers between devices with their start and end apart: 33, of which 17 were waited for; matrix products, arithmetic and copies ran while one was open for 3% of the time, Pallas kernels for 19%

profile of v5, /device:TPU:0, one launch (start us, length us, event | category | flops | bytes accessed | tf_op | source)
XLA Modules:
  0.0 85.4 jit_solution(8037980541707573914)
XLA Ops:
  0.6 2.4 %join.1 = (bf16[288,1152]{1,0:T(8,128)(2,1)}, bf16[288,1152]{1,0:T(8,128)(2,1)}) custom-call(bf16[144,1152]{1,0:T(8,128)(2,1)} %refs_0_.1, bf16[144,1152]{1,0:T(8,128)(2,1)} %refs_1_.1, bf16[144,1152]{1,0:T(8,128)(2,1)} %refs_2_.2, bf16[144,1152]{1,0:T(8,128)(2,1)} %refs_3_.1), custom_call_target="tpu_custom_call" | custom-call | tf_op jit(solution)/shard_map/join/pallas_call | solution.py:525
  3.5 2.9 %collective-permute-start = (bf16[288,1152]{1,0:T(8,128)(2,1)}, bf16[288,1152]{1,0:T(8,128)(2,1)S(1)}, u32[]{:S(2)}, u32[]{:S(2)}) collective-permute-start(bf16[288,1152]{1,0:T(8,128)(2,1)} %get-tuple-element.41.refs_6_), channel_id=1, source_target_pairs={{0,2},{1,3},{2,0},{3,1},{4,6},{5,7},{6,4},{7,5},{8,12},{9,13},{10,... | collective-permute-start | bytes 1990664 | tf_op jit(solution)/shard_map/ppermute | solution.py:480
  6.5 1.5 %collective-permute-start.1 = (bf16[288,1152]{1,0:T(8,128)(2,1)}, bf16[288,1152]{1,0:T(8,128)(2,1)S(1)}, u32[]{:S(2)}, u32[]{:S(2)}) collective-permute-start(bf16[288,1152]{1,0:T(8,128)(2,1)} %get-tuple-element.42.refs_0_), channel_id=1, source_target_pairs={{0,4},{1,5},{2,6},{3,7},{4,0},{5,1},{6,2},{7,3},{8,10},{9,11},{10,... | collective-permute-start | bytes 1990664 | tf_op jit(solution)/shard_map/ppermute | solution.py:480
  8.7 0.9 %constant_dynamic-slice_fusion = bf16[32,1152]{1,0:T(8,128)(2,1)S(1)} fusion(bf16[64,1152]{1,0:T(8,128)(2,1)} %bitcast.8, s32[]{:T(128)S(6)} %select_n.32), kind=kLoop, calls=%fused_computation.14 | loop fusion | bytes 147460 | tf_op jit(solution)/shard_map/dynamic_slice | solution.py:540
  9.6 1.6 %collective-permute-start.4 = (bf16[32,1152]{1,0:T(8,128)(2,1)S(1)}, bf16[32,1152]{1,0:T(8,128)(2,1)S(1)}, u32[]{:S(2)}, u32[]{:S(2)}) collective-permute-start(bf16[32,1152]{1,0:T(8,128)(2,1)S(1)} %constant_dynamic-slice_fusion), channel_id=1, source_target_pairs={{0,8},{8,0},{16,24},{24,16},{1,9},{9,1},{17,25},{25,17},{2,10},{10... | collective-permute-start | bytes 221192 | tf_op jit(solution)/shard_map/ppermute | solution.py:486
  11.2 2.6 %collective-permute-start.6 = (bf16[32,1152]{1,0:T(8,128)(2,1)S(1)}, bf16[32,1152]{1,0:T(8,128)(2,1)S(1)}, u32[]{:S(2)}, u32[]{:S(2)}) collective-permute-start(bf16[32,1152]{1,0:T(8,128)(2,1)S(1)} %constant_dynamic-slice_fusion), channel_id=1, source_target_pairs={{0,16},{8,24},{16,0},{24,8},{1,17},{9,25},{17,1},{25,9},{2,18},{10... | collective-permute-start | bytes 221192 | tf_op jit(solution)/shard_map/ppermute | solution.py:486
  14.9 3.7 %collective-permute-done.6.refs_1_ = bf16[32,1152]{1,0:T(8,128)(2,1)S(1)} collective-permute-done((bf16[32,1152]{1,0:T(8,128)(2,1)S(1)}, bf16[32,1152]{1,0:T(8,128)(2,1)S(1)}, u32[]{:S(2)}, u32[]{:S(2)}) %collective-permute-start.6) | collective-permute-done | bytes 73760 | tf_op jit(solution)/shard_map/ppermute | solution.py:486
  18.6 1.5 %collective-permute-done.8.refs_2_ = bf16[32,1152]{1,0:T(8,128)(2,1)S(1)} collective-permute-done((bf16[32,1152]{1,0:T(8,128)(2,1)S(1)}, bf16[32,1152]{1,0:T(8,128)(2,1)S(1)}, u32[]{:S(2)}, u32[]{:S(2)}) %collective-permute-start.8) | collective-permute-done | bytes 73760 | tf_op jit(solution)/shard_map/ppermute | solution.py:486
  20.1 1.6 %collective-permute-done.refs_7_ = bf16[288,1152]{1,0:T(8,128)(2,1)S(1)} collective-permute-done((bf16[288,1152]{1,0:T(8,128)(2,1)}, bf16[288,1152]{1,0:T(8,128)(2,1)S(1)}, u32[]{:S(2)}, u32[]{:S(2)}) %collective-permute-start) | collective-permute-done | bytes 663584 | tf_op jit(solution)/shard_map/ppermute | solution.py:480
  21.7 1.7 %collective-permute-start.10 = (bf16[288,1152]{1,0:T(8,128)(2,1)}, bf16[288,1152]{1,0:T(8,128)(2,1)S(1)}, u32[]{:S(2)}, u32[]{:S(2)}) collective-permute-start(bf16[288,1152]{1,0:T(8,128)(2,1)} %get-tuple-element.42.refs_0_), channel_id=1, source_target_pairs={{0,2},{1,3},{2,0},{3,1},{4,6},{5,7},{6,4},{7,5},{8,12},{9,13},{10,... | collective-permute-start | bytes 1990664 | tf_op jit(solution)/shard_map/ppermute | solution.py:480
  23.5 1.6 %collective-permute-start.13 = (bf16[288,1152]{1,0:T(8,128)(2,1)S(1)}, bf16[288,1152]{1,0:T(8,128)(2,1)S(1)}, u32[]{:S(2)}, u32[]{:S(2)}) collective-permute-start(bf16[288,1152]{1,0:T(8,128)(2,1)S(1)} %collective-permute-done.refs_7_), channel_id=1, source_target_pairs={{0,4},{1,5},{2,6},{3,7},{4,0},{5,1},{6,2},{7,3},{8,10},{9,11},{10,... | collective-permute-start | bytes 1990664 | tf_op jit(solution)/shard_map/ppermute | solution.py:480
  25.1 1.6 %collective-permute-start.14 = (bf16[288,1152]{1,0:T(8,128)(2,1)S(1)}, bf16[288,1152]{1,0:T(8,128)(2,1)S(1)}, u32[]{:S(2)}, u32[]{:S(2)}) collective-permute-start(bf16[288,1152]{1,0:T(8,128)(2,1)S(1)} %collective-permute-done.refs_7_), channel_id=1, source_target_pairs={{0,8},{8,0},{16,24},{24,16},{1,9},{9,1},{17,25},{25,17},{2,10},{10... | collective-permute-start | bytes 1990664 | tf_op jit(solution)/shard_map/ppermute | solution.py:486
  26.8 1.7 %copy-done.2 = bf16[1152,1152]{1,0:T(8,128)(2,1)S(1)} copy-done((bf16[1152,1152]{1,0:T(8,128)(2,1)S(1)}, bf16[1152,1152]{1,0:T(8,128)(2,1)}, u32[]{:S(2)}) %copy-start.2) | copy-done | bytes 2654232
  28.5 1.7 %copy-done.4 = bf16[2,512,1152]{2,1,0:T(8,128)(2,1)S(1)} copy-done((bf16[2,512,1152]{2,1,0:T(8,128)(2,1)S(1)}, bf16[2,512,1152]{2,1,0:T(8,128)(2,1)}, u32[]{:S(2)}) %copy-start.4) | copy-done | bytes 2359320
  30.2 4.2 %queries.1.refs_10_ = bf16[1024,1152]{1,0:T(8,128)(2,1)S(1)} custom-call(bf16[1024,1152]{1,0:T(8,128)(2,1)S(1)} %bitcast.10, bf16[1152,1152]{1,0:T(8,128)(2,1)S(1)} %copy-done.2), custom_call_target="tpu_custom_call" | custom-call | flops 3000000000 | bytes 8000000 | tf_op jit(solution)/shard_map/queries/pallas_call | solution.py:504
  34.4 3.8 %collective-permute-done.10.refs_2_ = bf16[288,1152]{1,0:T(8,128)(2,1)S(1)} collective-permute-done((bf16[288,1152]{1,0:T(8,128)(2,1)}, bf16[288,1152]{1,0:T(8,128)(2,1)S(1)}, u32[]{:S(2)}, u32[]{:S(2)}) %collective-permute-start.10) | collective-permute-done | bytes 663584 | tf_op jit(solution)/shard_map/ppermute | solution.py:480
  38.2 1.0 %collective-permute-done.13.refs_8_ = bf16[288,1152]{1,0:T(8,128)(2,1)S(1)} collective-permute-done((bf16[288,1152]{1,0:T(8,128)(2,1)S(1)}, bf16[288,1152]{1,0:T(8,128)(2,1)S(1)}, u32[]{:S(2)}, u32[]{:S(2)}) %collective-permute-start.13) | collective-permute-done | bytes 663584 | tf_op jit(solution)/shard_map/ppermute | solution.py:480
  39.3 1.2 %collective-permute-done.14.refs_9_ = bf16[288,1152]{1,0:T(8,128)(2,1)S(1)} collective-permute-done((bf16[288,1152]{1,0:T(8,128)(2,1)S(1)}, bf16[288,1152]{1,0:T(8,128)(2,1)S(1)}, u32[]{:S(2)}, u32[]{:S(2)}) %collective-permute-start.14) | collective-permute-done | bytes 663584 | tf_op jit(solution)/shard_map/ppermute | solution.py:486
  42.8 0.8 collective-permute-done.17.refs_13_
  43.6 2.7 %encode.1 = (bf16[64,1152]{1,0:T(8,128)(2,1)S(1)}, f32[256,1152]{1,0:T(8,128)S(1)}, bf16[256,144]{1,0:T(8,128)(2,1)S(1)}, bf16[256,144]{1,0:T(8,128)(2,1)S(1)}, ...) custom-call(s32[3]{0:T(128)S(1)} %pad_add_fusion.place_ref, bf16[64,1152]{1,0:T(8,128)(2,1)S(1)} %bitcast.9, ...), custom_call_target="tpu_custom_call" | custom-call | flops 1000000 | bytes 10000 | tf_op jit(solution)/shard_map/encode/pallas_call | solution.py:597
  46.3 4.5 %collective-permute-done.12.refs_4_ = bf16[144,1152]{1,0:T(8,128)(2,1)S(1)} collective-permute-done((bf16[144,1152]{1,0:T(8,128)(2,1)S(1)}, bf16[144,1152]{1,0:T(8,128)(2,1)S(1)}, u32[]{:S(2)}, u32[]{:S(2)}) %collective-permute-start.12) | collective-permute-done | bytes 331808 | tf_op jit(solution)/shard_map/ppermute | solution.py:480
  51.6 1.1 %collective-permute-done.20.refs_8_ = bf16[144,1152]{1,0:T(8,128)(2,1)S(1)} collective-permute-done((bf16[144,1152]{1,0:T(8,128)(2,1)S(1)}, bf16[144,1152]{1,0:T(8,128)(2,1)S(1)}, u32[]{:S(2)}, u32[]{:S(2)}) %collective-permute-start.20) | collective-permute-done | bytes 331808 | tf_op jit(solution)/shard_map/ppermute | solution.py:472
  53.2 7.5 %attend.1 = (bf16[64,1152]{1,0:T(8,128)(2,1)S(1)}, bf16[2,512,512]{2,1,0:T(8,128)(2,1)S(1)}, f32[32,1152]{1,0:T(8,128)S(1)}, f32[32,1152]{1,0:T(8,128)S(1)}) custom-call(s32[3]{0:T(128)S(1)} %pad_add_fusion.place_ref, bf16[64,1152]{1,0:T(8,128)(2,1)S(1)} %get-tuple-element.56.encoded_ref, bf16[288,1152]{1,0:T(8,128)(2,1)S(1)} %copy-done.6, ...), custom_call_target="tpu_custom_call" | custom-call | flops 10000000000 | bytes 12000000 | tf_op jit(solution)/shard_map/attend/pallas_call | solution.py:622
  60.9 1.2 %collective-permute-done.22 = f32[32,1152]{1,0:T(8,128)S(1)} collective-permute-done((f32[32,1152]{1,0:T(8,128)S(1)}, f32[32,1152]{1,0:T(8,128)S(1)}, u32[]{:S(2)}, u32[]{:S(2)}) %collective-permute-start.22) | collective-permute-done | bytes 147488 | tf_op jit(solution)/shard_map/ppermute | solution.py:472
  62.9 1.5 %collective-permute-start.24 = (bf16[32,1152]{1,0:T(8,128)(2,1)S(1)}, bf16[32,1152]{1,0:T(8,128)(2,1)S(1)}, u32[]{:S(2)}, u32[]{:S(2)}) collective-permute-start(bf16[32,1152]{1,0:T(8,128)(2,1)S(1)} %add_convert_fusion.1), channel_id=1, source_target_pairs={{0,4},{1,5},{2,6},{3,7},{4,0},{5,1},{6,2},{7,3},{8,12},{9,13},{10,... | collective-permute-start | bytes 221192 | tf_op jit(solution)/shard_map/ppermute | solution.py:472
  64.3 1.4 %collective-permute-start.25 = (bf16[32,1152]{1,0:T(8,128)(2,1)S(1)}, bf16[32,1152]{1,0:T(8,128)(2,1)S(1)}, u32[]{:S(2)}, u32[]{:S(2)}) collective-permute-start(bf16[32,1152]{1,0:T(8,128)(2,1)S(1)} %add_convert_fusion.1), channel_id=1, source_target_pairs={{0,6},{1,7},{2,4},{3,5},{4,2},{5,3},{6,0},{7,1},{8,14},{9,15},{10,... | collective-permute-start | bytes 221192 | tf_op jit(solution)/shard_map/ppermute | solution.py:472
  65.7 3.2 %latent.2._ = bf16[1024,1152]{1,0:T(8,128)(2,1)} custom-call(bf16[2,512,512]{2,1,0:T(8,128)(2,1)S(1)} %get-tuple-element.62.score_ref.refs_0_, bf16[64,1152]{1,0:T(8,128)(2,1)S(1)} %get-tuple-element.63.key_ref.refs_1_, bf16[1152,1152]{1,0:T(8,128)(2,1)S(1)} %copy-done.3), custom_call_target="tpu_custom_call" | custom-call | flops 3000000000 | bytes 4000000 | tf_op jit(solution)/shard_map/latent/pallas_call | solution.py:650
  69.7 1.8 %collective-permute-start.27 = (bf16[32,1152]{1,0:T(8,128)(2,1)S(1)}, bf16[32,1152]{1,0:T(8,128)(2,1)S(1)}, u32[]{:S(2)}, u32[]{:S(2)}) collective-permute-start(bf16[32,1152]{1,0:T(8,128)(2,1)S(1)} %add_convert_fusion.mine.refs_0_), channel_id=1, source_target_pairs={{0,8},{8,0},{16,24},{24,16},{1,9},{9,1},{17,25},{25,17},{2,10},{10... | collective-permute-start | bytes 221192 | tf_op jit(solution)/shard_map/ppermute | solution.py:486
  71.5 2.6 %collective-permute-start.28 = (bf16[32,1152]{1,0:T(8,128)(2,1)S(1)}, bf16[32,1152]{1,0:T(8,128)(2,1)S(1)}, u32[]{:S(2)}, u32[]{:S(2)}) collective-permute-start(bf16[32,1152]{1,0:T(8,128)(2,1)S(1)} %add_convert_fusion.mine.refs_0_), channel_id=1, source_target_pairs={{0,16},{8,24},{16,0},{24,8},{1,17},{9,25},{17,1},{25,9},{2,18},{10... | collective-permute-start | bytes 221192 | tf_op jit(solution)/shard_map/ppermute | solution.py:486
  74.1 3.4 %latent.3 = bf16[1024,1152]{1,0:T(8,128)(2,1)} custom-call(bf16[1024,1152]{1,0:T(8,128)(2,1)} %latent.2._, bf16[2,512,512]{2,1,0:T(8,128)(2,1)S(1)} %get-tuple-element.62.score_ref.refs_0_, bf16[64,1152]{1,0:T(8,128)(2,1)S(1)} %get-tuple-element.63.key_ref.refs_1_, bf16[1152,1152]{1,0:T(8,128)(2,1)S(1)} %copy-done.3), custom_call_target="tpu_custom_call", output_to_operand_aliasing={{}: (0, {})} | custom-call | flops 3000000000 | bytes 4000000 | tf_op jit(solution)/shard_map/latent/pallas_call | solution.py:650
  77.6 2.9 %own_grads.1 = (bf16[64,1152]{1,0:T(8,128)(2,1)}, bf16[64,1152]{1,0:T(8,128)(2,1)S(1)}) custom-call(s32[3]{0:T(128)S(1)} %pad_add_fusion.place_ref, bf16[32,1152]{1,0:T(8,128)(2,1)S(1)} %add_convert_fusion.mine.refs_0_, bf16[32,1152]{1,0:T(8,128)(2,1)S(1)} %collective-permute-done.26.far.refs_4_, bf16[1152,1152]{1,0:T(8,128)(2,1)S(1)} %get-tuple-element.66.first_weight, ...), custom_call_target="tpu_custom_call" | custom-call | flops 1000000000 | bytes 6000000 | tf_op jit(solution)/shard_map/own_grads/pallas_call | solution.py:675
  82.4 2.8 %weight_grads.1 = (f32[144,1152]{1,0:T(8,128)}, f32[144,1152]{1,0:T(8,128)}) custom-call(s32[3]{0:T(128)S(1)} %pad_add_fusion.place_ref, bf16[32,1152]{1,0:T(8,128)(2,1)S(1)} %add_convert_fusion.mine.refs_0_, bf16[32,1152]{1,0:T(8,128)(2,1)S(1)} %collective-permute-done.27.refs_1_, bf16[32,1152]{1,0:T(8,128)(2,1)S(1)} %collective-permute-done.28.refs_2_, ...), custom_call_target="tpu_custom_call" | custom-call | tf_op jit(solution)/shard_map/weight_grads/pallas_call | solution.py:686
  (65 shorter events, 9.6 us)
Async XLA Ops:
  3.0 5.7 %collective-permute-start.3 = (bf16[288,1152]{1,0:T(8,128)(2,1)}, bf16[288,1152]{1,0:T(8,128)(2,1)S(1)}, u32[]{:S(2)}, u32[]{:S(2)}) collective-permute-start(bf16[288,1152]{1,0:T(8,128)(2,1)} %get-tuple-element.42.refs_0_), channel_id=1, source_target_pairs={{0,1},{1,0},{2,3},{3,2},{4,5},{5,4},{6,7},{7,6},{8,9},{9,8},{10,11... | collective-permute-start | bytes 1990664 | tf_op jit(solution)/shard_map/ppermute | solution.py:472
  3.5 5.3 %collective-permute-start.2 = (bf16[288,1152]{1,0:T(8,128)(2,1)}, bf16[288,1152]{1,0:T(8,128)(2,1)S(1)}, u32[]{:S(2)}, u32[]{:S(2)}) collective-permute-start(bf16[288,1152]{1,0:T(8,128)(2,1)} %get-tuple-element.41.refs_6_), channel_id=1, source_target_pairs={{0,1},{1,0},{2,3},{3,2},{4,5},{5,4},{6,7},{7,6},{8,9},{9,8},{10,11... | collective-permute-start | bytes 1990664 | tf_op jit(solution)/shard_map/ppermute | solution.py:472
  3.5 18.2 %collective-permute-start = (bf16[288,1152]{1,0:T(8,128)(2,1)}, bf16[288,1152]{1,0:T(8,128)(2,1)S(1)}, u32[]{:S(2)}, u32[]{:S(2)}) collective-permute-start(bf16[288,1152]{1,0:T(8,128)(2,1)} %get-tuple-element.41.refs_6_), channel_id=1, source_target_pairs={{0,2},{1,3},{2,0},{3,1},{4,6},{5,7},{6,4},{7,5},{8,12},{9,13},{10,... | collective-permute-start | bytes 1990664 | tf_op jit(solution)/shard_map/ppermute | solution.py:480
  6.5 17.0 %collective-permute-start.1 = (bf16[288,1152]{1,0:T(8,128)(2,1)}, bf16[288,1152]{1,0:T(8,128)(2,1)S(1)}, u32[]{:S(2)}, u32[]{:S(2)}) collective-permute-start(bf16[288,1152]{1,0:T(8,128)(2,1)} %get-tuple-element.42.refs_0_), channel_id=1, source_target_pairs={{0,4},{1,5},{2,6},{3,7},{4,0},{5,1},{6,2},{7,3},{8,10},{9,11},{10,... | collective-permute-start | bytes 1990664 | tf_op jit(solution)/shard_map/ppermute | solution.py:480
  9.6 5.2 %collective-permute-start.4 = (bf16[32,1152]{1,0:T(8,128)(2,1)S(1)}, bf16[32,1152]{1,0:T(8,128)(2,1)S(1)}, u32[]{:S(2)}, u32[]{:S(2)}) collective-permute-start(bf16[32,1152]{1,0:T(8,128)(2,1)S(1)} %constant_dynamic-slice_fusion), channel_id=1, source_target_pairs={{0,8},{8,0},{16,24},{24,16},{1,9},{9,1},{17,25},{25,17},{2,10},{10... | collective-permute-start | bytes 221192 | tf_op jit(solution)/shard_map/ppermute | solution.py:486
  11.2 7.4 %collective-permute-start.6 = (bf16[32,1152]{1,0:T(8,128)(2,1)S(1)}, bf16[32,1152]{1,0:T(8,128)(2,1)S(1)}, u32[]{:S(2)}, u32[]{:S(2)}) collective-permute-start(bf16[32,1152]{1,0:T(8,128)(2,1)S(1)} %constant_dynamic-slice_fusion), channel_id=1, source_target_pairs={{0,16},{8,24},{16,0},{24,8},{1,17},{9,25},{17,1},{25,9},{2,18},{10... | collective-permute-start | bytes 221192 | tf_op jit(solution)/shard_map/ppermute | solution.py:486
  13.8 6.3 %collective-permute-start.8 = (bf16[32,1152]{1,0:T(8,128)(2,1)S(1)}, bf16[32,1152]{1,0:T(8,128)(2,1)S(1)}, u32[]{:S(2)}, u32[]{:S(2)}) collective-permute-start(bf16[32,1152]{1,0:T(8,128)(2,1)S(1)} %constant_dynamic-slice_fusion), channel_id=1, source_target_pairs={{0,24},{8,16},{16,8},{24,0},{1,25},{9,17},{17,9},{25,1},{2,26},{10... | collective-permute-start | bytes 221192 | tf_op jit(solution)/shard_map/ppermute | solution.py:486
  14.9 8.6 %collective-permute-start.5 = (bf16[32,1152]{1,0:T(8,128)(2,1)S(1)}, bf16[32,1152]{1,0:T(8,128)(2,1)S(1)}, u32[]{:S(2)}, u32[]{:S(2)}) collective-permute-start(bf16[32,1152]{1,0:T(8,128)(2,1)S(1)} %collective-permute-done.4.refs_0_), channel_id=1, source_target_pairs={{0,1},{1,0},{2,3},{3,2},{4,5},{5,4},{6,7},{7,6},{8,9},{9,8},{10,11... | collective-permute-start | bytes 221192 | tf_op jit(solution)/shard_map/ppermute | solution.py:472
  18.6 4.9 %collective-permute-start.7 = (bf16[32,1152]{1,0:T(8,128)(2,1)S(1)}, bf16[32,1152]{1,0:T(8,128)(2,1)S(1)}, u32[]{:S(2)}, u32[]{:S(2)}) collective-permute-start(bf16[32,1152]{1,0:T(8,128)(2,1)S(1)} %collective-permute-done.6.refs_1_), channel_id=1, source_target_pairs={{0,1},{1,0},{2,3},{3,2},{4,5},{5,4},{6,7},{7,6},{8,9},{9,8},{10,11... | collective-permute-start | bytes 221192 | tf_op jit(solution)/shard_map/ppermute | solution.py:472
  20.1 3.4 %collective-permute-start.9 = (bf16[32,1152]{1,0:T(8,128)(2,1)S(1)}, bf16[32,1152]{1,0:T(8,128)(2,1)S(1)}, u32[]{:S(2)}, u32[]{:S(2)}) collective-permute-start(bf16[32,1152]{1,0:T(8,128)(2,1)S(1)} %collective-permute-done.8.refs_2_), channel_id=1, source_target_pairs={{0,1},{1,0},{2,3},{3,2},{4,5},{5,4},{6,7},{7,6},{8,9},{9,8},{10,11... | collective-permute-start | bytes 221192 | tf_op jit(solution)/shard_map/ppermute | solution.py:472
  21.7 16.5 %collective-permute-start.10 = (bf16[288,1152]{1,0:T(8,128)(2,1)}, bf16[288,1152]{1,0:T(8,128)(2,1)S(1)}, u32[]{:S(2)}, u32[]{:S(2)}) collective-permute-start(bf16[288,1152]{1,0:T(8,128)(2,1)} %get-tuple-element.42.refs_0_), channel_id=1, source_target_pairs={{0,2},{1,3},{2,0},{3,1},{4,6},{5,7},{6,4},{7,5},{8,12},{9,13},{10,... | collective-permute-start | bytes 1990664 | tf_op jit(solution)/shard_map/ppermute | solution.py:480
  23.5 15.7 %collective-permute-start.13 = (bf16[288,1152]{1,0:T(8,128)(2,1)S(1)}, bf16[288,1152]{1,0:T(8,128)(2,1)S(1)}, u32[]{:S(2)}, u32[]{:S(2)}) collective-permute-start(bf16[288,1152]{1,0:T(8,128)(2,1)S(1)} %collective-permute-done.refs_7_), channel_id=1, source_target_pairs={{0,4},{1,5},{2,6},{3,7},{4,0},{5,1},{6,2},{7,3},{8,10},{9,11},{10,... | collective-permute-start | bytes 1990664 | tf_op jit(solution)/shard_map/ppermute | solution.py:480
  25.1 15.4 %collective-permute-start.14 = (bf16[288,1152]{1,0:T(8,128)(2,1)S(1)}, bf16[288,1152]{1,0:T(8,128)(2,1)S(1)}, u32[]{:S(2)}, u32[]{:S(2)}) collective-permute-start(bf16[288,1152]{1,0:T(8,128)(2,1)S(1)} %collective-permute-done.refs_7_), channel_id=1, source_target_pairs={{0,8},{8,0},{16,24},{24,16},{1,9},{9,1},{17,25},{25,17},{2,10},{10... | collective-permute-start | bytes 1990664 | tf_op jit(solution)/shard_map/ppermute | solution.py:486
  26.7 15.5 %collective-permute-start.15 = (bf16[288,1152]{1,0:T(8,128)(2,1)S(1)}, bf16[288,1152]{1,0:T(8,128)(2,1)S(1)}, u32[]{:S(2)}, u32[]{:S(2)}) collective-permute-start(bf16[288,1152]{1,0:T(8,128)(2,1)S(1)} %collective-permute-done.refs_7_), channel_id=1, source_target_pairs={{0,1},{1,0},{2,3},{3,2},{4,5},{5,4},{6,7},{7,6},{8,9},{9,8},{10,11... | collective-permute-start | bytes 1990664 | tf_op jit(solution)/shard_map/ppermute | solution.py:472
  40.5 2.1 %collective-permute-start.16 = (bf16[288,1152]{1,0:T(8,128)(2,1)S(1)}, bf16[288,1152]{1,0:T(8,128)(2,1)S(1)}, u32[]{:S(2)}, u32[]{:S(2)}) collective-permute-start(bf16[288,1152]{1,0:T(8,128)(2,1)S(1)} %collective-permute-done.13.refs_8_), channel_id=1, source_target_pairs={{0,1},{1,0},{2,3},{3,2},{4,5},{5,4},{6,7},{7,6},{8,9},{9,8},{10,11... | collective-permute-start | bytes 1990664 | tf_op jit(solution)/shard_map/ppermute | solution.py:472
  40.5 3.1 %collective-permute-start.17 = (bf16[288,1152]{1,0:T(8,128)(2,1)S(1)}, bf16[288,1152]{1,0:T(8,128)(2,1)S(1)}, u32[]{:S(2)}, u32[]{:S(2)}) collective-permute-start(bf16[288,1152]{1,0:T(8,128)(2,1)S(1)} %collective-permute-done.14.refs_9_), channel_id=1, source_target_pairs={{0,1},{1,0},{2,3},{3,2},{4,5},{5,4},{6,7},{7,6},{8,9},{9,8},{10,11... | collective-permute-start | bytes 1990664 | tf_op jit(solution)/shard_map/ppermute | solution.py:472
  41.1 9.8 %collective-permute-start.12 = (bf16[144,1152]{1,0:T(8,128)(2,1)S(1)}, bf16[144,1152]{1,0:T(8,128)(2,1)S(1)}, u32[]{:S(2)}, u32[]{:S(2)}) collective-permute-start(bf16[144,1152]{1,0:T(8,128)(2,1)S(1)} %slice.8), channel_id=1, source_target_pairs={{0,4},{1,5},{2,6},{3,7},{4,0},{5,1},{6,2},{7,3},{8,10},{9,11},{10,... | collective-permute-start | bytes 995336 | tf_op jit(solution)/shard_map/ppermute | solution.py:480
  41.6 9.4 %collective-permute-start.11 = (bf16[144,1152]{1,0:T(8,128)(2,1)S(1)}, bf16[144,1152]{1,0:T(8,128)(2,1)S(1)}, u32[]{:S(2)}, u32[]{:S(2)}) collective-permute-start(bf16[144,1152]{1,0:T(8,128)(2,1)S(1)} %slice.6), channel_id=1, source_target_pairs={{0,2},{1,3},{2,0},{3,1},{4,6},{5,7},{6,4},{7,5},{8,12},{9,13},{10,... | collective-permute-start | bytes 995336 | tf_op jit(solution)/shard_map/ppermute | solution.py:480
  42.2 9.3 %collective-permute-start.19 = (bf16[288,1152]{1,0:T(8,128)(2,1)S(1)}, bf16[288,1152]{1,0:T(8,128)(2,1)S(1)}, u32[]{:S(2)}, u32[]{:S(2)}) collective-permute-start(bf16[288,1152]{1,0:T(8,128)(2,1)S(1)} %collective-permute-done.10.refs_2_), channel_id=1, source_target_pairs={{0,1},{1,0},{2,3},{3,2},{4,5},{5,4},{6,7},{7,6},{8,9},{9,8},{10,11... | collective-permute-start | bytes 1990664 | tf_op jit(solution)/shard_map/ppermute | solution.py:472
  42.6 9.0 %collective-permute-start.18 = (bf16[288,1152]{1,0:T(8,128)(2,1)S(1)}, bf16[288,1152]{1,0:T(8,128)(2,1)S(1)}, u32[]{:S(2)}, u32[]{:S(2)}) collective-permute-start(bf16[288,1152]{1,0:T(8,128)(2,1)S(1)} %collective-permute-done.1.refs_1_), channel_id=1, source_target_pairs={{0,1},{1,0},{2,3},{3,2},{4,5},{5,4},{6,7},{7,6},{8,9},{9,8},{10,11... | collective-permute-start | bytes 1990664 | tf_op jit(solution)/shard_map/ppermute | solution.py:472
  51.1 1.6 %collective-permute-start.20 = (bf16[144,1152]{1,0:T(8,128)(2,1)S(1)}, bf16[144,1152]{1,0:T(8,128)(2,1)S(1)}, u32[]{:S(2)}, u32[]{:S(2)}) collective-permute-start(bf16[144,1152]{1,0:T(8,128)(2,1)S(1)} %collective-permute-done.11.refs_3_), channel_id=1, source_target_pairs={{0,1},{1,0},{2,3},{3,2},{4,5},{5,4},{6,7},{7,6},{8,9},{9,8},{10,11... | collective-permute-start | bytes 995336 | tf_op jit(solution)/shard_map/ppermute | solution.py:472
  51.1 2.1 %collective-permute-start.21 = (bf16[144,1152]{1,0:T(8,128)(2,1)S(1)}, bf16[144,1152]{1,0:T(8,128)(2,1)S(1)}, u32[]{:S(2)}, u32[]{:S(2)}) collective-permute-start(bf16[144,1152]{1,0:T(8,128)(2,1)S(1)} %collective-permute-done.12.refs_4_), channel_id=1, source_target_pairs={{0,1},{1,0},{2,3},{3,2},{4,5},{5,4},{6,7},{7,6},{8,9},{9,8},{10,11... | collective-permute-start | bytes 995336 | tf_op jit(solution)/shard_map/ppermute | solution.py:472
  60.7 1.4 %collective-permute-start.22 = (f32[32,1152]{1,0:T(8,128)S(1)}, f32[32,1152]{1,0:T(8,128)S(1)}, u32[]{:S(2)}, u32[]{:S(2)}) collective-permute-start(f32[32,1152]{1,0:T(8,128)S(1)} %get-tuple-element.61), channel_id=1, source_target_pairs={{0,1},{1,0},{2,3},{3,2},{4,5},{5,4},{6,7},{7,6},{8,9},{9,8},{10,11... | collective-permute-start | bytes 442376 | tf_op jit(solution)/shard_map/ppermute | solution.py:472
  62.2 6.7 %collective-permute-start.23 = (bf16[32,1152]{1,0:T(8,128)(2,1)S(1)}, bf16[32,1152]{1,0:T(8,128)(2,1)S(1)}, u32[]{:S(2)}, u32[]{:S(2)}) collective-permute-start(bf16[32,1152]{1,0:T(8,128)(2,1)S(1)} %add_convert_fusion.1), channel_id=1, source_target_pairs={{0,2},{1,3},{2,0},{3,1},{4,6},{5,7},{6,4},{7,5},{8,10},{9,11},{10,... | collective-permute-start | bytes 221192 | tf_op jit(solution)/shard_map/ppermute | solution.py:472
  62.9 6.1 %collective-permute-start.24 = (bf16[32,1152]{1,0:T(8,128)(2,1)S(1)}, bf16[32,1152]{1,0:T(8,128)(2,1)S(1)}, u32[]{:S(2)}, u32[]{:S(2)}) collective-permute-start(bf16[32,1152]{1,0:T(8,128)(2,1)S(1)} %add_convert_fusion.1), channel_id=1, source_target_pairs={{0,4},{1,5},{2,6},{3,7},{4,0},{5,1},{6,2},{7,3},{8,12},{9,13},{10,... | collective-permute-start | bytes 221192 | tf_op jit(solution)/shard_map/ppermute | solution.py:472
  64.3 5.3 %collective-permute-start.25 = (bf16[32,1152]{1,0:T(8,128)(2,1)S(1)}, bf16[32,1152]{1,0:T(8,128)(2,1)S(1)}, u32[]{:S(2)}, u32[]{:S(2)}) collective-permute-start(bf16[32,1152]{1,0:T(8,128)(2,1)S(1)} %add_convert_fusion.1), channel_id=1, source_target_pairs={{0,6},{1,7},{2,4},{3,5},{4,2},{5,3},{6,0},{7,1},{8,14},{9,15},{10,... | collective-permute-start | bytes 221192 | tf_op jit(solution)/shard_map/ppermute | solution.py:472
  69.6 7.9 %collective-permute-start.26 = (bf16[32,1152]{1,0:T(8,128)(2,1)S(1)}, bf16[32,1152]{1,0:T(8,128)(2,1)S(1)}, u32[]{:S(2)}, u32[]{:S(2)}) collective-permute-start(bf16[32,1152]{1,0:T(8,128)(2,1)S(1)} %add_convert_fusion.mine.refs_0_), channel_id=1, source_target_pairs={{0,1},{1,0},{2,3},{3,2},{4,5},{5,4},{6,7},{7,6},{8,9},{9,8},{10,11... | collective-permute-start | bytes 221192 | tf_op jit(solution)/shard_map/ppermute | solution.py:472
  69.7 10.8 %collective-permute-start.27 = (bf16[32,1152]{1,0:T(8,128)(2,1)S(1)}, bf16[32,1152]{1,0:T(8,128)(2,1)S(1)}, u32[]{:S(2)}, u32[]{:S(2)}) collective-permute-start(bf16[32,1152]{1,0:T(8,128)(2,1)S(1)} %add_convert_fusion.mine.refs_0_), channel_id=1, source_target_pairs={{0,8},{8,0},{16,24},{24,16},{1,9},{9,1},{17,25},{25,17},{2,10},{10... | collective-permute-start | bytes 221192 | tf_op jit(solution)/shard_map/ppermute | solution.py:486
  71.5 9.0 %collective-permute-start.28 = (bf16[32,1152]{1,0:T(8,128)(2,1)S(1)}, bf16[32,1152]{1,0:T(8,128)(2,1)S(1)}, u32[]{:S(2)}, u32[]{:S(2)}) collective-permute-start(bf16[32,1152]{1,0:T(8,128)(2,1)S(1)} %add_convert_fusion.mine.refs_0_), channel_id=1, source_target_pairs={{0,16},{8,24},{16,0},{24,8},{1,17},{9,25},{17,1},{25,9},{2,18},{10... | collective-permute-start | bytes 221192 | tf_op jit(solution)/shard_map/ppermute | solution.py:486
  74.1 6.4 %collective-permute-start.29 = (bf16[32,1152]{1,0:T(8,128)(2,1)S(1)}, bf16[32,1152]{1,0:T(8,128)(2,1)S(1)}, u32[]{:S(2)}, u32[]{:S(2)}) collective-permute-start(bf16[32,1152]{1,0:T(8,128)(2,1)S(1)} %add_convert_fusion.mine.refs_0_), channel_id=1, source_target_pairs={{0,24},{8,16},{16,8},{24,0},{1,25},{9,17},{17,9},{25,1},{2,26},{10... | collective-permute-start | bytes 221192 | tf_op jit(solution)/shard_map/ppermute | solution.py:486
  80.5 1.3 %collective-permute-start.30 = (bf16[32,1152]{1,0:T(8,128)(2,1)S(1)}, bf16[32,1152]{1,0:T(8,128)(2,1)S(1)}, u32[]{:S(2)}, u32[]{:S(2)}) collective-permute-start(bf16[32,1152]{1,0:T(8,128)(2,1)S(1)} %collective-permute-done.27.refs_1_), channel_id=1, source_target_pairs={{0,1},{1,0},{2,3},{3,2},{4,5},{5,4},{6,7},{7,6},{8,9},{9,8},{10,11... | collective-permute-start | bytes 221192 | tf_op jit(solution)/shard_map/ppermute | solution.py:472
  80.6 1.4 %collective-permute-start.31 = (bf16[32,1152]{1,0:T(8,128)(2,1)S(1)}, bf16[32,1152]{1,0:T(8,128)(2,1)S(1)}, u32[]{:S(2)}, u32[]{:S(2)}) collective-permute-start(bf16[32,1152]{1,0:T(8,128)(2,1)S(1)} %collective-permute-done.28.refs_2_), channel_id=1, source_target_pairs={{0,1},{1,0},{2,3},{3,2},{4,5},{5,4},{6,7},{7,6},{8,9},{9,8},{10,11... | collective-permute-start | bytes 221192 | tf_op jit(solution)/shard_map/ppermute | solution.py:472
  (8 other events, 68.2 us)

commit v6 on v5

--- a/solution.py
+++ b/solution.py
@@ -98,15 +98,14 @@
 
 
 def join_kernel(*refs):
-    outs = [ref for ref in refs if ref.shape[0] == max(r.shape[0] for r in refs)]
-    parts = iter(refs[: len(refs) - len(outs)])
-    for out in outs:
-        start = 0
-        while start < out.shape[0]:
-            part = next(parts)
-            stop = min(start + part.shape[0], out.shape[0])
-            out[start:stop] = part[: stop - start]
-            start = stop
+    *parts, encoder_out, projector_out, sem = refs
+    rows = parts[0].shape[0]
+    copies = []
+    for i, part in enumerate(parts):
+        out = (encoder_out, projector_out)[i // 2].at[pl.ds(i % 2 * rows, rows)]
+        copies.append(pltpu.make_async_copy(part, out, sem.at[i]))
+        copies[-1].start()
+    wait_all(copies)
 
 
 def join_halves(out_ref, core, start, mine, far):
@@ -525,8 +524,9 @@
         return pl.pallas_call(
             join_kernel,
             out_shape=[shape((whole_rows, features), jnp.bfloat16)] * lengths,
-            in_specs=[VMEM] * len(parts),
+            in_specs=[ANY] * len(parts),
             out_specs=[VMEM] * lengths,
+            scratch_shapes=[pltpu.SemaphoreType.DMA((len(parts),))],
             name="join",
         )(*parts)
 

time: 85.7 us -> 85.8 us (level)
  transfers between devices with their start and end apart: 33 -> 33, of which waited for: 17 -> 18; matrix products, arithmetic and copies ran while one was open for 3% -> 3% of each run, Pallas kernels for 19% -> 19%
where the time goes in v6:
time: 85.8 us; the launch traced here: 85.5 us
  Pallas kernels  28.9 us (34%)
  starting transfers between devices  25.7 us (30%)
  waiting for transfers between devices  23.8 us (28%)
  local copies, waits for them, and re-layouts  4.38 us (5%)
  other arithmetic  1.67 us (2%)
  between operations  1.03 us (1%)
    ppermute x6, waiting for transfers between devices, swap_by_plane(): return lax.ppermute(array, ('dp', 'seq'), pairs)  11.6 us
    ppermute x7, starting transfers between devices, plane_swap(): return lax.ppermute(array, 'dp', [(i, i ^ distance) for i in range(planes)])  10.4 us
    ppermute x6, starting transfers between devices, swap_by_plane(): return lax.ppermute(array, ('dp', 'seq'), pairs)  8.94 us
    pallas_call x1, Pallas kernels, tiled(): pl.pallas_call(functools.partial(attend_kernel, chips, images, projector_...  7.54 us
    pallas_call x2, Pallas kernels, latent_part(): pl.pallas_call(kernel if whole is None else lambda _, *refs: kernel(*refs...  6.52 us
    ppermute x7, waiting for transfers between devices, plane_swap(): return lax.ppermute(array, 'dp', [(i, i ^ distance) for i in range(planes)])  6.41 us
    ppermute x20, starting transfers between devices, swap(): lax.ppermute(array, 'seq', [(i, i ^ distance) for i in range(shards)])  6.33 us
    ppermute x20, waiting for transfers between devices, swap(): lax.ppermute(array, 'seq', [(i, i ^ distance) for i in range(shards)])  5.84 us
  transfers between devices with their start and end apart: 33, of which 18 were waited for; matrix products, arithmetic and copies ran while one was open for 3% of the time, Pallas kernels for 19%

profile of v6, /device:TPU:0, one launch (start us, length us, event | category | flops | bytes accessed | tf_op | source)
XLA Modules:
  0.0 85.5 jit_solution(15955870409266710649)
XLA Ops:
  0.6 2.4 %join.1 = (bf16[288,1152]{1,0:T(8,128)(2,1)}, bf16[288,1152]{1,0:T(8,128)(2,1)}) custom-call(bf16[144,1152]{1,0:T(8,128)(2,1)} %refs_0_.1, bf16[144,1152]{1,0:T(8,128)(2,1)} %refs_1_.1, bf16[144,1152]{1,0:T(8,128)(2,1)} %refs_2_.2, bf16[144,1152]{1,0:T(8,128)(2,1)} %refs_3_.1), custom_call_target="tpu_custom_call" | custom-call | tf_op jit(solution)/shard_map/join/pallas_call | solution.py:524
  3.6 2.9 %collective-permute-start = (bf16[288,1152]{1,0:T(8,128)(2,1)}, bf16[288,1152]{1,0:T(8,128)(2,1)S(1)}, u32[]{:S(2)}, u32[]{:S(2)}) collective-permute-start(bf16[288,1152]{1,0:T(8,128)(2,1)} %get-tuple-element.41.refs_6_), channel_id=1, source_target_pairs={{0,2},{1,3},{2,0},{3,1},{4,6},{5,7},{6,4},{7,5},{8,12},{9,13},{10,... | collective-permute-start | bytes 1990664 | tf_op jit(solution)/shard_map/ppermute | solution.py:479
  6.5 1.5 %collective-permute-start.1 = (bf16[288,1152]{1,0:T(8,128)(2,1)}, bf16[288,1152]{1,0:T(8,128)(2,1)S(1)}, u32[]{:S(2)}, u32[]{:S(2)}) collective-permute-start(bf16[288,1152]{1,0:T(8,128)(2,1)} %get-tuple-element.42.refs_0_), channel_id=1, source_target_pairs={{0,4},{1,5},{2,6},{3,7},{4,0},{5,1},{6,2},{7,3},{8,10},{9,11},{10,... | collective-permute-start | bytes 1990664 | tf_op jit(solution)/shard_map/ppermute | solution.py:479
  8.8 0.9 %constant_dynamic-slice_fusion = bf16[32,1152]{1,0:T(8,128)(2,1)S(1)} fusion(bf16[64,1152]{1,0:T(8,128)(2,1)} %bitcast.8, s32[]{:T(128)S(6)} %select_n.32), kind=kLoop, calls=%fused_computation.14 | loop fusion | bytes 147460 | tf_op jit(solution)/shard_map/dynamic_slice | solution.py:540
  9.7 1.6 %collective-permute-start.4 = (bf16[32,1152]{1,0:T(8,128)(2,1)S(1)}, bf16[32,1152]{1,0:T(8,128)(2,1)S(1)}, u32[]{:S(2)}, u32[]{:S(2)}) collective-permute-start(bf16[32,1152]{1,0:T(8,128)(2,1)S(1)} %constant_dynamic-slice_fusion), channel_id=1, source_target_pairs={{0,8},{8,0},{16,24},{24,16},{1,9},{9,1},{17,25},{25,17},{2,10},{10... | collective-permute-start | bytes 221192 | tf_op jit(solution)/shard_map/ppermute | solution.py:485
  11.3 2.6 %collective-permute-start.6 = (bf16[32,1152]{1,0:T(8,128)(2,1)S(1)}, bf16[32,1152]{1,0:T(8,128)(2,1)S(1)}, u32[]{:S(2)}, u32[]{:S(2)}) collective-permute-start(bf16[32,1152]{1,0:T(8,128)(2,1)S(1)} %constant_dynamic-slice_fusion), channel_id=1, source_target_pairs={{0,16},{8,24},{16,0},{24,8},{1,17},{9,25},{17,1},{25,9},{2,18},{10... | collective-permute-start | bytes 221192 | tf_op jit(solution)/shard_map/ppermute | solution.py:485
  15.0 3.7 %collective-permute-done.6.refs_1_ = bf16[32,1152]{1,0:T(8,128)(2,1)S(1)} collective-permute-done((bf16[32,1152]{1,0:T(8,128)(2,1)S(1)}, bf16[32,1152]{1,0:T(8,128)(2,1)S(1)}, u32[]{:S(2)}, u32[]{:S(2)}) %collective-permute-start.6) | collective-permute-done | bytes 73760 | tf_op jit(solution)/shard_map/ppermute | solution.py:485
  18.7 1.4 %collective-permute-done.8.refs_2_ = bf16[32,1152]{1,0:T(8,128)(2,1)S(1)} collective-permute-done((bf16[32,1152]{1,0:T(8,128)(2,1)S(1)}, bf16[32,1152]{1,0:T(8,128)(2,1)S(1)}, u32[]{:S(2)}, u32[]{:S(2)}) %collective-permute-start.8) | collective-permute-done | bytes 73760 | tf_op jit(solution)/shard_map/ppermute | solution.py:485
  20.2 1.7 %collective-permute-done.refs_7_ = bf16[288,1152]{1,0:T(8,128)(2,1)S(1)} collective-permute-done((bf16[288,1152]{1,0:T(8,128)(2,1)}, bf16[288,1152]{1,0:T(8,128)(2,1)S(1)}, u32[]{:S(2)}, u32[]{:S(2)}) %collective-permute-start) | collective-permute-done | bytes 663584 | tf_op jit(solution)/shard_map/ppermute | solution.py:479
  21.9 1.7 %collective-permute-start.10 = (bf16[288,1152]{1,0:T(8,128)(2,1)}, bf16[288,1152]{1,0:T(8,128)(2,1)S(1)}, u32[]{:S(2)}, u32[]{:S(2)}) collective-permute-start(bf16[288,1152]{1,0:T(8,128)(2,1)} %get-tuple-element.42.refs_0_), channel_id=1, source_target_pairs={{0,2},{1,3},{2,0},{3,1},{4,6},{5,7},{6,4},{7,5},{8,12},{9,13},{10,... | collective-permute-start | bytes 1990664 | tf_op jit(solution)/shard_map/ppermute | solution.py:479
  23.6 1.6 %collective-permute-start.13 = (bf16[288,1152]{1,0:T(8,128)(2,1)S(1)}, bf16[288,1152]{1,0:T(8,128)(2,1)S(1)}, u32[]{:S(2)}, u32[]{:S(2)}) collective-permute-start(bf16[288,1152]{1,0:T(8,128)(2,1)S(1)} %collective-permute-done.refs_7_), channel_id=1, source_target_pairs={{0,4},{1,5},{2,6},{3,7},{4,0},{5,1},{6,2},{7,3},{8,10},{9,11},{10,... | collective-permute-start | bytes 1990664 | tf_op jit(solution)/shard_map/ppermute | solution.py:479
  25.2 1.6 %collective-permute-start.14 = (bf16[288,1152]{1,0:T(8,128)(2,1)S(1)}, bf16[288,1152]{1,0:T(8,128)(2,1)S(1)}, u32[]{:S(2)}, u32[]{:S(2)}) collective-permute-start(bf16[288,1152]{1,0:T(8,128)(2,1)S(1)} %collective-permute-done.refs_7_), channel_id=1, source_target_pairs={{0,8},{8,0},{16,24},{24,16},{1,9},{9,1},{17,25},{25,17},{2,10},{10... | collective-permute-start | bytes 1990664 | tf_op jit(solution)/shard_map/ppermute | solution.py:485
  26.9 1.7 %copy-done.2 = bf16[1152,1152]{1,0:T(8,128)(2,1)S(1)} copy-done((bf16[1152,1152]{1,0:T(8,128)(2,1)S(1)}, bf16[1152,1152]{1,0:T(8,128)(2,1)}, u32[]{:S(2)}) %copy-start.2) | copy-done | bytes 2654232
  28.7 1.7 %copy-done.4 = bf16[2,512,1152]{2,1,0:T(8,128)(2,1)S(1)} copy-done((bf16[2,512,1152]{2,1,0:T(8,128)(2,1)S(1)}, bf16[2,512,1152]{2,1,0:T(8,128)(2,1)}, u32[]{:S(2)}) %copy-start.4) | copy-done | bytes 2359320
  30.3 4.0 %queries.1.refs_10_ = bf16[1024,1152]{1,0:T(8,128)(2,1)S(1)} custom-call(bf16[1024,1152]{1,0:T(8,128)(2,1)S(1)} %bitcast.10, bf16[1152,1152]{1,0:T(8,128)(2,1)S(1)} %copy-done.2), custom_call_target="tpu_custom_call" | custom-call | flops 3000000000 | bytes 8000000 | tf_op jit(solution)/shard_map/queries/pallas_call | solution.py:503
  34.4 4.1 %collective-permute-done.10.refs_2_ = bf16[288,1152]{1,0:T(8,128)(2,1)S(1)} collective-permute-done((bf16[288,1152]{1,0:T(8,128)(2,1)}, bf16[288,1152]{1,0:T(8,128)(2,1)S(1)}, u32[]{:S(2)}, u32[]{:S(2)}) %collective-permute-start.10) | collective-permute-done | bytes 663584 | tf_op jit(solution)/shard_map/ppermute | solution.py:479
  38.5 1.0 %collective-permute-done.13.refs_8_ = bf16[288,1152]{1,0:T(8,128)(2,1)S(1)} collective-permute-done((bf16[288,1152]{1,0:T(8,128)(2,1)S(1)}, bf16[288,1152]{1,0:T(8,128)(2,1)S(1)}, u32[]{:S(2)}, u32[]{:S(2)}) %collective-permute-start.13) | collective-permute-done | bytes 663584 | tf_op jit(solution)/shard_map/ppermute | solution.py:479
  39.5 1.2 %collective-permute-done.14.refs_9_ = bf16[288,1152]{1,0:T(8,128)(2,1)S(1)} collective-permute-done((bf16[288,1152]{1,0:T(8,128)(2,1)S(1)}, bf16[288,1152]{1,0:T(8,128)(2,1)S(1)}, u32[]{:S(2)}, u32[]{:S(2)}) %collective-permute-start.14) | collective-permute-done | bytes 663584 | tf_op jit(solution)/shard_map/ppermute | solution.py:485
  43.0 0.8 collective-permute-done.17.refs_13_
  43.8 2.7 %encode.1 = (bf16[64,1152]{1,0:T(8,128)(2,1)S(1)}, f32[256,1152]{1,0:T(8,128)S(1)}, bf16[256,144]{1,0:T(8,128)(2,1)S(1)}, bf16[256,144]{1,0:T(8,128)(2,1)S(1)}, ...) custom-call(s32[3]{0:T(128)S(1)} %pad_add_fusion.place_ref, bf16[64,1152]{1,0:T(8,128)(2,1)S(1)} %bitcast.9, ...), custom_call_target="tpu_custom_call" | custom-call | flops 1000000 | bytes 10000 | tf_op jit(solution)/shard_map/encode/pallas_call | solution.py:597
  46.5 4.5 %collective-permute-done.12.refs_4_ = bf16[144,1152]{1,0:T(8,128)(2,1)S(1)} collective-permute-done((bf16[144,1152]{1,0:T(8,128)(2,1)S(1)}, bf16[144,1152]{1,0:T(8,128)(2,1)S(1)}, u32[]{:S(2)}, u32[]{:S(2)}) %collective-permute-start.12) | collective-permute-done | bytes 331808 | tf_op jit(solution)/shard_map/ppermute | solution.py:479
  51.8 1.1 %collective-permute-done.20.refs_8_ = bf16[144,1152]{1,0:T(8,128)(2,1)S(1)} collective-permute-done((bf16[144,1152]{1,0:T(8,128)(2,1)S(1)}, bf16[144,1152]{1,0:T(8,128)(2,1)S(1)}, u32[]{:S(2)}, u32[]{:S(2)}) %collective-permute-start.20) | collective-permute-done | bytes 331808 | tf_op jit(solution)/shard_map/ppermute | solution.py:471
  53.4 7.5 %attend.1 = (bf16[64,1152]{1,0:T(8,128)(2,1)S(1)}, bf16[2,512,512]{2,1,0:T(8,128)(2,1)S(1)}, f32[32,1152]{1,0:T(8,128)S(1)}, f32[32,1152]{1,0:T(8,128)S(1)}) custom-call(s32[3]{0:T(128)S(1)} %pad_add_fusion.place_ref, bf16[64,1152]{1,0:T(8,128)(2,1)S(1)} %get-tuple-element.56.encoded_ref, bf16[288,1152]{1,0:T(8,128)(2,1)S(1)} %copy-done.6, ...), custom_call_target="tpu_custom_call" | custom-call | flops 10000000000 | bytes 12000000 | tf_op jit(solution)/shard_map/attend/pallas_call | solution.py:622
  61.1 1.2 %collective-permute-done.22 = f32[32,1152]{1,0:T(8,128)S(1)} collective-permute-done((f32[32,1152]{1,0:T(8,128)S(1)}, f32[32,1152]{1,0:T(8,128)S(1)}, u32[]{:S(2)}, u32[]{:S(2)}) %collective-permute-start.22) | collective-permute-done | bytes 147488 | tf_op jit(solution)/shard_map/ppermute | solution.py:471
  63.1 1.5 %collective-permute-start.24 = (bf16[32,1152]{1,0:T(8,128)(2,1)S(1)}, bf16[32,1152]{1,0:T(8,128)(2,1)S(1)}, u32[]{:S(2)}, u32[]{:S(2)}) collective-permute-start(bf16[32,1152]{1,0:T(8,128)(2,1)S(1)} %add_convert_fusion.1), channel_id=1, source_target_pairs={{0,4},{1,5},{2,6},{3,7},{4,0},{5,1},{6,2},{7,3},{8,12},{9,13},{10,... | collective-permute-start | bytes 221192 | tf_op jit(solution)/shard_map/ppermute | solution.py:471
  64.5 1.4 %collective-permute-start.25 = (bf16[32,1152]{1,0:T(8,128)(2,1)S(1)}, bf16[32,1152]{1,0:T(8,128)(2,1)S(1)}, u32[]{:S(2)}, u32[]{:S(2)}) collective-permute-start(bf16[32,1152]{1,0:T(8,128)(2,1)S(1)} %add_convert_fusion.1), channel_id=1, source_target_pairs={{0,6},{1,7},{2,4},{3,5},{4,2},{5,3},{6,0},{7,1},{8,14},{9,15},{10,... | collective-permute-start | bytes 221192 | tf_op jit(solution)/shard_map/ppermute | solution.py:471
  66.0 3.2 %latent.2._ = bf16[1024,1152]{1,0:T(8,128)(2,1)} custom-call(bf16[2,512,512]{2,1,0:T(8,128)(2,1)S(1)} %get-tuple-element.62.score_ref.refs_0_, bf16[64,1152]{1,0:T(8,128)(2,1)S(1)} %get-tuple-element.63.key_ref.refs_1_, bf16[1152,1152]{1,0:T(8,128)(2,1)S(1)} %copy-done.3), custom_call_target="tpu_custom_call" | custom-call | flops 3000000000 | bytes 4000000 | tf_op jit(solution)/shard_map/latent/pallas_call | solution.py:650
  69.9 1.8 %collective-permute-start.27 = (bf16[32,1152]{1,0:T(8,128)(2,1)S(1)}, bf16[32,1152]{1,0:T(8,128)(2,1)S(1)}, u32[]{:S(2)}, u32[]{:S(2)}) collective-permute-start(bf16[32,1152]{1,0:T(8,128)(2,1)S(1)} %add_convert_fusion.mine.refs_0_), channel_id=1, source_target_pairs={{0,8},{8,0},{16,24},{24,16},{1,9},{9,1},{17,25},{25,17},{2,10},{10... | collective-permute-start | bytes 221192 | tf_op jit(solution)/shard_map/ppermute | solution.py:485
  71.7 2.6 %collective-permute-start.28 = (bf16[32,1152]{1,0:T(8,128)(2,1)S(1)}, bf16[32,1152]{1,0:T(8,128)(2,1)S(1)}, u32[]{:S(2)}, u32[]{:S(2)}) collective-permute-start(bf16[32,1152]{1,0:T(8,128)(2,1)S(1)} %add_convert_fusion.mine.refs_0_), channel_id=1, source_target_pairs={{0,16},{8,24},{16,0},{24,8},{1,17},{9,25},{17,1},{25,9},{2,18},{10... | collective-permute-start | bytes 221192 | tf_op jit(solution)/shard_map/ppermute | solution.py:485
  74.4 3.4 %latent.3 = bf16[1024,1152]{1,0:T(8,128)(2,1)} custom-call(bf16[1024,1152]{1,0:T(8,128)(2,1)} %latent.2._, bf16[2,512,512]{2,1,0:T(8,128)(2,1)S(1)} %get-tuple-element.62.score_ref.refs_0_, bf16[64,1152]{1,0:T(8,128)(2,1)S(1)} %get-tuple-element.63.key_ref.refs_1_, bf16[1152,1152]{1,0:T(8,128)(2,1)S(1)} %copy-done.3), custom_call_target="tpu_custom_call", output_to_operand_aliasing={{}: (0, {})} | custom-call | flops 3000000000 | bytes 4000000 | tf_op jit(solution)/shard_map/latent/pallas_call | solution.py:650
  77.7 2.9 %own_grads.1 = (bf16[64,1152]{1,0:T(8,128)(2,1)}, bf16[64,1152]{1,0:T(8,128)(2,1)S(1)}) custom-call(s32[3]{0:T(128)S(1)} %pad_add_fusion.place_ref, bf16[32,1152]{1,0:T(8,128)(2,1)S(1)} %add_convert_fusion.mine.refs_0_, bf16[32,1152]{1,0:T(8,128)(2,1)S(1)} %collective-permute-done.26.far.refs_4_, bf16[1152,1152]{1,0:T(8,128)(2,1)S(1)} %get-tuple-element.66.first_weight, ...), custom_call_target="tpu_custom_call" | custom-call | flops 1000000000 | bytes 6000000 | tf_op jit(solution)/shard_map/own_grads/pallas_call | solution.py:675
  82.5 2.8 %weight_grads.1 = (f32[144,1152]{1,0:T(8,128)}, f32[144,1152]{1,0:T(8,128)}) custom-call(s32[3]{0:T(128)S(1)} %pad_add_fusion.place_ref, bf16[32,1152]{1,0:T(8,128)(2,1)S(1)} %add_convert_fusion.mine.refs_0_, bf16[32,1152]{1,0:T(8,128)(2,1)S(1)} %collective-permute-done.27.refs_1_, bf16[32,1152]{1,0:T(8,128)(2,1)S(1)} %collective-permute-done.28.refs_2_, ...), custom_call_target="tpu_custom_call" | custom-call | tf_op jit(solution)/shard_map/weight_grads/pallas_call | solution.py:686
  (65 shorter events, 9.6 us)
Async XLA Ops:
  3.0 5.8 %collective-permute-start.3 = (bf16[288,1152]{1,0:T(8,128)(2,1)}, bf16[288,1152]{1,0:T(8,128)(2,1)S(1)}, u32[]{:S(2)}, u32[]{:S(2)}) collective-permute-start(bf16[288,1152]{1,0:T(8,128)(2,1)} %get-tuple-element.42.refs_0_), channel_id=1, source_target_pairs={{0,1},{1,0},{2,3},{3,2},{4,5},{5,4},{6,7},{7,6},{8,9},{9,8},{10,11... | collective-permute-start | bytes 1990664 | tf_op jit(solution)/shard_map/ppermute | solution.py:471
  3.5 5.3 %collective-permute-start.2 = (bf16[288,1152]{1,0:T(8,128)(2,1)}, bf16[288,1152]{1,0:T(8,128)(2,1)S(1)}, u32[]{:S(2)}, u32[]{:S(2)}) collective-permute-start(bf16[288,1152]{1,0:T(8,128)(2,1)} %get-tuple-element.41.refs_6_), channel_id=1, source_target_pairs={{0,1},{1,0},{2,3},{3,2},{4,5},{5,4},{6,7},{7,6},{8,9},{9,8},{10,11... | collective-permute-start | bytes 1990664 | tf_op jit(solution)/shard_map/ppermute | solution.py:471
  3.6 18.3 %collective-permute-start = (bf16[288,1152]{1,0:T(8,128)(2,1)}, bf16[288,1152]{1,0:T(8,128)(2,1)S(1)}, u32[]{:S(2)}, u32[]{:S(2)}) collective-permute-start(bf16[288,1152]{1,0:T(8,128)(2,1)} %get-tuple-element.41.refs_6_), channel_id=1, source_target_pairs={{0,2},{1,3},{2,0},{3,1},{4,6},{5,7},{6,4},{7,5},{8,12},{9,13},{10,... | collective-permute-start | bytes 1990664 | tf_op jit(solution)/shard_map/ppermute | solution.py:479
  6.5 17.1 %collective-permute-start.1 = (bf16[288,1152]{1,0:T(8,128)(2,1)}, bf16[288,1152]{1,0:T(8,128)(2,1)S(1)}, u32[]{:S(2)}, u32[]{:S(2)}) collective-permute-start(bf16[288,1152]{1,0:T(8,128)(2,1)} %get-tuple-element.42.refs_0_), channel_id=1, source_target_pairs={{0,4},{1,5},{2,6},{3,7},{4,0},{5,1},{6,2},{7,3},{8,10},{9,11},{10,... | collective-permute-start | bytes 1990664 | tf_op jit(solution)/shard_map/ppermute | solution.py:479
  9.7 5.2 %collective-permute-start.4 = (bf16[32,1152]{1,0:T(8,128)(2,1)S(1)}, bf16[32,1152]{1,0:T(8,128)(2,1)S(1)}, u32[]{:S(2)}, u32[]{:S(2)}) collective-permute-start(bf16[32,1152]{1,0:T(8,128)(2,1)S(1)} %constant_dynamic-slice_fusion), channel_id=1, source_target_pairs={{0,8},{8,0},{16,24},{24,16},{1,9},{9,1},{17,25},{25,17},{2,10},{10... | collective-permute-start | bytes 221192 | tf_op jit(solution)/shard_map/ppermute | solution.py:485
  11.3 7.5 %collective-permute-start.6 = (bf16[32,1152]{1,0:T(8,128)(2,1)S(1)}, bf16[32,1152]{1,0:T(8,128)(2,1)S(1)}, u32[]{:S(2)}, u32[]{:S(2)}) collective-permute-start(bf16[32,1152]{1,0:T(8,128)(2,1)S(1)} %constant_dynamic-slice_fusion), channel_id=1, source_target_pairs={{0,16},{8,24},{16,0},{24,8},{1,17},{9,25},{17,1},{25,9},{2,18},{10... | collective-permute-start | bytes 221192 | tf_op jit(solution)/shard_map/ppermute | solution.py:485
  13.9 6.3 %collective-permute-start.8 = (bf16[32,1152]{1,0:T(8,128)(2,1)S(1)}, bf16[32,1152]{1,0:T(8,128)(2,1)S(1)}, u32[]{:S(2)}, u32[]{:S(2)}) collective-permute-start(bf16[32,1152]{1,0:T(8,128)(2,1)S(1)} %constant_dynamic-slice_fusion), channel_id=1, source_target_pairs={{0,24},{8,16},{16,8},{24,0},{1,25},{9,17},{17,9},{25,1},{2,26},{10... | collective-permute-start | bytes 221192 | tf_op jit(solution)/shard_map/ppermute | solution.py:485
  14.9 8.7 %collective-permute-start.5 = (bf16[32,1152]{1,0:T(8,128)(2,1)S(1)}, bf16[32,1152]{1,0:T(8,128)(2,1)S(1)}, u32[]{:S(2)}, u32[]{:S(2)}) collective-permute-start(bf16[32,1152]{1,0:T(8,128)(2,1)S(1)} %collective-permute-done.4.refs_0_), channel_id=1, source_target_pairs={{0,1},{1,0},{2,3},{3,2},{4,5},{5,4},{6,7},{7,6},{8,9},{9,8},{10,11... | collective-permute-start | bytes 221192 | tf_op jit(solution)/shard_map/ppermute | solution.py:471
  18.7 4.9 %collective-permute-start.7 = (bf16[32,1152]{1,0:T(8,128)(2,1)S(1)}, bf16[32,1152]{1,0:T(8,128)(2,1)S(1)}, u32[]{:S(2)}, u32[]{:S(2)}) collective-permute-start(bf16[32,1152]{1,0:T(8,128)(2,1)S(1)} %collective-permute-done.6.refs_1_), channel_id=1, source_target_pairs={{0,1},{1,0},{2,3},{3,2},{4,5},{5,4},{6,7},{7,6},{8,9},{9,8},{10,11... | collective-permute-start | bytes 221192 | tf_op jit(solution)/shard_map/ppermute | solution.py:471
  20.1 3.5 %collective-permute-start.9 = (bf16[32,1152]{1,0:T(8,128)(2,1)S(1)}, bf16[32,1152]{1,0:T(8,128)(2,1)S(1)}, u32[]{:S(2)}, u32[]{:S(2)}) collective-permute-start(bf16[32,1152]{1,0:T(8,128)(2,1)S(1)} %collective-permute-done.8.refs_2_), channel_id=1, source_target_pairs={{0,1},{1,0},{2,3},{3,2},{4,5},{5,4},{6,7},{7,6},{8,9},{9,8},{10,11... | collective-permute-start | bytes 221192 | tf_op jit(solution)/shard_map/ppermute | solution.py:471
  21.9 16.6 %collective-permute-start.10 = (bf16[288,1152]{1,0:T(8,128)(2,1)}, bf16[288,1152]{1,0:T(8,128)(2,1)S(1)}, u32[]{:S(2)}, u32[]{:S(2)}) collective-permute-start(bf16[288,1152]{1,0:T(8,128)(2,1)} %get-tuple-element.42.refs_0_), channel_id=1, source_target_pairs={{0,2},{1,3},{2,0},{3,1},{4,6},{5,7},{6,4},{7,5},{8,12},{9,13},{10,... | collective-permute-start | bytes 1990664 | tf_op jit(solution)/shard_map/ppermute | solution.py:479
  23.6 15.8 %collective-permute-start.13 = (bf16[288,1152]{1,0:T(8,128)(2,1)S(1)}, bf16[288,1152]{1,0:T(8,128)(2,1)S(1)}, u32[]{:S(2)}, u32[]{:S(2)}) collective-permute-start(bf16[288,1152]{1,0:T(8,128)(2,1)S(1)} %collective-permute-done.refs_7_), channel_id=1, source_target_pairs={{0,4},{1,5},{2,6},{3,7},{4,0},{5,1},{6,2},{7,3},{8,10},{9,11},{10,... | collective-permute-start | bytes 1990664 | tf_op jit(solution)/shard_map/ppermute | solution.py:479
  25.2 15.5 %collective-permute-start.14 = (bf16[288,1152]{1,0:T(8,128)(2,1)S(1)}, bf16[288,1152]{1,0:T(8,128)(2,1)S(1)}, u32[]{:S(2)}, u32[]{:S(2)}) collective-permute-start(bf16[288,1152]{1,0:T(8,128)(2,1)S(1)} %collective-permute-done.refs_7_), channel_id=1, source_target_pairs={{0,8},{8,0},{16,24},{24,16},{1,9},{9,1},{17,25},{25,17},{2,10},{10... | collective-permute-start | bytes 1990664 | tf_op jit(solution)/shard_map/ppermute | solution.py:485
  26.8 15.6 %collective-permute-start.15 = (bf16[288,1152]{1,0:T(8,128)(2,1)S(1)}, bf16[288,1152]{1,0:T(8,128)(2,1)S(1)}, u32[]{:S(2)}, u32[]{:S(2)}) collective-permute-start(bf16[288,1152]{1,0:T(8,128)(2,1)S(1)} %collective-permute-done.refs_7_), channel_id=1, source_target_pairs={{0,1},{1,0},{2,3},{3,2},{4,5},{5,4},{6,7},{7,6},{8,9},{9,8},{10,11... | collective-permute-start | bytes 1990664 | tf_op jit(solution)/shard_map/ppermute | solution.py:471
  40.7 2.1 %collective-permute-start.16 = (bf16[288,1152]{1,0:T(8,128)(2,1)S(1)}, bf16[288,1152]{1,0:T(8,128)(2,1)S(1)}, u32[]{:S(2)}, u32[]{:S(2)}) collective-permute-start(bf16[288,1152]{1,0:T(8,128)(2,1)S(1)} %collective-permute-done.13.refs_8_), channel_id=1, source_target_pairs={{0,1},{1,0},{2,3},{3,2},{4,5},{5,4},{6,7},{7,6},{8,9},{9,8},{10,11... | collective-permute-start | bytes 1990664 | tf_op jit(solution)/shard_map/ppermute | solution.py:471
  40.7 3.1 %collective-permute-start.17 = (bf16[288,1152]{1,0:T(8,128)(2,1)S(1)}, bf16[288,1152]{1,0:T(8,128)(2,1)S(1)}, u32[]{:S(2)}, u32[]{:S(2)}) collective-permute-start(bf16[288,1152]{1,0:T(8,128)(2,1)S(1)} %collective-permute-done.14.refs_9_), channel_id=1, source_target_pairs={{0,1},{1,0},{2,3},{3,2},{4,5},{5,4},{6,7},{7,6},{8,9},{9,8},{10,11... | collective-permute-start | bytes 1990664 | tf_op jit(solution)/shard_map/ppermute | solution.py:471
  41.3 9.8 %collective-permute-start.12 = (bf16[144,1152]{1,0:T(8,128)(2,1)S(1)}, bf16[144,1152]{1,0:T(8,128)(2,1)S(1)}, u32[]{:S(2)}, u32[]{:S(2)}) collective-permute-start(bf16[144,1152]{1,0:T(8,128)(2,1)S(1)} %slice.8), channel_id=1, source_target_pairs={{0,4},{1,5},{2,6},{3,7},{4,0},{5,1},{6,2},{7,3},{8,10},{9,11},{10,... | collective-permute-start | bytes 995336 | tf_op jit(solution)/shard_map/ppermute | solution.py:479
  41.9 9.4 %collective-permute-start.11 = (bf16[144,1152]{1,0:T(8,128)(2,1)S(1)}, bf16[144,1152]{1,0:T(8,128)(2,1)S(1)}, u32[]{:S(2)}, u32[]{:S(2)}) collective-permute-start(bf16[144,1152]{1,0:T(8,128)(2,1)S(1)} %slice.6), channel_id=1, source_target_pairs={{0,2},{1,3},{2,0},{3,1},{4,6},{5,7},{6,4},{7,5},{8,12},{9,13},{10,... | collective-permute-start | bytes 995336 | tf_op jit(solution)/shard_map/ppermute | solution.py:479
  42.5 9.3 %collective-permute-start.19 = (bf16[288,1152]{1,0:T(8,128)(2,1)S(1)}, bf16[288,1152]{1,0:T(8,128)(2,1)S(1)}, u32[]{:S(2)}, u32[]{:S(2)}) collective-permute-start(bf16[288,1152]{1,0:T(8,128)(2,1)S(1)} %collective-permute-done.10.refs_2_), channel_id=1, source_target_pairs={{0,1},{1,0},{2,3},{3,2},{4,5},{5,4},{6,7},{7,6},{8,9},{9,8},{10,11... | collective-permute-start | bytes 1990664 | tf_op jit(solution)/shard_map/ppermute | solution.py:471
  42.8 9.0 %collective-permute-start.18 = (bf16[288,1152]{1,0:T(8,128)(2,1)S(1)}, bf16[288,1152]{1,0:T(8,128)(2,1)S(1)}, u32[]{:S(2)}, u32[]{:S(2)}) collective-permute-start(bf16[288,1152]{1,0:T(8,128)(2,1)S(1)} %collective-permute-done.1.refs_1_), channel_id=1, source_target_pairs={{0,1},{1,0},{2,3},{3,2},{4,5},{5,4},{6,7},{7,6},{8,9},{9,8},{10,11... | collective-permute-start | bytes 1990664 | tf_op jit(solution)/shard_map/ppermute | solution.py:471
  51.3 1.6 %collective-permute-start.20 = (bf16[144,1152]{1,0:T(8,128)(2,1)S(1)}, bf16[144,1152]{1,0:T(8,128)(2,1)S(1)}, u32[]{:S(2)}, u32[]{:S(2)}) collective-permute-start(bf16[144,1152]{1,0:T(8,128)(2,1)S(1)} %collective-permute-done.11.refs_3_), channel_id=1, source_target_pairs={{0,1},{1,0},{2,3},{3,2},{4,5},{5,4},{6,7},{7,6},{8,9},{9,8},{10,11... | collective-permute-start | bytes 995336 | tf_op jit(solution)/shard_map/ppermute | solution.py:471
  51.3 2.1 %collective-permute-start.21 = (bf16[144,1152]{1,0:T(8,128)(2,1)S(1)}, bf16[144,1152]{1,0:T(8,128)(2,1)S(1)}, u32[]{:S(2)}, u32[]{:S(2)}) collective-permute-start(bf16[144,1152]{1,0:T(8,128)(2,1)S(1)} %collective-permute-done.12.refs_4_), channel_id=1, source_target_pairs={{0,1},{1,0},{2,3},{3,2},{4,5},{5,4},{6,7},{7,6},{8,9},{9,8},{10,11... | collective-permute-start | bytes 995336 | tf_op jit(solution)/shard_map/ppermute | solution.py:471
  60.9 1.4 %collective-permute-start.22 = (f32[32,1152]{1,0:T(8,128)S(1)}, f32[32,1152]{1,0:T(8,128)S(1)}, u32[]{:S(2)}, u32[]{:S(2)}) collective-permute-start(f32[32,1152]{1,0:T(8,128)S(1)} %get-tuple-element.61), channel_id=1, source_target_pairs={{0,1},{1,0},{2,3},{3,2},{4,5},{5,4},{6,7},{7,6},{8,9},{9,8},{10,11... | collective-permute-start | bytes 442376 | tf_op jit(solution)/shard_map/ppermute | solution.py:471
  62.4 6.7 %collective-permute-start.23 = (bf16[32,1152]{1,0:T(8,128)(2,1)S(1)}, bf16[32,1152]{1,0:T(8,128)(2,1)S(1)}, u32[]{:S(2)}, u32[]{:S(2)}) collective-permute-start(bf16[32,1152]{1,0:T(8,128)(2,1)S(1)} %add_convert_fusion.1), channel_id=1, source_target_pairs={{0,2},{1,3},{2,0},{3,1},{4,6},{5,7},{6,4},{7,5},{8,10},{9,11},{10,... | collective-permute-start | bytes 221192 | tf_op jit(solution)/shard_map/ppermute | solution.py:471
  63.1 6.1 %collective-permute-start.24 = (bf16[32,1152]{1,0:T(8,128)(2,1)S(1)}, bf16[32,1152]{1,0:T(8,128)(2,1)S(1)}, u32[]{:S(2)}, u32[]{:S(2)}) collective-permute-start(bf16[32,1152]{1,0:T(8,128)(2,1)S(1)} %add_convert_fusion.1), channel_id=1, source_target_pairs={{0,4},{1,5},{2,6},{3,7},{4,0},{5,1},{6,2},{7,3},{8,12},{9,13},{10,... | collective-permute-start | bytes 221192 | tf_op jit(solution)/shard_map/ppermute | solution.py:471
  64.5 5.3 %collective-permute-start.25 = (bf16[32,1152]{1,0:T(8,128)(2,1)S(1)}, bf16[32,1152]{1,0:T(8,128)(2,1)S(1)}, u32[]{:S(2)}, u32[]{:S(2)}) collective-permute-start(bf16[32,1152]{1,0:T(8,128)(2,1)S(1)} %add_convert_fusion.1), channel_id=1, source_target_pairs={{0,6},{1,7},{2,4},{3,5},{4,2},{5,3},{6,0},{7,1},{8,14},{9,15},{10,... | collective-permute-start | bytes 221192 | tf_op jit(solution)/shard_map/ppermute | solution.py:471
  69.8 7.9 %collective-permute-start.26 = (bf16[32,1152]{1,0:T(8,128)(2,1)S(1)}, bf16[32,1152]{1,0:T(8,128)(2,1)S(1)}, u32[]{:S(2)}, u32[]{:S(2)}) collective-permute-start(bf16[32,1152]{1,0:T(8,128)(2,1)S(1)} %add_convert_fusion.mine.refs_0_), channel_id=1, source_target_pairs={{0,1},{1,0},{2,3},{3,2},{4,5},{5,4},{6,7},{7,6},{8,9},{9,8},{10,11... | collective-permute-start | bytes 221192 | tf_op jit(solution)/shard_map/ppermute | solution.py:471
  69.9 10.8 %collective-permute-start.27 = (bf16[32,1152]{1,0:T(8,128)(2,1)S(1)}, bf16[32,1152]{1,0:T(8,128)(2,1)S(1)}, u32[]{:S(2)}, u32[]{:S(2)}) collective-permute-start(bf16[32,1152]{1,0:T(8,128)(2,1)S(1)} %add_convert_fusion.mine.refs_0_), channel_id=1, source_target_pairs={{0,8},{8,0},{16,24},{24,16},{1,9},{9,1},{17,25},{25,17},{2,10},{10... | collective-permute-start | bytes 221192 | tf_op jit(solution)/shard_map/ppermute | solution.py:485
  71.7 9.0 %collective-permute-start.28 = (bf16[32,1152]{1,0:T(8,128)(2,1)S(1)}, bf16[32,1152]{1,0:T(8,128)(2,1)S(1)}, u32[]{:S(2)}, u32[]{:S(2)}) collective-permute-start(bf16[32,1152]{1,0:T(8,128)(2,1)S(1)} %add_convert_fusion.mine.refs_0_), channel_id=1, source_target_pairs={{0,16},{8,24},{16,0},{24,8},{1,17},{9,25},{17,1},{25,9},{2,18},{10... | collective-permute-start | bytes 221192 | tf_op jit(solution)/shard_map/ppermute | solution.py:485
  74.3 6.4 %collective-permute-start.29 = (bf16[32,1152]{1,0:T(8,128)(2,1)S(1)}, bf16[32,1152]{1,0:T(8,128)(2,1)S(1)}, u32[]{:S(2)}, u32[]{:S(2)}) collective-permute-start(bf16[32,1152]{1,0:T(8,128)(2,1)S(1)} %add_convert_fusion.mine.refs_0_), channel_id=1, source_target_pairs={{0,24},{8,16},{16,8},{24,0},{1,25},{9,17},{17,9},{25,1},{2,26},{10... | collective-permute-start | bytes 221192 | tf_op jit(solution)/shard_map/ppermute | solution.py:485
  80.7 1.3 %collective-permute-start.30 = (bf16[32,1152]{1,0:T(8,128)(2,1)S(1)}, bf16[32,1152]{1,0:T(8,128)(2,1)S(1)}, u32[]{:S(2)}, u32[]{:S(2)}) collective-permute-start(bf16[32,1152]{1,0:T(8,128)(2,1)S(1)} %collective-permute-done.27.refs_1_), channel_id=1, source_target_pairs={{0,1},{1,0},{2,3},{3,2},{4,5},{5,4},{6,7},{7,6},{8,9},{9,8},{10,11... | collective-permute-start | bytes 221192 | tf_op jit(solution)/shard_map/ppermute | solution.py:471
  80.8 1.4 %collective-permute-start.31 = (bf16[32,1152]{1,0:T(8,128)(2,1)S(1)}, bf16[32,1152]{1,0:T(8,128)(2,1)S(1)}, u32[]{:S(2)}, u32[]{:S(2)}) collective-permute-start(bf16[32,1152]{1,0:T(8,128)(2,1)S(1)} %collective-permute-done.28.refs_2_), channel_id=1, source_target_pairs={{0,1},{1,0},{2,3},{3,2},{4,5},{5,4},{6,7},{7,6},{8,9},{9,8},{10,11... | collective-permute-start | bytes 221192 | tf_op jit(solution)/shard_map/ppermute | solution.py:471
  (8 other events, 68.4 us)
